TPU v7x, 128 devices: a whole 4x4x4 slice. The times are simulated.
128 devices in a mesh: pre: 32 (over y, x, core), suf: 4 (over z).
Axes of the slice: x: 4, y: 4, z: 4, core: 2. Of those that a mesh axis runs over, the one named last changes fastest.
Arguments:
- values: bfloat16 [128, 192, 128, 128], P(('pre', 'suf'))
- block_rows: int32 [128, 192], P(('pre', 'suf')), may hold values from 0 to 15, as said below
- block_cols: int32 [128, 192], P(('pre', 'suf')), may hold values from 0 to 15
- block_count: int32 [128], P(('pre', 'suf')), may hold values from 1 to 192, as said below
- test_matrix: bfloat16 [8192, 512], P(('suf', 'pre')), may hold values from -6 to 6
Outputs:
- prefix_basis: float32 [65536, 512], P(('pre', 'suf'))
- suffix_basis: float32 [8192, 512], P(('suf', 'pre'))
Inputs may be any that keep to these rules, and one draw needn't show every extreme that they name: The live (block_rows, block_cols) pairs of one list are distinct. `block_count`: the live slots of a list are its first ones; some list has all 192 slots live.
All inputs are finite; a program needn't handle non-finite values.
Results may differ from a plain program's by a relative error of at most 0.003.
Values may be sent and summed in bfloat16 or wider, within the bound.
No kernel may reach another device: no remote copies, remote signals or barrier semaphores. Data moves between devices by JAX's collectives and lax.ppermute only.
A program may use at most 128 MiB of HBM per device.

v0:
```python
import math

import jax
import jax.numpy as jnp
from jax import lax
from jax.sharding import PartitionSpec as P

BLK = 128
PB = 16
SB = 16


highest = lax.Precision.HIGHEST


def block_product(block_values, take_ids, place_ids, live_count, panel, out_blocks, pattern):
    block = block_values.shape[-1]
    columns = panel.shape[1]
    tiles = panel.reshape(panel.shape[0] // block, block, columns)
    width = math.gcd(block_values.shape[0], 32)
    turns = (live_count + width - 1) // width

    def visit(turn, total):
        start = turn * width
        group_values = lax.dynamic_slice_in_dim(block_values, start, width, 0)
        group_take = lax.dynamic_slice_in_dim(take_ids, start, width, 0)
        group_place = lax.dynamic_slice_in_dim(place_ids, start, width, 0)
        alive = start + jnp.arange(width, dtype=jnp.int32) < live_count
        picked = jnp.take(tiles, group_take, axis=0)
        products = jnp.einsum(pattern, group_values, picked, preferred_element_type=jnp.float32)
        products = jnp.where(alive[:, None, None], products, jnp.float32(0.0))
        return total.at[group_place].add(products)

    empty = jnp.zeros((out_blocks, block, columns), jnp.float32)
    total = lax.fori_loop(0, turns, visit, empty)
    return total.reshape(out_blocks * block, columns)


def gram_of(matrix):
    return jnp.dot(matrix.T, matrix, precision=highest, preferred_element_type=jnp.float32)


def orthonormal(matrix, gram_sum, total_rows):
    factor = jnp.linalg.cholesky(gram_sum / total_rows)
    return lax.linalg.triangular_solve(
        factor, matrix, left_side=False, lower=True, transpose_a=True
    )


def prefix_share(partial_value, total_rows):
    share = lax.psum_scatter(partial_value, "suf", scatter_dimension=0, tiled=True)
    gram_sum = lax.psum(gram_of(share), ("pre", "suf"))
    return orthonormal(share, gram_sum, total_rows)


def local(values, block_rows, block_cols, block_count, test_matrix):
    block_values = values[0]
    row_ids = block_rows[0]
    col_ids = block_cols[0]
    live_count = block_count[0]
    prefix_total = PB * BLK * lax.axis_size("pre")
    suffix_total = SB * BLK * lax.axis_size("suf")
    panel = lax.all_gather(test_matrix, "pre", axis=0, tiled=True)
    sketch = block_product(block_values, col_ids, row_ids, live_count, panel, PB, "gij,gjr->gir")
    first_share = prefix_share(sketch, prefix_total)
    first_rounded = lax.all_gather(first_share.astype(jnp.bfloat16), "suf", axis=0, tiled=True)
    suffix_raw = block_product(
        block_values, row_ids, col_ids, live_count, first_rounded, SB, "gji,gjr->gir"
    )
    share = lax.psum_scatter(suffix_raw, "pre", scatter_dimension=0, tiled=True)
    gram_sum = lax.psum(gram_of(share), ("pre", "suf"))
    suffix_basis = orthonormal(share, gram_sum, suffix_total)
    suffix_rounded = lax.all_gather(suffix_basis.astype(jnp.bfloat16), "pre", axis=0, tiled=True)
    refined = block_product(
        block_values, col_ids, row_ids, live_count, suffix_rounded, PB, "gij,gjr->gir"
    )
    prefix_basis = prefix_share(refined, prefix_total)
    return (prefix_basis, suffix_basis)


def solution(mesh):
    in_specs = (
        P(("pre", "suf"), None, None, None),
        P(("pre", "suf"), None),
        P(("pre", "suf"), None),
        P(("pre", "suf")),
        P(("suf", "pre"), None),
    )
    out_specs = (P(("pre", "suf"), None), P(("suf", "pre"), None))
    return jax.shard_map(local, mesh=mesh, in_specs=in_specs, out_specs=out_specs, check_vma=False)
```

profile of v0, /device:TPU:1, one launch (start us, length us, event | category | flops | bytes accessed | tf_op | source)
XLA Modules:
  0.0 1722.8 jit_solution(16994706518038570902)
XLA Ops:
  8.6 49.0 %all-gather.4.cloned.1.call-done = bf16[2048,512]{1,0:T(8,128)(2,1)} async-done(((bf16[64,512]{1,0:T(8,128)(2,1)}), bf16[2048,512]{1,0:T(8,128)(2,1)}) %all-gather.4.cloned.1.call-update) | async-done | bytes 2097168 | tf_op jit(solution)/shard_map/all_gather | solution.py:63
  60.2 86.6 %while.35 = (s32[]{:T(128)}, f32[16,128,512]{2,1,0:T(8,128)}, s32[]{:T(128)}, s32[192]{0:T(256)S(1)}, s32[]{:T(128)}, /*index=5*/bf16[192,128,128]{2,1,0:T(8,128...) while((s32[]{:T(128)}, f32[16,128,512]{2,1,0:T(8,128)}, ...), condition=%wide.region_2.4_spmd, body=%wide.region_0.3_spmd.sunk | while | flops 543163776 | bytes 47191224 | solution.py:35
  70.8 18.2 %scatter_fusion = f32[16,128,512]{2,1,0:T(8,128)} fusion(f32[16,128,512]{2,1,0:T(8,128)} %get-tuple-element.566, s32[32]{0:T(128)S(1)} %compare_select_fusion.12, f32[32,128,512]{2,1,0:T(8,128)} %broadcast_select_fusion.6), kind=kCustom, calls=%fused_computation.3.clone.1 | custom fusion | flops 2097152 | bytes 25165952 | tf_op jit(solution)/shard_map/while/body/scatter-add | solution.py:32
  99.6 18.2 %scatter_fusion = f32[16,128,512]{2,1,0:T(8,128)} fusion(f32[16,128,512]{2,1,0:T(8,128)} %get-tuple-element.566, s32[32]{0:T(128)S(1)} %compare_select_fusion.12, f32[32,128,512]{2,1,0:T(8,128)} %broadcast_select_fusion.6), kind=kCustom, calls=%fused_computation.3.clone.1 | custom fusion | flops 2097152 | bytes 25165952 | tf_op jit(solution)/shard_map/while/body/scatter-add | solution.py:32
  128.5 18.2 %scatter_fusion = f32[16,128,512]{2,1,0:T(8,128)} fusion(f32[16,128,512]{2,1,0:T(8,128)} %get-tuple-element.566, s32[32]{0:T(128)S(1)} %compare_select_fusion.12, f32[32,128,512]{2,1,0:T(8,128)} %broadcast_select_fusion.6), kind=kCustom, calls=%fused_computation.3.clone.1 | custom fusion | flops 2097152 | bytes 25165952 | tf_op jit(solution)/shard_map/while/body/scatter-add | solution.py:32
  146.8 134.2 %reduce-scatter.4.cloned.1.call-done = f32[512,512]{1,0:T(8,128)} async-done(((f32[2048,512]{1,0:T(8,128)}), f32[512,512]{1,0:T(8,128)}) %reduce-scatter.4.cloned.1.call-update) | async-done | bytes 1048592 | tf_op jit(solution)/shard_map/reduce_scatter | solution.py:51
  285.7 148.4 %all-reduce.5.cloned.1.call-done = f32[512,512]{0,1:T(8,128)} async-done(((f32[512,512]{0,1:T(8,128)}), f32[512,512]{0,1:T(8,128)}) %all-reduce.5.cloned.1.call-update) | async-done | bytes 1048592 | tf_op jit(solution)/shard_map/psum | solution.py:52
  528.5 39.3 %custom-call.37 = f32[4,128,128]{1,2,0:T(8,128)S(1)} custom-call(f32[4,128,128]{2,1,0:T(8,128)S(1)} %get-tuple-element.159), custom_call_target="InvertDiagBlocksLowerTriangular" | custom-call | tf_op jit(solution)/shard_map/triangular_solve/custom-call.3 | solution.py:45
  573.5 29.7 %all-gather.6.cloned.1.call-done = bf16[2048,512]{0,1:T(8,128)(2,1)} async-done(((bf16[512,512]{0,1:T(8,128)(2,1)}), bf16[2048,512]{0,1:T(8,128)(2,1)}) %all-gather.6.cloned.1.call-update) | async-done | bytes 2097168 | tf_op jit(solution)/shard_map/all_gather | solution.py:66
  608.6 88.9 %while.36 = (s32[]{:T(128)}, f32[16,128,512]{2,1,0:T(8,128)}, s32[]{:T(128)}, s32[192]{0:T(256)S(1)}, s32[]{:T(128)}, /*index=5*/bf16[192,128,128]{2,1,0:T(8,128...) while((s32[]{:T(128)}, f32[16,128,512]{2,1,0:T(8,128)}, ...), condition=%wide.region_15.19_spmd, body=%wide.region_13.18_spmd.sunk | while | flops 543163776 | bytes 47191224 | solution.py:35
  619.7 18.6 %scatter_fusion.1 = f32[16,128,512]{2,1,0:T(8,128)} fusion(f32[16,128,512]{2,1,0:T(8,128)} %get-tuple-element.617, s32[32]{0:T(128)S(1)} %compare_select_fusion.13, f32[32,128,512]{2,1,0:T(8,128)} %broadcast_select_fusion.7), kind=kCustom, calls=%fused_computation.4.clone.1 | custom fusion | flops 2097152 | bytes 25165952 | tf_op jit(solution)/shard_map/while/body/scatter-add | solution.py:32
  649.3 18.6 %scatter_fusion.1 = f32[16,128,512]{2,1,0:T(8,128)} fusion(f32[16,128,512]{2,1,0:T(8,128)} %get-tuple-element.617, s32[32]{0:T(128)S(1)} %compare_select_fusion.13, f32[32,128,512]{2,1,0:T(8,128)} %broadcast_select_fusion.7), kind=kCustom, calls=%fused_computation.4.clone.1 | custom fusion | flops 2097152 | bytes 25165952 | tf_op jit(solution)/shard_map/while/body/scatter-add | solution.py:32
  679.0 18.4 %scatter_fusion.1 = f32[16,128,512]{2,1,0:T(8,128)} fusion(f32[16,128,512]{2,1,0:T(8,128)} %get-tuple-element.617, s32[32]{0:T(128)S(1)} %compare_select_fusion.13, f32[32,128,512]{2,1,0:T(8,128)} %broadcast_select_fusion.7), kind=kCustom, calls=%fused_computation.4.clone.1 | custom fusion | flops 2097152 | bytes 25165952 | tf_op jit(solution)/shard_map/while/body/scatter-add | solution.py:32
  697.5 167.8 %reduce-scatter.6.cloned.1.call-done = f32[64,512]{1,0:T(8,128)} async-done(((f32[2048,512]{1,0:T(8,128)}), f32[64,512]{1,0:T(8,128)}) %reduce-scatter.6.cloned.1.call-update) | async-done | bytes 131088 | tf_op jit(solution)/shard_map/reduce_scatter | solution.py:70
  868.5 151.2 %all-reduce.7.cloned.1.call-done = f32[512,512]{0,1:T(8,128)} async-done(((f32[512,512]{0,1:T(8,128)}), f32[512,512]{0,1:T(8,128)}) %all-reduce.7.cloned.1.call-update) | async-done | bytes 1048592 | tf_op jit(solution)/shard_map/psum | solution.py:71
  1114.6 39.3 %custom-call.26 = f32[4,128,128]{1,2,0:T(8,128)S(1)} custom-call(f32[4,128,128]{2,1,0:T(8,128)S(1)} %get-tuple-element.152), custom_call_target="InvertDiagBlocksLowerTriangular" | custom-call | tf_op jit(solution)/shard_map/triangular_solve | solution.py:45
  1156.4 42.8 %all-gather.8.cloned.1.call-done = bf16[2048,512]{1,0:T(8,128)(2,1)} async-done(((bf16[64,512]{1,0:T(8,128)(2,1)}), bf16[2048,512]{1,0:T(8,128)(2,1)}) %all-gather.8.cloned.1.call-update) | async-done | bytes 2097168 | tf_op jit(solution)/shard_map/all_gather | solution.py:73
  1201.7 86.5 %while.37 = (s32[]{:T(128)}, f32[16,128,512]{2,1,0:T(8,128)}, s32[]{:T(128)}, s32[192]{0:T(256)S(1)}, s32[]{:T(128)}, /*index=5*/bf16[192,128,128]{2,1,0:T(8,128...) while((s32[]{:T(128)}, f32[16,128,512]{2,1,0:T(8,128)}, ...), condition=%wide.region_20.24_spmd, body=%wide.region_18.23_spmd.sunk | while | flops 543163776 | bytes 47191224 | solution.py:35
  1212.3 18.2 %scatter_fusion.2 = f32[16,128,512]{2,1,0:T(8,128)} fusion(f32[16,128,512]{2,1,0:T(8,128)} %get-tuple-element.668, s32[32]{0:T(128)S(1)} %compare_select_fusion.14, f32[32,128,512]{2,1,0:T(8,128)} %broadcast_select_fusion.8), kind=kCustom, calls=%fused_computation.5.clone.1 | custom fusion | flops 2097152 | bytes 25165952 | tf_op jit(solution)/shard_map/while/body/scatter-add | solution.py:32
  1241.1 18.2 %scatter_fusion.2 = f32[16,128,512]{2,1,0:T(8,128)} fusion(f32[16,128,512]{2,1,0:T(8,128)} %get-tuple-element.668, s32[32]{0:T(128)S(1)} %compare_select_fusion.14, f32[32,128,512]{2,1,0:T(8,128)} %broadcast_select_fusion.8), kind=kCustom, calls=%fused_computation.5.clone.1 | custom fusion | flops 2097152 | bytes 25165952 | tf_op jit(solution)/shard_map/while/body/scatter-add | solution.py:32
  1270.0 18.2 %scatter_fusion.2 = f32[16,128,512]{2,1,0:T(8,128)} fusion(f32[16,128,512]{2,1,0:T(8,128)} %get-tuple-element.668, s32[32]{0:T(128)S(1)} %compare_select_fusion.14, f32[32,128,512]{2,1,0:T(8,128)} %broadcast_select_fusion.8), kind=kCustom, calls=%fused_computation.5.clone.1 | custom fusion | flops 2097152 | bytes 25165952 | tf_op jit(solution)/shard_map/while/body/scatter-add | solution.py:32
  1288.3 134.2 %reduce-scatter.8.cloned.1.call-done = f32[512,512]{1,0:T(8,128)} async-done(((f32[2048,512]{1,0:T(8,128)}), f32[512,512]{1,0:T(8,128)}) %reduce-scatter.8.cloned.1.call-update) | async-done | bytes 1048592 | tf_op jit(solution)/shard_map/reduce_scatter | solution.py:51
  1426.9 148.6 %all-reduce.9.cloned.1.call-done = f32[512,512]{0,1:T(8,128)} async-done(((f32[512,512]{0,1:T(8,128)}), f32[512,512]{0,1:T(8,128)}) %all-reduce.9.cloned.1.call-update) | async-done | bytes 1048592 | tf_op jit(solution)/shard_map/psum | solution.py:52
  1670.5 39.3 %custom-call.44 = f32[4,128,128]{1,2,0:T(8,128)S(1)} custom-call(f32[4,128,128]{2,1,0:T(8,128)S(1)} %get-tuple-element.160), custom_call_target="InvertDiagBlocksLowerTriangular" | custom-call | tf_op jit(solution)/shard_map/triangular_solve/custom-call.3 | solution.py:45
  (245 shorter events, 435.9 us)
Async XLA Ops:
  7.2 53.0 %copy-start.9 = (s32[1,192]{1,0:T(1,128)S(1)}, s32[1,192]{1,0:T(1,128)}, u32[]{:S(2)}) copy-start(s32[1,192]{1,0:T(1,128)} %param.17) | copy-start | bytes 2308
  7.2 53.0 %copy-start.8 = (s32[1,192]{1,0:T(1,128)S(1)}, s32[1,192]{1,0:T(1,128)}, u32[]{:S(2)}) copy-start(s32[1,192]{1,0:T(1,128)} %param.18) | copy-start | bytes 2308
  7.2 50.5 %all-gather.4.cloned.1.call-start = ((), (), s32[]{:S(2)}) async-start(), calls=%async_computation.3 | async-start | bytes 2162688 | tf_op jit(solution)/shard_map/all_gather | solution.py:63
  7.9 273.1 %reduce-scatter.4.cloned.1.call-start = ((), (), s32[]{:S(2)}) async-start(), calls=%async_computation.4 | async-start | bytes 5242880 | tf_op jit(solution)/shard_map/reduce_scatter | solution.py:51
  57.7 2.5 copy-start
  146.8 287.3 %all-reduce.5.cloned.1.call-start = ((), (), s32[]{:S(2)}) async-start(), calls=%async_computation.5 | async-start | bytes 2097152 | tf_op jit(solution)/shard_map/psum | solution.py:52
  285.5 317.8 %all-gather.6.cloned.1.call-start = ((), (), s32[]{:S(2)}) async-start(), calls=%async_computation.6 | async-start | bytes 2621440 | tf_op jit(solution)/shard_map/all_gather | solution.py:66
  434.1 1.8 copy-start.4
  436.1 131.7 %copy-start.2 = (f32[512,512]{1,0:T(8,128)S(1)}, f32[512,512]{1,0:T(8,128)}, u32[]{:S(2)}) copy-start(f32[512,512]{1,0:T(8,128)} %reduce-scatter.4.cloned.1.call-done) | copy-start | bytes 3145732
  573.4 291.8 %reduce-scatter.6.cloned.1.call-start = ((), (), s32[]{:S(2)}) async-start(), calls=%async_computation.7 | async-start | bytes 4325376 | tf_op jit(solution)/shard_map/reduce_scatter | solution.py:70
  697.5 322.2 %all-reduce.7.cloned.1.call-start = ((), (), s32[]{:S(2)}) async-start(), calls=%async_computation.8 | async-start | bytes 2097152 | tf_op jit(solution)/shard_map/psum | solution.py:71
  868.3 330.9 %all-gather.8.cloned.1.call-start = ((), (), s32[]{:S(2)}) async-start(), calls=%async_computation.9 | async-start | bytes 2162688 | tf_op jit(solution)/shard_map/all_gather | solution.py:73
  1019.7 1.8 copy-start.5
  1021.7 132.2 %copy-start.7 = (f32[64,512]{1,0:T(8,128)S(1)}, f32[64,512]{1,0:T(8,128)}, u32[]{:S(2)}) copy-start(f32[64,512]{1,0:T(8,128)} %reduce-scatter.6.cloned.1.call-done) | copy-start | bytes 393220
  1156.3 266.2 %reduce-scatter.8.cloned.1.call-start = ((), (), s32[]{:S(2)}) async-start(), calls=%async_computation.10 | async-start | bytes 5242880 | tf_op jit(solution)/shard_map/reduce_scatter | solution.py:51
  1199.2 2.5 copy-start.1
  1288.2 287.3 %all-reduce.9.cloned.1.call-start = ((), (), s32[]{:S(2)}) async-start(), calls=%async_computation.11 | async-start | bytes 2097152 | tf_op jit(solution)/shard_map/psum | solution.py:52
  1575.6 1.8 copy-start.6
  1577.6 132.3 %copy-start.3 = (f32[512,512]{1,0:T(8,128)S(1)}, f32[512,512]{1,0:T(8,128)}, u32[]{:S(2)}) copy-start(f32[512,512]{1,0:T(8,128)} %reduce-scatter.8.cloned.1.call-done) | copy-start | bytes 3145732
Sparse Core Ops, SparseCore 0:
  10.3 47.3 all-gather.3
  146.9 134.1 reduce-scatter.3
  287.2 146.9 all-reduce.4
  573.6 29.6 all-gather.5
  697.6 167.6 reduce-scatter.5
  871.2 148.4 all-reduce.6
  1156.4 42.6 all-gather.7
  1288.4 134.1 reduce-scatter.7
  1428.6 146.9 all-reduce.8
where the time goes:
time: 1730 us; the launch traced here: 1720 us
  waiting for transfers between devices  1010 us (58%)
  other arithmetic  535 us (31%)
  matrix products  93.2 us (5%)
  local copies, waits for them, and re-layouts  63.4 us (4%)
  between operations  23 us (1%)
    psum x2, waiting for transfers between devices, prefix_share(): gram_sum = lax.psum(gram_of(share), ('pre', 'suf'))  297 us
    reduce_scatter x2, waiting for transfers between devices, prefix_share(): lax.psum_scatter(partial_value, 'suf', scatter_dimension=0, tiled=True)  268 us
    another operation x44, other arithmetic, orthonormal(): factor = jnp.linalg.cholesky(gram_sum / total_rows)  238 us
    reduce_scatter x1, waiting for transfers between devices, local(): share = lax.psum_scatter(suffix_raw, 'pre', scatter_dimension=0, tiled=True)  168 us
    scatter-add x9, other arithmetic, visit(): return total.at[group_place].add(products)  165 us
    psum x1, waiting for transfers between devices, local(): gram_sum = lax.psum(gram_of(share), ('pre', 'suf'))  151 us
    another operation x8, other arithmetic, orthonormal(): lax.linalg.triangular_solve(factor, matrix, left_side=False, lower=True,...  118 us
    dot_general x9, matrix products, visit(): jnp.einsum(pattern, group_values, picked, preferred_element_type=jnp.floa...  64.7 us
  transfers between devices with their start and end apart: 9, of which 9 were waited for; matrix products, arithmetic and copies ran while one was open for 0% of the time, Pallas kernels for 0%

commit v1 on v0

v1 whole, which is shorter than its diff:
```python
import functools

import jax
import jax.numpy as jnp
from jax import lax
from jax.experimental import pallas as pl
from jax.experimental.pallas import tpu as pltpu
from jax.sharding import PartitionSpec as P

BLK = 128
PB = 16
SB = 16
TILE = 128
SUB = 8
RING = 4
VMEM_BYTES = 48 * 1024 * 1024

highest = lax.Precision.HIGHEST


def dense_kernel(count_ref, rows_ref, cols_ref, values_ref, out_ref, sem):
    out_ref[...] = jnp.zeros(out_ref.shape, out_ref.dtype)
    live = count_ref[0]

    def copy(k):
        row = pl.multiple_of(rows_ref[k] * BLK, BLK)
        col = pl.multiple_of(cols_ref[k] * BLK, BLK)
        return pltpu.make_async_copy(
            values_ref.at[k], out_ref.at[pl.ds(row, BLK), pl.ds(col, BLK)], sem
        )

    def start(k, carry):
        copy(k).start()
        return carry

    def wait(k, carry):
        copy(k).wait()
        return carry

    lax.fori_loop(0, live, start, 0)
    lax.fori_loop(0, live, wait, 0)


def dense_blocks(block_values, row_ids, col_ids, live_count):
    smem = pl.BlockSpec(memory_space=pltpu.SMEM)
    return pl.pallas_call(
        dense_kernel,
        out_shape=jax.ShapeDtypeStruct((PB * BLK, SB * BLK), jnp.bfloat16),
        in_specs=[smem, smem, smem, pl.BlockSpec(memory_space=pl.ANY)],
        out_specs=pl.BlockSpec(memory_space=pltpu.VMEM),
        scratch_shapes=[pltpu.SemaphoreType.DMA],
        compiler_params=pltpu.CompilerParams(vmem_limit_bytes=VMEM_BYTES),
        name="dense_blocks",
    )(live_count, row_ids, col_ids, block_values)


def orth_kernel(gram_ref, rows_ref, *refs, scale, rounded):
    if rounded:
        round_ref, out_ref, work_ref, panel_ref, spread_ref = refs
    else:
        out_ref, work_ref, panel_ref, spread_ref = refs
    rank = gram_ref.shape[0]
    panels = rank // TILE
    groups = TILE // SUB
    work_ref[...] = gram_ref[...] * scale
    for p in range(panels):
        width = rank - p * TILE
        total = width + TILE
        panel_ref[:, :width] = work_ref[p * TILE:(p + 1) * TILE, p * TILE:]
        row_ids = lax.broadcasted_iota(jnp.int32, (TILE, TILE), 0)
        lane_ids = lax.broadcasted_iota(jnp.int32, (TILE, TILE), 1)
        panel_ref[:, width:total] = jnp.where(row_ids == lane_ids, 1.0, 0.0).astype(jnp.float32)

        def step(b, first_group, total=total):
            base = pl.multiple_of(b * SUB, SUB)
            shift = (TILE - base) % TILE
            square = pltpu.roll(panel_ref[pl.ds(base, SUB), :TILE], shift, 1)
            for j in range(SUB):
                spread_ref[j] = jnp.broadcast_to(square[:, j:j + 1], (SUB, TILE))
            e = [
                [jnp.broadcast_to(spread_ref[j, i:i + 1, :], (SUB, TILE)) for j in range(i + 1)]
                for i in range(SUB)
            ]
            inv = [None] * SUB
            for k in range(SUB):
                inv[k] = lax.rsqrt(e[k][k])
                for i in range(k + 1, SUB):
                    e[i][k] = e[i][k] * inv[k]
                for i in range(k + 1, SUB):
                    for j in range(k + 1, i + 1):
                        e[i][j] = e[i][j] - e[i][k] * e[j][k]
            tiles = total // TILE
            strip = [panel_ref[pl.ds(base, SUB), t * TILE:(t + 1) * TILE] for t in range(tiles)]
            r = []
            for k in range(SUB):
                row = []
                for t in range(tiles):
                    v = jnp.broadcast_to(strip[t][k:k + 1, :], (SUB, TILE))
                    for j in range(k):
                        v = v - e[k][j] * r[j][t]
                    row.append(v * inv[k])
                r.append(row)
            sub_ids = lax.broadcasted_iota(jnp.int32, (SUB, TILE), 0)
            for t in range(tiles):
                v = r[0][t]
                for k in range(1, SUB):
                    v = jnp.where(sub_ids == k, r[k][t], v)
                panel_ref[pl.ds(base, SUB), t * TILE:(t + 1) * TILE] = v
                if t == 0:
                    turned = v.T
            for g in range(first_group, groups):
                lo = g * SUB
                mult = jnp.where(g > b, turned[lo:lo + SUB, :], 0.0)
                cols = [jnp.broadcast_to(mult[:, k:k + 1], (SUB, TILE)) for k in range(SUB)]
                for t in range(tiles):
                    v = panel_ref[lo:lo + SUB, t * TILE:(t + 1) * TILE]
                    for k in range(SUB):
                        v = v - cols[k] * r[k][t]
                    panel_ref[lo:lo + SUB, t * TILE:(t + 1) * TILE] = v

        parts = 4
        for q in range(parts):
            size = groups // parts

            def body(i, carry, q=q, size=size, step=step):
                step(q * size + i, q * size + 1)
                return carry

            lax.fori_loop(0, size, body, 0)

        for q in range(p + 1, panels):
            lhs = panel_ref[:, (q - p) * TILE:(q - p + 1) * TILE]
            rhs = panel_ref[:, (q - p) * TILE:width]
            update = lax.dot_general(
                lhs, rhs, (((0,), (0,)), ((), ())), precision=highest,
                preferred_element_type=jnp.float32,
            )
            work_ref[q * TILE:(q + 1) * TILE, q * TILE:] = (
                work_ref[q * TILE:(q + 1) * TILE, q * TILE:] - update
            )
        left = rows_ref[:, p * TILE:(p + 1) * TILE]
        for q in range(p):
            left = left - jnp.dot(
                out_ref[:, q * TILE:(q + 1) * TILE],
                work_ref[q * TILE:(q + 1) * TILE, p * TILE:(p + 1) * TILE],
                precision=highest, preferred_element_type=jnp.float32,
            )
        solved = lax.dot_general(
            left, panel_ref[:, width:total], (((1,), (1,)), ((), ())), precision=highest,
            preferred_element_type=jnp.float32,
        )
        out_ref[:, p * TILE:(p + 1) * TILE] = solved
        if rounded:
            round_ref[:, p * TILE:(p + 1) * TILE] = solved.astype(jnp.bfloat16)
        work_ref[p * TILE:(p + 1) * TILE, p * TILE:] = panel_ref[:, :width]


def orthonormal(matrix, gram, total_rows, rounded):
    rank = gram.shape[0]
    wide = jax.ShapeDtypeStruct(matrix.shape, jnp.float32)
    narrow = jax.ShapeDtypeStruct(matrix.shape, jnp.bfloat16)
    return pl.pallas_call(
        functools.partial(orth_kernel, scale=1.0 / total_rows, rounded=rounded),
        out_shape=(narrow, wide) if rounded else wide,
        scratch_shapes=[
            pltpu.VMEM((rank, rank), jnp.float32),
            pltpu.VMEM((TILE, rank + TILE), jnp.float32),
            pltpu.VMEM((SUB, SUB, TILE), jnp.float32),
        ],
        compiler_params=pltpu.CompilerParams(vmem_limit_bytes=VMEM_BYTES),
        name="orth",
    )(gram, matrix)


def along(axis, step):
    pairs = []
    for y in range(RING):
        for x in range(RING):
            for core in range(2):
                to = {
                    "y": ((y + step) % RING, x, core),
                    "x": (y, (x + step) % RING, core),
                    "core": (y, x, 1 - core),
                }[axis]
                pairs.append(((y * RING + x) * 2 + core, (to[0] * RING + to[1]) * 2 + to[2]))
    return pairs


def to_suf(value, step):
    return lax.ppermute(value, "suf", [(s, (s + step) % RING) for s in range(RING)])


def to_pre(value, axis, step=1):
    return lax.ppermute(value, "pre", along(axis, step))


def gather_suf(value):
    return jnp.concatenate([value] + [to_suf(value, -k) for k in range(1, RING)], axis=0)


def gather_pre(value, core):
    held = value[None]
    for axis in ("y", "x"):
        held = jnp.stack([held] + [to_pre(held, axis, -k) for k in range(1, RING)], axis=0)
    held = jnp.swapaxes(held[:, :, 0], 0, 1)
    other = to_pre(held, "core")
    first = jnp.where(core == 0, held, other)
    second = jnp.where(core == 0, other, held)
    full = jnp.stack([first, second], axis=2)
    return full.reshape(-1, value.shape[-1])


def scatter_suf(chunks):
    total = chunks[0]
    for k in (2, 1, 3):
        total = total + to_suf(chunks[k], k)
    return total


def scatter_pre(partial_value, core):
    rows, columns = partial_value.shape
    held = partial_value.reshape(RING, RING, 2, rows // (RING * RING * 2), columns)
    mine = jnp.where(core == 0, held[:, :, 0], held[:, :, 1])
    theirs = jnp.where(core == 0, held[:, :, 1], held[:, :, 0])
    held = mine + to_pre(theirs, "core")
    for axis in ("y", "x"):
        total = held[0]
        for k in range(1, RING):
            total = total + to_pre(held[k], axis, k)
        held = total
    return held


def sum_all(gram):
    rank = gram.shape[0]
    pre = lax.axis_size("pre")
    pieces = lax.all_to_all(gram, "pre", 0, 0, tiled=True)
    piece = jnp.sum(pieces.reshape(pre, rank // pre, rank), axis=0)
    total = piece
    for k in range(1, RING):
        total = total + to_suf(piece, k)
    spread = jnp.broadcast_to(total[None], (pre,) + total.shape)
    return lax.all_to_all(spread, "pre", 0, 0, tiled=True).reshape(rank, rank)


def gram_of(matrix):
    return jnp.dot(matrix.T, matrix, precision=highest, preferred_element_type=jnp.float32)


def local(values, block_rows, block_cols, block_count, test_matrix):
    pre, suf = lax.axis_index("pre"), lax.axis_index("suf")
    core, x, y = pre % 2, pre // 2 % RING, pre // (2 * RING)
    prefix_total = PB * BLK * lax.axis_size("pre")
    suffix_total = SB * BLK * lax.axis_size("suf")
    row_ids = ((block_rows[0] // RING - suf) % RING) * RING + block_rows[0] % RING
    col_ids = ((block_cols[0] // RING - y) % RING) * RING + (block_cols[0] % RING - x) % RING
    panel = gather_pre(test_matrix, core)
    dense = dense_blocks(values[0], row_ids, col_ids, block_count)
    share_rows = PB * BLK // RING

    def prefix_sums(panel):
        chunks = [None] * RING
        for k in (2, 1, 3, 0):
            chunks[k] = jnp.dot(
                dense[k * share_rows:(k + 1) * share_rows], panel,
                preferred_element_type=jnp.float32,
            )
        return scatter_suf(chunks)

    sketch = prefix_sums(panel)
    first_rounded, _ = orthonormal(sketch, sum_all(gram_of(sketch)), prefix_total, True)
    suffix_partial = lax.dot_general(
        dense, gather_suf(first_rounded), (((0,), (0,)), ((), ())),
        preferred_element_type=jnp.float32,
    )
    suffix_raw = scatter_pre(suffix_partial, core)
    suffix_rounded, suffix_basis = orthonormal(
        suffix_raw, sum_all(gram_of(suffix_raw)), suffix_total, True
    )
    refined = prefix_sums(gather_pre(suffix_rounded, core))
    prefix_basis = orthonormal(refined, sum_all(gram_of(refined)), prefix_total, False)
    return (prefix_basis, suffix_basis)


def solution(mesh):
    in_specs = (
        P(("pre", "suf"), None, None, None),
        P(("pre", "suf"), None),
        P(("pre", "suf"), None),
        P(("pre", "suf")),
        P(("suf", "pre"), None),
    )
    out_specs = (P(("pre", "suf"), None), P(("suf", "pre"), None))
    return jax.shard_map(local, mesh=mesh, in_specs=in_specs, out_specs=out_specs, check_vma=False)
```

time: 1730 us -> 528 us (0.31)
  waiting for transfers between devices: 1010 us -> 186 us
  other arithmetic: 535 us -> 3.75 us
  blocking collectives: 0 us -> 140 us
  Pallas kernels: 0 us -> 113 us
  matrix products: 93.2 us -> 21.7 us
  local copies, waits for them, and re-layouts: 63.4 us -> 3.89 us
  starting transfers between devices: 0.72 us -> 49.6 us
  between operations: 23 us -> 2.09 us
    psum x3 -> x0, waiting for transfers between devices: 448 us -> none  [the longest x2 297 us: prefix_share(): gram_sum = lax.psum(gram_of(share), ('pre', 'suf'))]
    reduce_scatter x3 -> x0, waiting for transfers between devices: 436 us -> none  [the longest x2 268 us: prefix_share(): lax.psum_scatter(partial_value, 'suf', scatter_dimension=0, tiled=True)]
    another operation x52 -> x6, other arithmetic: 357 us -> 1.71 us  [the longest x2 0.94 us: gather_pre(): jnp.stack([held] + [to_pre(held, axis, -k) for k in range(1, RING)], axis=0)]
    ppermute x0 -> x39, waiting for transfers between devices: none -> 186 us  [the longest x18 124 us: to_suf(): lax.ppermute(value, 'suf', [(s, (s + step) % RING) for s in range(RING)])]
    scatter-add x9 -> x0, other arithmetic: 165 us -> none  [visit(): return total.at[group_place].add(products)]
    all_to_all x0 -> x6, blocking collectives: none -> 140 us  [the longest x3 73.1 us: sum_all(): pieces = lax.all_to_all(gram, 'pre', 0, 0, tiled=True)]
    all_gather x3 -> x0, waiting for transfers between devices: 122 us -> none  [the longest x1 49 us: local(): panel = lax.all_gather(test_matrix, 'pre', axis=0, tiled=True)]
    pallas_call x0 -> x4, Pallas kernels: none -> 113 us  [the longest x3 107 us: orthonormal(): pl.pallas_call(functools.partial(orth_kernel, scale=1.0 / total_rows, rou...]
  transfers between devices with their start and end apart: 9 -> 39, of which waited for: 9 -> 28; matrix products, arithmetic and copies ran while one was open for 0% -> 0% of each run, Pallas kernels for 0% -> 1%
where the time goes in v1:
time: 528 us; the launch traced here: 520 us
  waiting for transfers between devices  186 us (35%)
  blocking collectives  140 us (27%)
  Pallas kernels  113 us (21%)
  starting transfers between devices  49.6 us (9%)
  matrix products  21.7 us (4%)
    ppermute x18, waiting for transfers between devices, to_suf(): lax.ppermute(value, 'suf', [(s, (s + step) % RING) for s in range(RING)])  124 us
    pallas_call x3, Pallas kernels, orthonormal(): pl.pallas_call(functools.partial(orth_kernel, scale=1.0 / total_rows, rou...  107 us
    all_to_all x3, blocking collectives, sum_all(): pieces = lax.all_to_all(gram, 'pre', 0, 0, tiled=True)  73.1 us
    all_to_all x3, blocking collectives, sum_all(): return lax.all_to_all(spread, 'pre', 0, 0, tiled=True).reshape(rank, rank)  66.5 us
    ppermute x21, waiting for transfers between devices, to_pre(): return lax.ppermute(value, 'pre', along(axis, step))  61.6 us
    ppermute x21, starting transfers between devices, to_pre(): return lax.ppermute(value, 'pre', along(axis, step))  27.4 us
    ppermute x18, starting transfers between devices, to_suf(): lax.ppermute(value, 'suf', [(s, (s + step) % RING) for s in range(RING)])  22.2 us
  transfers between devices with their start and end apart: 39, of which 28 were waited for; matrix products, arithmetic and copies ran while one was open for 0% of the time, Pallas kernels for 1%

profile of v1, /device:TPU:1, one launch (start us, length us, event | category | flops | bytes accessed | tf_op | source)
XLA Modules:
  0.0 519.7 jit_solution(8653374658527594955)
XLA Ops:
  17.3 7.0 %collective-permute-done.3 = bf16[4,1,64,512]{3,2,0,1:T(8,128)(2,1)S(1)} collective-permute-done((bf16[4,1,64,512]{3,2,0,1:T(8,128)(2,1)S(1)}, bf16[4,1,64,512]{3,2,0,1:T(8,128)(2,1)S(1)}, u32[]{:S(2)}, u32[]{:S(2)}) %collective-permute-start.3) | collective-permute-done | bytes 262176 | tf_op jit(solution)/shard_map/ppermute | solution.py:194
  27.0 6.0 %dense_blocks.1 = bf16[2048,2048]{1,0:T(8,128)(2,1)} custom-call(s32[1]{0:T(128)S(6)} %copy.27.count_ref, s32[192]{0:T(256)S(1)} %get-tuple-element.24.rows_ref, s32[192]{0:T(256)S(1)} %get-tuple-element.23.cols_ref, bf16[192,128,128]{2,1,0:T(8,128)(2,1)} %bitcast.139), custom_call_target="tpu_custom_call" | custom-call | tf_op jit(solution)/shard_map/dense_blocks/pallas_call | solution.py:46
  40.3 3.5 collective-permute-start.7
  46.5 19.8 %collective-permute-done.7 = f32[512,512]{1,0:T(8,128)S(1)} collective-permute-done((f32[512,512]{1,0:T(8,128)S(1)}, f32[512,512]{1,0:T(8,128)S(1)}, u32[]{:S(2)}, u32[]{:S(2)}) %collective-permute-start.7) | collective-permute-done | bytes 1048608 | tf_op jit(solution)/shard_map/ppermute | solution.py:190
  66.3 23.6 %collective-permute-done.8 = f32[512,512]{1,0:T(8,128)S(1)} collective-permute-done((f32[512,512]{1,0:T(8,128)S(1)}, f32[512,512]{1,0:T(8,128)S(1)}, u32[]{:S(2)}, u32[]{:S(2)}) %collective-permute-start.8) | collective-permute-done | bytes 1048608 | tf_op jit(solution)/shard_map/ppermute | solution.py:190
  94.2 23.5 %all_to_all.42 = f32[32,16,512]{2,1,0:T(8,128)S(1)} all-to-all(f32[32,16,512]{2,1,0:T(8,128)S(1)} %bitcast.140), channel_id=1, replica_groups=mesh['pre'=32,'suf'=4] {'pre'}, dimensions={0} | all-to-all | bytes 2097152 | tf_op jit(solution)/shard_map/all_to_all | solution.py:237
  121.2 3.2 collective-permute-done.11
  125.1 22.6 %all_to_all.43 = f32[32,16,512]{2,1,0:T(8,128)S(1)} all-to-all(f32[32,16,512]{2,1,0:T(8,128)S(1)} %broadcast_in_dim.11), channel_id=1, replica_groups=mesh['pre'=32,'suf'=4] {'pre'}, dimensions={0} | all-to-all | bytes 2097152 | tf_op jit(solution)/shard_map/all_to_all | solution.py:243
  147.8 36.6 %orth.3 = (bf16[512,512]{1,0:T(8,128)(2,1)S(1)}, f32[512,512]{1,0:T(8,128)}) custom-call(f32[512,512]{1,0:T(8,128)S(1)} %bitcast.129, f32[512,512]{1,0:T(8,128)S(1)} %fusion.39.rows_ref), custom_call_target="tpu_custom_call" | custom-call | tf_op jit(solution)/shard_map/orth/pallas_call | solution.py:162
  187.4 22.5 %collective-permute-done.15 = bf16[512,512]{1,0:T(8,128)(2,1)S(1)} collective-permute-done((bf16[512,512]{1,0:T(8,128)(2,1)S(1)}, bf16[512,512]{1,0:T(8,128)(2,1)S(1)}, u32[]{:S(2)}, u32[]{:S(2)}) %collective-permute-start.15) | collective-permute-done | bytes 524320 | tf_op jit(solution)/shard_map/ppermute | solution.py:190
  210.2 7.0 %fusion = f32[2048,512]{1,0:T(8,128)S(1)} fusion(bf16[2048,2048]{1,0:T(8,128)(2,1)} %dense_blocks.1, bf16[512,512]{1,0:T(8,128)(2,1)S(1)} %collective-permute-done.15, bf16[512,512]{1,0:T(8,128)(2,1)S(1)} %collective-permute-done.14, bf16[512,512]{1,0:T(8,128)(2,1)S(1)} %collective-permute-done.13, bf16[512,512]{1,0:T(8,128)(2,1)S(1)} %get-tuple-element.5), kind=kOutput, calls=%fused_computation.3 | convolution fusion | flops 4303355904 | bytes 14680064 | tf_op jit(solution)/shard_map/dot_general | solution.py:272
  219.5 3.8 collective-permute-done.16
  226.9 22.9 %collective-permute-done.17 = f32[4,64,512]{2,1,0:T(8,128)S(1)} collective-permute-done((f32[4,64,512]{2,1,0:T(8,128)S(1)}, f32[4,64,512]{2,1,0:T(8,128)S(1)}, u32[]{:S(2)}, u32[]{:S(2)}) %collective-permute-start.17) | collective-permute-done | bytes 524320 | tf_op jit(solution)/shard_map/ppermute | solution.py:194
  259.3 25.3 %all_to_all.44 = f32[32,16,512]{2,1,0:T(8,128)S(1)} all-to-all(f32[32,16,512]{2,1,0:T(8,128)S(1)} %bitcast.142), channel_id=1, replica_groups=mesh['pre'=32,'suf'=4] {'pre'}, dimensions={0} | all-to-all | bytes 2097152 | tf_op jit(solution)/shard_map/all_to_all | solution.py:237
  288.1 3.3 collective-permute-done.24
  291.6 22.0 %all_to_all.45 = f32[32,16,512]{2,1,0:T(8,128)S(1)} all-to-all(f32[32,16,512]{2,1,0:T(8,128)S(1)} %broadcast_in_dim.12), channel_id=1, replica_groups=mesh['pre'=32,'suf'=4] {'pre'}, dimensions={0} | all-to-all | bytes 2097152 | tf_op jit(solution)/shard_map/all_to_all | solution.py:243
  313.5 34.3 %orth.4 = (bf16[64,512]{1,0:T(8,128)(2,1)S(1)}, f32[64,512]{1,0:T(8,128)}) custom-call(f32[512,512]{1,0:T(8,128)S(1)} %bitcast.130, f32[64,512]{1,0:T(8,128)S(1)} %fusion.47.rows_ref), custom_call_target="tpu_custom_call" | custom-call | tf_op jit(solution)/shard_map/orth/pallas_call | solution.py:162
  357.7 4.1 collective-permute-done.31
  361.8 7.5 %collective-permute-done.30 = bf16[4,1,64,512]{3,2,0,1:T(8,128)(2,1)S(1)} collective-permute-done((bf16[4,1,64,512]{3,2,0,1:T(8,128)(2,1)S(1)}, bf16[4,1,64,512]{3,2,0,1:T(8,128)(2,1)S(1)}, u32[]{:S(2)}, u32[]{:S(2)}) %collective-permute-start.30) | collective-permute-done | bytes 262176 | tf_op jit(solution)/shard_map/ppermute | solution.py:194
  381.8 21.6 %collective-permute-done.33 = f32[512,512]{1,0:T(8,128)S(1)} collective-permute-done((f32[512,512]{1,0:T(8,128)S(1)}, f32[512,512]{1,0:T(8,128)S(1)}, u32[]{:S(2)}, u32[]{:S(2)}) %collective-permute-start.33) | collective-permute-done | bytes 1048608 | tf_op jit(solution)/shard_map/ppermute | solution.py:190
  403.4 23.1 %collective-permute-done.34 = f32[512,512]{1,0:T(8,128)S(1)} collective-permute-done((f32[512,512]{1,0:T(8,128)S(1)}, f32[512,512]{1,0:T(8,128)S(1)}, u32[]{:S(2)}, u32[]{:S(2)}) %collective-permute-start.34) | collective-permute-done | bytes 1048608 | tf_op jit(solution)/shard_map/ppermute | solution.py:190
  429.7 24.3 %all_to_all.46 = f32[32,16,512]{2,1,0:T(8,128)S(1)} all-to-all(f32[32,16,512]{2,1,0:T(8,128)S(1)} %bitcast.141), channel_id=1, replica_groups=mesh['pre'=32,'suf'=4] {'pre'}, dimensions={0} | all-to-all | bytes 2097152 | tf_op jit(solution)/shard_map/all_to_all | solution.py:237
  460.7 22.0 %all_to_all.47 = f32[32,16,512]{2,1,0:T(8,128)S(1)} all-to-all(f32[32,16,512]{2,1,0:T(8,128)S(1)} %broadcast_in_dim.28), channel_id=1, replica_groups=mesh['pre'=32,'suf'=4] {'pre'}, dimensions={0} | all-to-all | bytes 2097152 | tf_op jit(solution)/shard_map/all_to_all | solution.py:243
  482.6 36.6 %orth.5 = f32[512,512]{1,0:T(8,128)} custom-call(f32[512,512]{1,0:T(8,128)S(1)} %bitcast.128, f32[512,512]{1,0:T(8,128)S(1)} %fusion.36.rows_ref), custom_call_target="tpu_custom_call" | custom-call | tf_op jit(solution)/shard_map/orth/pallas_call | solution.py:162
  (113 shorter events, 91.5 us)
Async XLA Ops:
  0.7 5.9 %collective-permute-start.2 = (bf16[1,64,512]{2,1,0:T(8,128)(2,1)}, bf16[1,64,512]{2,1,0:T(8,128)(2,1)S(1)}, u32[]{:S(2)}, u32[]{:S(2)}) collective-permute-start(bf16[1,64,512]{2,1,0:T(8,128)(2,1)} %bitcast.163), channel_id=1, source_target_pairs={{0,32},{4,36},{8,40},{12,44},{16,48},{20,52},{24,56},{28,60},{32,6... | collective-permute-start | bytes 196616 | tf_op jit(solution)/shard_map/ppermute | solution.py:194
  10.0 7.3 %collective-permute-start.4 = (bf16[4,1,64,512]{3,2,0,1:T(8,128)(2,1)S(1)}, bf16[4,1,64,512]{3,2,0,1:T(8,128)(2,1)S(1)}, u32[]{:S(2)}, u32[]{:S(2)}) collective-permute-start(bf16[4,1,64,512]{3,2,0,1:T(8,128)(2,1)S(1)} %get-tuple-element.22), channel_id=1, source_target_pairs={{0,16},{4,20},{8,24},{12,28},{16,0},{20,4},{24,8},{28,12},{32,48},... | collective-permute-start | bytes 786440 | tf_op jit(solution)/shard_map/ppermute | solution.py:194
  12.8 11.4 %collective-permute-start.3 = (bf16[4,1,64,512]{3,2,0,1:T(8,128)(2,1)S(1)}, bf16[4,1,64,512]{3,2,0,1:T(8,128)(2,1)S(1)}, u32[]{:S(2)}, u32[]{:S(2)}) collective-permute-start(bf16[4,1,64,512]{3,2,0,1:T(8,128)(2,1)S(1)} %get-tuple-element.22), channel_id=1, source_target_pairs={{0,24},{4,28},{8,0},{12,4},{16,8},{20,12},{24,16},{28,20},{32,56},... | collective-permute-start | bytes 786440 | tf_op jit(solution)/shard_map/ppermute | solution.py:194
  13.7 10.6 %collective-permute-start.5 = (bf16[4,1,64,512]{3,2,0,1:T(8,128)(2,1)S(1)}, bf16[4,1,64,512]{3,2,0,1:T(8,128)(2,1)S(1)}, u32[]{:S(2)}, u32[]{:S(2)}) collective-permute-start(bf16[4,1,64,512]{3,2,0,1:T(8,128)(2,1)S(1)} %get-tuple-element.22), channel_id=1, source_target_pairs={{0,8},{4,12},{8,16},{12,20},{16,24},{20,28},{24,0},{28,4},{32,40},... | collective-permute-start | bytes 786440 | tf_op jit(solution)/shard_map/ppermute | solution.py:194
  24.4 8.6 %collective-permute-start.6 = (bf16[4,4,64,512]{3,2,0,1:T(8,128)(2,1)S(1)}, bf16[4,4,64,512]{3,2,0,1:T(8,128)(2,1)S(1)}, u32[]{:S(2)}, u32[]{:S(2)}) collective-permute-start(bf16[4,4,64,512]{3,2,0,1:T(8,128)(2,1)S(1)} %maximum_bitcast_fusion), channel_id=1, source_target_pairs={{0,4},{4,0},{8,12},{12,8},{16,20},{20,16},{24,28},{28,24},{32,36},... | collective-permute-start | bytes 3145736 | tf_op jit(solution)/shard_map/ppermute | solution.py:194
  40.3 26.0 %collective-permute-start.7 = (f32[512,512]{1,0:T(8,128)S(1)}, f32[512,512]{1,0:T(8,128)S(1)}, u32[]{:S(2)}, u32[]{:S(2)}) collective-permute-start(f32[512,512]{1,0:T(8,128)S(1)} %fusion.18), channel_id=1, source_target_pairs={{0,2},{1,3},{2,0},{3,1},{4,6},{5,7},{6,4},{7,5},{8,10},{9,11},{10,... | collective-permute-start | bytes 3145736 | tf_op jit(solution)/shard_map/ppermute | solution.py:190
  43.8 46.1 %collective-permute-start.8 = (f32[512,512]{1,0:T(8,128)S(1)}, f32[512,512]{1,0:T(8,128)S(1)}, u32[]{:S(2)}, u32[]{:S(2)}) collective-permute-start(f32[512,512]{1,0:T(8,128)S(1)} %fusion.14), channel_id=1, source_target_pairs={{0,1},{1,2},{2,3},{3,0},{4,5},{5,6},{6,7},{7,4},{8,9},{9,10},{10,1... | collective-permute-start | bytes 3145736 | tf_op jit(solution)/shard_map/ppermute | solution.py:190
  45.7 45.4 %collective-permute-start.9 = (f32[512,512]{1,0:T(8,128)S(1)}, f32[512,512]{1,0:T(8,128)S(1)}, u32[]{:S(2)}, u32[]{:S(2)}) collective-permute-start(f32[512,512]{1,0:T(8,128)S(1)} %fusion.10), channel_id=1, source_target_pairs={{0,3},{1,0},{2,1},{3,2},{4,7},{5,4},{6,5},{7,6},{8,11},{9,8},{10,9... | collective-permute-start | bytes 3145736 | tf_op jit(solution)/shard_map/ppermute | solution.py:190
  184.3 25.6 %collective-permute-start.15 = (bf16[512,512]{1,0:T(8,128)(2,1)S(1)}, bf16[512,512]{1,0:T(8,128)(2,1)S(1)}, u32[]{:S(2)}, u32[]{:S(2)}) collective-permute-start(bf16[512,512]{1,0:T(8,128)(2,1)S(1)} %get-tuple-element.5), channel_id=1, source_target_pairs={{0,1},{1,2},{2,3},{3,0},{4,5},{5,6},{6,7},{7,4},{8,9},{9,10},{10,1... | collective-permute-start | bytes 1572872 | tf_op jit(solution)/shard_map/ppermute | solution.py:190
  184.3 25.6 %collective-permute-start.14 = (bf16[512,512]{1,0:T(8,128)(2,1)S(1)}, bf16[512,512]{1,0:T(8,128)(2,1)S(1)}, u32[]{:S(2)}, u32[]{:S(2)}) collective-permute-start(bf16[512,512]{1,0:T(8,128)(2,1)S(1)} %get-tuple-element.5), channel_id=1, source_target_pairs={{0,2},{1,3},{2,0},{3,1},{4,6},{5,7},{6,4},{7,5},{8,10},{9,11},{10,... | collective-permute-start | bytes 1572872 | tf_op jit(solution)/shard_map/ppermute | solution.py:190
  185.5 24.7 %collective-permute-start.13 = (bf16[512,512]{1,0:T(8,128)(2,1)S(1)}, bf16[512,512]{1,0:T(8,128)(2,1)S(1)}, u32[]{:S(2)}, u32[]{:S(2)}) collective-permute-start(bf16[512,512]{1,0:T(8,128)(2,1)S(1)} %get-tuple-element.5), channel_id=1, source_target_pairs={{0,3},{1,0},{2,1},{3,2},{4,7},{5,4},{6,5},{7,6},{8,11},{9,8},{10,9... | collective-permute-start | bytes 1572872 | tf_op jit(solution)/shard_map/ppermute | solution.py:190
  217.7 5.6 %collective-permute-start.16 = (f32[4,4,64,512]{3,2,1,0:T(8,128)S(1)}, f32[4,4,64,512]{3,2,1,0:T(8,128)S(1)}, u32[]{:S(2)}, u32[]{:S(2)}) collective-permute-start(f32[4,4,64,512]{3,2,1,0:T(8,128)S(1)} %select_bitcast_fusion), channel_id=1, source_target_pairs={{0,4},{4,0},{8,12},{12,8},{16,20},{20,16},{24,28},{28,24},{32,36},... | collective-permute-start | bytes 6291464 | tf_op jit(solution)/shard_map/ppermute | solution.py:194
  224.2 25.7 %collective-permute-start.17 = (f32[4,64,512]{2,1,0:T(8,128)S(1)}, f32[4,64,512]{2,1,0:T(8,128)S(1)}, u32[]{:S(2)}, u32[]{:S(2)}) collective-permute-start(f32[4,64,512]{2,1,0:T(8,128)S(1)} %get-tuple-element.10), channel_id=1, source_target_pairs={{0,32},{4,36},{8,40},{12,44},{16,48},{20,52},{24,56},{28,60},{32,6... | collective-permute-start | bytes 1572872 | tf_op jit(solution)/shard_map/ppermute | solution.py:194
  224.2 25.6 %collective-permute-start.19 = (f32[4,64,512]{2,1,0:T(8,128)S(1)}, f32[4,64,512]{2,1,0:T(8,128)S(1)}, u32[]{:S(2)}, u32[]{:S(2)}) collective-permute-start(f32[4,64,512]{2,1,0:T(8,128)S(1)} %get-tuple-element.11), channel_id=1, source_target_pairs={{0,96},{4,100},{8,104},{12,108},{16,112},{20,116},{24,120},{28,124... | collective-permute-start | bytes 1572872 | tf_op jit(solution)/shard_map/ppermute | solution.py:194
  226.9 22.9 %collective-permute-start.18 = (f32[4,64,512]{2,1,0:T(8,128)S(1)}, f32[4,64,512]{2,1,0:T(8,128)S(1)}, u32[]{:S(2)}, u32[]{:S(2)}) collective-permute-start(f32[4,64,512]{2,1,0:T(8,128)S(1)} %get-tuple-element.12), channel_id=1, source_target_pairs={{0,64},{4,68},{8,72},{12,76},{16,80},{20,84},{24,88},{28,92},{32,9... | collective-permute-start | bytes 1572872 | tf_op jit(solution)/shard_map/ppermute | solution.py:194
  250.2 6.3 %collective-permute-start.22 = (f32[64,512]{1,0:T(8,128)S(1)}, f32[64,512]{1,0:T(8,128)S(1)}, u32[]{:S(2)}, u32[]{:S(2)}) collective-permute-start(f32[64,512]{1,0:T(8,128)S(1)} %get-tuple-element.16), channel_id=1, source_target_pairs={{0,24},{4,28},{8,0},{12,4},{16,8},{20,12},{24,16},{28,20},{32,56},... | collective-permute-start | bytes 393224 | tf_op jit(solution)/shard_map/ppermute | solution.py:194
  347.8 6.4 %collective-permute-start.28 = (bf16[1,64,512]{2,1,0:T(8,128)(2,1)S(1)}, bf16[1,64,512]{2,1,0:T(8,128)(2,1)S(1)}, u32[]{:S(2)}, u32[]{:S(2)}) collective-permute-start(bf16[1,64,512]{2,1,0:T(8,128)(2,1)S(1)} %bitcast.131), channel_id=1, source_target_pairs={{0,32},{4,36},{8,40},{12,44},{16,48},{20,52},{24,56},{28,60},{32,6... | collective-permute-start | bytes 196616 | tf_op jit(solution)/shard_map/ppermute | solution.py:194
  348.0 6.2 %collective-permute-start.27 = (bf16[1,64,512]{2,1,0:T(8,128)(2,1)S(1)}, bf16[1,64,512]{2,1,0:T(8,128)(2,1)S(1)}, u32[]{:S(2)}, u32[]{:S(2)}) collective-permute-start(bf16[1,64,512]{2,1,0:T(8,128)(2,1)S(1)} %bitcast.132), channel_id=1, source_target_pairs={{0,64},{4,68},{8,72},{12,76},{16,80},{20,84},{24,88},{28,92},{32,9... | collective-permute-start | bytes 196616 | tf_op jit(solution)/shard_map/ppermute | solution.py:194
  354.2 7.6 %collective-permute-start.31 = (bf16[4,1,64,512]{3,2,1,0:T(8,128)(2,1)S(1)}, bf16[4,1,64,512]{3,2,1,0:T(8,128)(2,1)S(1)}, u32[]{:S(2)}, u32[]{:S(2)}) collective-permute-start(bf16[4,1,64,512]{3,2,1,0:T(8,128)(2,1)S(1)} %get-tuple-element.20), channel_id=1, source_target_pairs={{0,8},{4,12},{8,16},{12,20},{16,24},{20,28},{24,0},{28,4},{32,40},... | collective-permute-start | bytes 786440 | tf_op jit(solution)/shard_map/ppermute | solution.py:194
  354.7 14.6 %collective-permute-start.30 = (bf16[4,1,64,512]{3,2,0,1:T(8,128)(2,1)S(1)}, bf16[4,1,64,512]{3,2,0,1:T(8,128)(2,1)S(1)}, u32[]{:S(2)}, u32[]{:S(2)}) collective-permute-start(bf16[4,1,64,512]{3,2,0,1:T(8,128)(2,1)S(1)} %get-tuple-element.19), channel_id=1, source_target_pairs={{0,16},{4,20},{8,24},{12,28},{16,0},{20,4},{24,8},{28,12},{32,48},... | collective-permute-start | bytes 786440 | tf_op jit(solution)/shard_map/ppermute | solution.py:194
  357.7 11.6 %collective-permute-start.29 = (bf16[4,1,64,512]{3,2,0,1:T(8,128)(2,1)S(1)}, bf16[4,1,64,512]{3,2,0,1:T(8,128)(2,1)S(1)}, u32[]{:S(2)}, u32[]{:S(2)}) collective-permute-start(bf16[4,1,64,512]{3,2,0,1:T(8,128)(2,1)S(1)} %get-tuple-element.19), channel_id=1, source_target_pairs={{0,24},{4,28},{8,0},{12,4},{16,8},{20,12},{24,16},{28,20},{32,56},... | collective-permute-start | bytes 786440 | tf_op jit(solution)/shard_map/ppermute | solution.py:194
  377.4 26.0 %collective-permute-start.33 = (f32[512,512]{1,0:T(8,128)S(1)}, f32[512,512]{1,0:T(8,128)S(1)}, u32[]{:S(2)}, u32[]{:S(2)}) collective-permute-start(f32[512,512]{1,0:T(8,128)S(1)} %fusion.16), channel_id=1, source_target_pairs={{0,2},{1,3},{2,0},{3,1},{4,6},{5,7},{6,4},{7,5},{8,10},{9,11},{10,... | collective-permute-start | bytes 3145736 | tf_op jit(solution)/shard_map/ppermute | solution.py:190
  379.1 47.4 %collective-permute-start.34 = (f32[512,512]{1,0:T(8,128)S(1)}, f32[512,512]{1,0:T(8,128)S(1)}, u32[]{:S(2)}, u32[]{:S(2)}) collective-permute-start(f32[512,512]{1,0:T(8,128)S(1)} %fusion.12), channel_id=1, source_target_pairs={{0,1},{1,2},{2,3},{3,0},{4,5},{5,6},{6,7},{7,4},{8,9},{9,10},{10,1... | collective-permute-start | bytes 3145736 | tf_op jit(solution)/shard_map/ppermute | solution.py:190
  379.1 47.4 %collective-permute-start.35 = (f32[512,512]{1,0:T(8,128)S(1)}, f32[512,512]{1,0:T(8,128)S(1)}, u32[]{:S(2)}, u32[]{:S(2)}) collective-permute-start(f32[512,512]{1,0:T(8,128)S(1)} %fusion.8), channel_id=1, source_target_pairs={{0,3},{1,0},{2,1},{3,2},{4,7},{5,4},{6,5},{7,6},{8,11},{9,8},{10,9... | collective-permute-start | bytes 3145736 | tf_op jit(solution)/shard_map/ppermute | solution.py:190
  (20 other events, 183.3 us)

commit v2 on v1

v2 whole, which is shorter than its diff:
```python
import functools

import jax
import jax.numpy as jnp
from jax import lax
from jax.experimental import pallas as pl
from jax.experimental.pallas import tpu as pltpu
from jax.sharding import PartitionSpec as P

BLK = 128
PB = 16
SB = 16
TILE = 128
SUB = 8
RING = 4
VMEM_BYTES = 48 * 1024 * 1024

highest = lax.Precision.HIGHEST


def dense_kernel(count_ref, rows_ref, cols_ref, values_ref, out_ref, sem):
    out_ref[...] = jnp.zeros(out_ref.shape, out_ref.dtype)
    live = count_ref[0]

    def copy(k):
        row = pl.multiple_of(rows_ref[k] * BLK, BLK)
        col = pl.multiple_of(cols_ref[k] * BLK, BLK)
        return pltpu.make_async_copy(
            values_ref.at[k], out_ref.at[pl.ds(row, BLK), pl.ds(col, BLK)], sem
        )

    def start(k, carry):
        copy(k).start()
        return carry

    def wait(k, carry):
        copy(k).wait()
        return carry

    lax.fori_loop(0, live, start, 0)
    lax.fori_loop(0, live, wait, 0)


def dense_blocks(block_values, row_ids, col_ids, live_count):
    smem = pl.BlockSpec(memory_space=pltpu.SMEM)
    return pl.pallas_call(
        dense_kernel,
        out_shape=jax.ShapeDtypeStruct((PB * BLK, SB * BLK), jnp.bfloat16),
        in_specs=[smem, smem, smem, pl.BlockSpec(memory_space=pl.ANY)],
        out_specs=pl.BlockSpec(memory_space=pltpu.VMEM),
        scratch_shapes=[pltpu.SemaphoreType.DMA],
        compiler_params=pltpu.CompilerParams(vmem_limit_bytes=VMEM_BYTES),
        name="dense_blocks",
    )(live_count, row_ids, col_ids, block_values)


def tile_pairs(rank):
    panels = rank // TILE
    return [(p, t) for p in range(panels) for t in range(p, panels)]


def gram_kernel(*refs):
    parts, (total_ref, gram_ref) = refs[:-2], refs[-2:]
    total = parts[0][...]
    for part in parts[1:]:
        total = total + part[...]
    total_ref[...] = total
    rank = total.shape[1]
    at = 0
    for p in range(rank // TILE):
        row = lax.dot_general(
            total[:, p * TILE:(p + 1) * TILE], total[:, p * TILE:], (((0,), (0,)), ((), ())),
            precision=highest, preferred_element_type=jnp.float32,
        )
        for t in range(rank // TILE - p):
            gram_ref[at:at + TILE, :] = row[:, t * TILE:(t + 1) * TILE]
            at += TILE


def sum_and_gram(parts):
    rows, rank = parts[0].shape
    packed = len(tile_pairs(rank)) * TILE
    return pl.pallas_call(
        gram_kernel,
        out_shape=(
            jax.ShapeDtypeStruct((rows, rank), jnp.float32),
            jax.ShapeDtypeStruct((packed, TILE), jnp.float32),
        ),
        compiler_params=pltpu.CompilerParams(vmem_limit_bytes=VMEM_BYTES),
        name="gram",
    )(*parts)


def eliminate(panel_ref, spread_ref):
    total = panel_ref.shape[1]
    tiles = total // TILE
    groups = TILE // SUB
    sub_ids = lax.broadcasted_iota(jnp.int32, (SUB, TILE), 0)
    for b in range(groups):
        base = b * SUB
        here = slice(base, base + SUB)
        square = panel_ref[here, here]
        slot = b % 2
        for j in range(SUB):
            spread_ref[slot, j] = jnp.broadcast_to(square[:, j:j + 1], (SUB, TILE))
        e = [
            [jnp.broadcast_to(spread_ref[slot, j, i:i + 1, :], (SUB, TILE)) for j in range(i + 1)]
            for i in range(SUB)
        ]
        if b + 1 < groups:
            below = panel_ref[base + SUB:base + 2 * SUB, here]
            raw = [jnp.broadcast_to(below[:, k:k + 1], (SUB, TILE)) for k in range(SUB)]
        inv = [None] * SUB
        for k in range(SUB):
            inv[k] = lax.rsqrt(e[k][k])
            for i in range(k + 1, SUB):
                e[i][k] = e[i][k] * inv[k]
            for i in range(k + 1, SUB):
                for j in range(k + 1, i + 1):
                    e[i][j] = e[i][j] - e[i][k] * e[j][k]
        r = []
        for k in range(SUB):
            row = []
            for t in range(tiles):
                v = jnp.broadcast_to(panel_ref[base + k:base + k + 1, t * TILE:(t + 1) * TILE], (SUB, TILE))
                for j in range(k):
                    v = v - e[k][j] * r[j][t]
                row.append(v * inv[k])
            r.append(row)
        for t in range(tiles):
            v = r[0][t]
            for k in range(1, SUB):
                v = jnp.where(sub_ids == k, r[k][t], v)
            panel_ref[here, t * TILE:(t + 1) * TILE] = v
            if t == 0:
                turned = v.T
        for g in range(b + 1, groups):
            there = slice(g * SUB, (g + 1) * SUB)
            if g == b + 1:
                cols = []
                for k in range(SUB):
                    v = raw[k]
                    for j in range(k):
                        v = v - e[k][j] * cols[j]
                    cols.append(v * inv[k])
            else:
                cols = [jnp.broadcast_to(turned[there, k:k + 1], (SUB, TILE)) for k in range(SUB)]
            for t in range(tiles):
                v = panel_ref[there, t * TILE:(t + 1) * TILE]
                for k in range(SUB):
                    v = v - cols[k] * r[k][t]
                panel_ref[there, t * TILE:(t + 1) * TILE] = v


def orth_kernel(gram_ref, rows_ref, *refs, scale, rounded):
    if rounded:
        round_ref, out_ref, work_ref, left_ref, panel_ref, spread_ref = refs
    else:
        out_ref, work_ref, left_ref, panel_ref, spread_ref = refs
    rank = rows_ref.shape[1]
    panels = rank // TILE
    pairs = tile_pairs(rank)
    for t in range(panels):
        for p in range(panels):
            rows = slice(p * TILE, (p + 1) * TILE)
            if (p, t) in pairs:
                at = pairs.index((p, t)) * TILE
                work_ref[t, rows, :] = gram_ref[at:at + TILE, :] * scale
            else:
                work_ref[t, rows, :] = jnp.zeros((TILE, TILE), jnp.float32)
        left_ref[t] = rows_ref[:, t * TILE:(t + 1) * TILE]
    row_ids = lax.broadcasted_iota(jnp.int32, (TILE, TILE), 0)
    lane_ids = lax.broadcasted_iota(jnp.int32, (TILE, TILE), 1)
    unit = jnp.where(row_ids == lane_ids, 1.0, 0.0).astype(jnp.float32)

    def panel_step(p, carry):
        rows = pl.ds(pl.multiple_of(p * TILE, TILE), TILE)
        for t in range(panels):
            panel_ref[:, t * TILE:(t + 1) * TILE] = work_ref[(p + t) % panels, rows, :]
        panel_ref[:, rank:rank + TILE] = unit
        eliminate(panel_ref, spread_ref)
        solved = lax.dot_general(
            left_ref[p], panel_ref[:, rank:rank + TILE], (((1,), (1,)), ((), ())), precision=highest,
            preferred_element_type=jnp.float32,
        )
        for t in range(panels):
            @pl.when(p == t)
            def _():
                out_ref[:, t * TILE:(t + 1) * TILE] = solved
                if rounded:
                    round_ref[:, t * TILE:(t + 1) * TILE] = solved.astype(jnp.bfloat16)
        @pl.when(p < panels - 1)
        def _():
            across = panel_ref[:, TILE:rank]
            moved = jnp.dot(solved, across, precision=highest, preferred_element_type=jnp.float32)
            update = lax.dot_general(
                across, across, (((0,), (0,)), ((), ())), precision=highest,
                preferred_element_type=jnp.float32,
            )
            for t in range(1, panels):
                tile = (p + t) % panels
                lanes = slice((t - 1) * TILE, t * TILE)
                left_ref[tile] = left_ref[tile] - moved[:, lanes]
                for u in range(1, panels):
                    under = pl.ds(pl.multiple_of((p + u) % panels * TILE, TILE), TILE)
                    work_ref[tile, under, :] = (
                        work_ref[tile, under, :] - update[(u - 1) * TILE:u * TILE, lanes]
                    )
        return carry

    lax.fori_loop(0, panels, panel_step, 0)


def orthonormal(matrix, gram, total_rows, rounded):
    rank = matrix.shape[1]
    wide = jax.ShapeDtypeStruct(matrix.shape, jnp.float32)
    narrow = jax.ShapeDtypeStruct(matrix.shape, jnp.bfloat16)
    return pl.pallas_call(
        functools.partial(orth_kernel, scale=1.0 / total_rows, rounded=rounded),
        out_shape=(narrow, wide) if rounded else wide,
        scratch_shapes=[
            pltpu.VMEM((rank // TILE, rank, TILE), jnp.float32),
            pltpu.VMEM((rank // TILE, matrix.shape[0], TILE), jnp.float32),
            pltpu.VMEM((TILE, rank + TILE), jnp.float32),
            pltpu.VMEM((2, SUB, SUB, TILE), jnp.float32),
        ],
        compiler_params=pltpu.CompilerParams(vmem_limit_bytes=VMEM_BYTES),
        name="orth",
    )(gram, matrix)


def along(axis, step):
    pairs = []
    for y in range(RING):
        for x in range(RING):
            for core in range(2):
                to = {
                    "y": ((y + step) % RING, x, core),
                    "x": (y, (x + step) % RING, core),
                    "core": (y, x, 1 - core),
                }[axis]
                pairs.append(((y * RING + x) * 2 + core, (to[0] * RING + to[1]) * 2 + to[2]))
    return pairs


def to_suf(value, step):
    return lax.ppermute(value, "suf", [(s, (s + step) % RING) for s in range(RING)])


def to_pre(value, axis, step=1):
    return lax.ppermute(value, "pre", along(axis, step))


def gather_suf(value):
    return jnp.concatenate([value] + [to_suf(value, -k) for k in range(1, RING)], axis=0)


def gather_pre(value, core, beside=None):
    held = value[None]
    for axis in ("y", "x"):
        held = jnp.stack([held] + [to_pre(held, axis, -k) for k in range(1, RING)], axis=0)
    held = jnp.swapaxes(held[:, :, 0], 0, 1)
    if beside is not None:
        held, beside = lax.optimization_barrier((held, beside))
    other = to_pre(held, "core")
    first = jnp.where(core == 0, held, other)
    second = jnp.where(core == 0, other, held)
    full = jnp.stack([first, second], axis=2)
    full = full.reshape(-1, value.shape[-1])
    return full if beside is None else (full, beside)


def scatter_suf(chunks):
    moved = {k: to_suf(chunks[k], k) for k in (2, 1, 3)}
    return [chunks[0]] + [moved[k] for k in (1, 2, 3)]


def scatter_pre(partial_value, core):
    rows, columns = partial_value.shape
    share = rows // (RING * RING * 2)
    held = partial_value.reshape(RING, RING, 2, share, columns)
    mine = jnp.where(core == 0, held[:, :, 0], held[:, :, 1])
    theirs = jnp.where(core == 0, held[:, :, 1], held[:, :, 0])
    held = mine + to_pre(theirs, "core")
    upper, lower = held[:, :, :share // 2], held[:, :, share // 2:]
    upper_parts = [upper[k] if k == 0 else to_pre(upper[k], "y", k) for k in range(RING)]
    lower_parts = [lower[:, k] if k == 0 else to_pre(lower[:, k], "x", k) for k in range(RING)]
    upper, lower = sum(upper_parts[1:], upper_parts[0]), sum(lower_parts[1:], lower_parts[0])
    upper_parts = [upper[k] if k == 0 else to_pre(upper[k], "x", k) for k in range(RING)]
    lower_parts = [lower[k] if k == 0 else to_pre(lower[k], "y", k) for k in range(RING)]
    return [jnp.concatenate(pair, axis=0) for pair in zip(upper_parts, lower_parts)]


def swap_chips(value):
    groups = [[chip * 2 + core for chip in range(RING * RING)] for core in range(2)]
    return lax.all_to_all(value, "pre", 0, 0, axis_index_groups=groups, tiled=True)


def sum_all(gram, core):
    rows, lanes = gram.shape
    chips = RING * RING
    half = rows // 2
    low, high = gram[:half], gram[half:]
    mine = jnp.where(core == 0, low, high)
    mine = mine + to_pre(jnp.where(core == 0, high, low), "core")
    pieces = swap_chips(mine)
    piece = jnp.sum(pieces.reshape(chips, half // chips, lanes), axis=0)
    parts = [piece] + [to_suf(piece, k) for k in range(1, RING)]
    total = sum(parts[1:], parts[0])
    spread = jnp.broadcast_to(total[None], (chips,) + total.shape).reshape(half, lanes)
    mine = swap_chips(spread)
    other = to_pre(mine, "core")
    low = jnp.where(core == 0, mine, other)
    high = jnp.where(core == 0, other, mine)
    return jnp.concatenate([low, high], axis=0)


def local(values, block_rows, block_cols, block_count, test_matrix):
    pre, suf = lax.axis_index("pre"), lax.axis_index("suf")
    core, x, y = pre % 2, pre // 2 % RING, pre // (2 * RING)
    prefix_total = PB * BLK * lax.axis_size("pre")
    suffix_total = SB * BLK * lax.axis_size("suf")
    row_ids = ((block_rows[0] // RING - suf) % RING) * RING + block_rows[0] % RING
    col_ids = ((block_cols[0] // RING - y) % RING) * RING + (block_cols[0] % RING - x) % RING
    dense = dense_blocks(values[0], row_ids, col_ids, block_count)
    panel, dense = gather_pre(test_matrix, core, dense)
    share_rows = PB * BLK // RING

    def prefix_sums(panel):
        chunks = [None] * RING
        for k in (2, 1, 3, 0):
            chunks[k] = jnp.dot(
                dense[k * share_rows:(k + 1) * share_rows], panel,
                preferred_element_type=jnp.float32,
            )
        return sum_and_gram(scatter_suf(chunks))

    sketch, gram = prefix_sums(panel)
    first_rounded, _ = orthonormal(sketch, sum_all(gram, core), prefix_total, True)
    suffix_partial = lax.dot_general(
        dense, gather_suf(first_rounded), (((0,), (0,)), ((), ())),
        preferred_element_type=jnp.float32,
    )
    suffix_raw, gram = sum_and_gram(scatter_pre(suffix_partial, core))
    suffix_rounded, suffix_basis = orthonormal(
        suffix_raw, sum_all(gram, core), suffix_total, True
    )
    refined, gram = prefix_sums(gather_pre(suffix_rounded, core))
    prefix_basis = orthonormal(refined, sum_all(gram, core), prefix_total, False)
    return (prefix_basis, suffix_basis)


def solution(mesh):
    in_specs = (
        P(("pre", "suf"), None, None, None),
        P(("pre", "suf"), None),
        P(("pre", "suf"), None),
        P(("pre", "suf")),
        P(("suf", "pre"), None),
    )
    out_specs = (P(("pre", "suf"), None), P(("suf", "pre"), None))
    return jax.shard_map(local, mesh=mesh, in_specs=in_specs, out_specs=out_specs, check_vma=False)
```

time: 528 us -> 449 us (0.85)
  blocking collectives: 140 us -> 74.9 us
  Pallas kernels: 113 us -> 86.9 us
  starting transfers between devices: 49.6 us -> 71.1 us
  waiting for transfers between devices: 186 us -> 179 us
    all_to_all x6, blocking collectives: 140 us -> 74.9 us  [swap_chips(): lax.all_to_all(value, 'pre', 0, 0, axis_index_groups=groups, tiled=True)]
    pallas_call x3, Pallas kernels: 107 us -> 76 us  [orthonormal(): pl.pallas_call(functools.partial(orth_kernel, scale=1.0 / total_rows, rou...]
    ppermute x21 -> x33, starting transfers between devices: 27.4 us -> 49.4 us  [to_pre(): return lax.ppermute(value, 'pre', along(axis, step))]
    ppermute x21 -> x33, waiting for transfers between devices: 61.6 us -> 58.1 us  [to_pre(): return lax.ppermute(value, 'pre', along(axis, step))]
  transfers between devices with their start and end apart: 39 -> 51, of which waited for: 28 -> 36; matrix products, arithmetic and copies ran while one was open for 0% -> 1% of each run, Pallas kernels for 1% -> 2%
where the time goes in v2:
time: 449 us; the launch traced here: 441 us
  waiting for transfers between devices  179 us (40%)
  Pallas kernels  86.9 us (19%)
  blocking collectives  74.9 us (17%)
  starting transfers between devices  71.1 us (16%)
  matrix products  16.9 us (4%)
  local copies, waits for them, and re-layouts  5.34 us (1%)
  other arithmetic  4.78 us (1%)
    ppermute x18, waiting for transfers between devices, to_suf(): lax.ppermute(value, 'suf', [(s, (s + step) % RING) for s in range(RING)])  121 us
    pallas_call x3, Pallas kernels, orthonormal(): pl.pallas_call(functools.partial(orth_kernel, scale=1.0 / total_rows, rou...  76 us
    all_to_all x6, blocking collectives, swap_chips(): lax.all_to_all(value, 'pre', 0, 0, axis_index_groups=groups, tiled=True)  74.9 us
    ppermute x33, waiting for transfers between devices, to_pre(): return lax.ppermute(value, 'pre', along(axis, step))  58.1 us
    ppermute x33, starting transfers between devices, to_pre(): return lax.ppermute(value, 'pre', along(axis, step))  49.4 us
    ppermute x18, starting transfers between devices, to_suf(): lax.ppermute(value, 'suf', [(s, (s + step) % RING) for s in range(RING)])  21.7 us
    dot_general x8, matrix products, prefix_sums(): jnp.dot(dense[k * share_rows:(k + 1) * share_rows], panel, preferred_elem...  9.97 us
  transfers between devices with their start and end apart: 51, of which 36 were waited for; matrix products, arithmetic and copies ran while one was open for 1% of the time, Pallas kernels for 2%

profile of v2, /device:TPU:1, one launch (start us, length us, event | category | flops | bytes accessed | tf_op | source)
XLA Modules:
  0.0 440.7 jit_solution(155936769935659528)
XLA Ops:
  15.6 6.7 %dense_blocks.1 = bf16[2048,2048]{1,0:T(8,128)(2,1)} custom-call(s32[1]{0:T(128)S(6)} %copy.33.count_ref, s32[192]{0:T(256)S(1)} %get-tuple-element.56.rows_ref, s32[192]{0:T(256)S(1)} %get-tuple-element.55.cols_ref, bf16[192,128,128]{2,1,0:T(8,128)(2,1)} %bitcast.152), custom_call_target="tpu_custom_call" | custom-call | tf_op jit(solution)/shard_map/dense_blocks/pallas_call | solution.py:46
  42.8 20.0 %collective-permute-done.7.refs_1_ = f32[512,512]{1,0:T(8,128)S(1)} collective-permute-done((f32[512,512]{1,0:T(8,128)S(1)}, f32[512,512]{1,0:T(8,128)S(1)}, u32[]{:S(2)}, u32[]{:S(2)}) %collective-permute-start.7) | collective-permute-done | bytes 1048608 | tf_op jit(solution)/shard_map/ppermute | solution.py:247
  62.9 23.3 %collective-permute-done.8.refs_2_ = f32[512,512]{1,0:T(8,128)S(1)} collective-permute-done((f32[512,512]{1,0:T(8,128)S(1)}, f32[512,512]{1,0:T(8,128)S(1)}, u32[]{:S(2)}, u32[]{:S(2)}) %collective-permute-start.8) | collective-permute-done | bytes 1048608 | tf_op jit(solution)/shard_map/ppermute | solution.py:247
  90.6 14.4 %all_to_all.54 = f32[16,40,128]{2,1,0:T(8,128)S(1)} all-to-all(f32[16,40,128]{2,1,0:T(8,128)S(1)} %bitcast.164), channel_id=1, replica_groups={{0,8,16,24,32,40,48,56,64,72,80,88,96,104,112,120},{4,12,20,28,36,44,52..., dimensions={0} | all-to-all | bytes 655360 | tf_op jit(solution)/shard_map/all_to_all | solution.py:296
  111.7 10.7 %all_to_all.55 = f32[16,40,128]{2,1,0:T(8,128)S(1)} all-to-all(f32[16,40,128]{2,1,0:T(8,128)S(1)} %broadcast_in_dim.11), channel_id=1, replica_groups={{0,8,16,24,32,40,48,56,64,72,80,88,96,104,112,120},{4,12,20,28,36,44,52..., dimensions={0} | all-to-all | bytes 655360 | tf_op jit(solution)/shard_map/all_to_all | solution.py:296
  122.4 4.9 %collective-permute-start.14 = (f32[640,128]{1,0:T(8,128)S(1)}, f32[640,128]{1,0:T(8,128)S(1)}, u32[]{:S(2)}, u32[]{:S(2)}) collective-permute-start(f32[640,128]{1,0:T(8,128)S(1)} %bitcast.162), channel_id=1, source_target_pairs={{0,4},{4,0},{8,12},{12,8},{16,20},{20,16},{24,28},{28,24},{32,36},... | collective-permute-start | bytes 983048 | tf_op jit(solution)/shard_map/ppermute | solution.py:251
  128.7 26.4 %orth.3 = (bf16[512,512]{1,0:T(8,128)(2,1)S(1)}, f32[512,512]{1,0:T(8,128)}) custom-call(f32[1280,128]{1,0:T(8,128)S(1)} %pad_maximum_fusion.2.gram_ref, f32[512,512]{1,0:T(8,128)S(1)} %get-tuple-element.16.rows_ref), custom_call_target="tpu_custom_call" | custom-call | tf_op jit(solution)/shard_map/orth/pallas_call | solution.py:218
  158.0 22.6 %collective-permute-done.17 = bf16[512,512]{1,0:T(8,128)(2,1)S(1)} collective-permute-done((bf16[512,512]{1,0:T(8,128)(2,1)S(1)}, bf16[512,512]{1,0:T(8,128)(2,1)S(1)}, u32[]{:S(2)}, u32[]{:S(2)}) %collective-permute-start.17) | collective-permute-done | bytes 524320 | tf_op jit(solution)/shard_map/ppermute | solution.py:247
  181.0 7.0 %fusion = f32[2048,512]{1,0:T(8,128)S(1)} fusion(bf16[2048,2048]{1,0:T(8,128)(2,1)} %dense_blocks.1, bf16[512,512]{1,0:T(8,128)(2,1)S(1)} %collective-permute-done.17, bf16[512,512]{1,0:T(8,128)(2,1)S(1)} %collective-permute-done.16, bf16[512,512]{1,0:T(8,128)(2,1)S(1)} %collective-permute-done.15, bf16[512,512]{1,0:T(8,128)(2,1)S(1)} %get-tuple-element.17), kind=kOutput, calls=%fused_computation.3 | convolution fusion | flops 4303355904 | bytes 14680064 | tf_op jit(solution)/shard_map/dot_general | solution.py:340
  190.0 3.8 collective-permute-done.18
  200.4 8.6 %collective-permute-done.22 = f32[4,32,512]{2,1,0:T(8,128)S(1)} collective-permute-done((f32[4,32,512]{2,1,0:T(8,128)S(1)}, f32[4,32,512]{2,1,0:T(8,128)S(1)}, u32[]{:S(2)}, u32[]{:S(2)}) %collective-permute-start.22) | collective-permute-done | bytes 262176 | tf_op jit(solution)/shard_map/ppermute | solution.py:251
  209.4 7.7 %collective-permute-done.20 = f32[4,32,512]{2,1,0:T(8,128)S(1)} collective-permute-done((f32[4,32,512]{2,1,0:T(8,128)S(1)}, f32[4,32,512]{2,1,0:T(8,128)S(1)}, u32[]{:S(2)}, u32[]{:S(2)}) %collective-permute-start.20) | collective-permute-done | bytes 262176 | tf_op jit(solution)/shard_map/ppermute | solution.py:251
  226.0 4.3 collective-permute-start.31
  231.5 14.7 %all_to_all.56 = f32[16,40,128]{2,1,0:T(8,128)S(1)} all-to-all(f32[16,40,128]{2,1,0:T(8,128)S(1)} %bitcast.165), channel_id=1, replica_groups={{0,8,16,24,32,40,48,56,64,72,80,88,96,104,112,120},{4,12,20,28,36,44,52..., dimensions={0} | all-to-all | bytes 655360 | tf_op jit(solution)/shard_map/all_to_all | solution.py:296
  252.9 10.9 %all_to_all.57 = f32[16,40,128]{2,1,0:T(8,128)S(1)} all-to-all(f32[16,40,128]{2,1,0:T(8,128)S(1)} %broadcast_in_dim.12), channel_id=1, replica_groups={{0,8,16,24,32,40,48,56,64,72,80,88,96,104,112,120},{4,12,20,28,36,44,52..., dimensions={0} | all-to-all | bytes 655360 | tf_op jit(solution)/shard_map/all_to_all | solution.py:296
  263.7 4.0 collective-permute-start.35
  269.1 23.2 %orth.4 = (bf16[64,512]{1,0:T(8,128)(2,1)S(1)}, f32[64,512]{1,0:T(8,128)}) custom-call(f32[1280,128]{1,0:T(8,128)S(1)} %pad_maximum_fusion.3.gram_ref, f32[64,512]{1,0:T(8,128)S(1)} %get-tuple-element.19.rows_ref), custom_call_target="tpu_custom_call" | custom-call | tf_op jit(solution)/shard_map/orth/pallas_call | solution.py:218
  295.0 3.6 collective-permute-done.38
  301.6 5.9 %collective-permute-done.41 = bf16[4,1,64,512]{3,2,1,0:T(8,128)(2,1)S(1)} collective-permute-done((bf16[4,1,64,512]{3,2,1,0:T(8,128)(2,1)S(1)}, bf16[4,1,64,512]{3,2,1,0:T(8,128)(2,1)S(1)}, u32[]{:S(2)}, u32[]{:S(2)}) %collective-permute-start.41) | collective-permute-done | bytes 262176 | tf_op jit(solution)/shard_map/ppermute | solution.py:251
  328.8 43.0 %collective-permute-done.43.refs_1_ = f32[512,512]{1,0:T(8,128)S(1)} collective-permute-done((f32[512,512]{1,0:T(8,128)S(1)}, f32[512,512]{1,0:T(8,128)S(1)}, u32[]{:S(2)}, u32[]{:S(2)}) %collective-permute-start.43) | collective-permute-done | bytes 1048608 | tf_op jit(solution)/shard_map/ppermute | solution.py:247
  376.8 13.5 %all_to_all.58 = f32[16,40,128]{2,1,0:T(8,128)S(1)} all-to-all(f32[16,40,128]{2,1,0:T(8,128)S(1)} %bitcast.166), channel_id=1, replica_groups={{0,8,16,24,32,40,48,56,64,72,80,88,96,104,112,120},{4,12,20,28,36,44,52..., dimensions={0} | all-to-all | bytes 655360 | tf_op jit(solution)/shard_map/all_to_all | solution.py:296
  397.2 10.7 %all_to_all.59 = f32[16,40,128]{2,1,0:T(8,128)S(1)} all-to-all(f32[16,40,128]{2,1,0:T(8,128)S(1)} %broadcast_in_dim.28), channel_id=1, replica_groups={{0,8,16,24,32,40,48,56,64,72,80,88,96,104,112,120},{4,12,20,28,36,44,52..., dimensions={0} | all-to-all | bytes 655360 | tf_op jit(solution)/shard_map/all_to_all | solution.py:296
  407.9 4.6 %collective-permute-start.50 = (f32[640,128]{1,0:T(8,128)S(1)}, f32[640,128]{1,0:T(8,128)S(1)}, u32[]{:S(2)}, u32[]{:S(2)}) collective-permute-start(f32[640,128]{1,0:T(8,128)S(1)} %bitcast.161), channel_id=1, source_target_pairs={{0,4},{4,0},{8,12},{12,8},{16,20},{20,16},{24,28},{28,24},{32,36},... | collective-permute-start | bytes 983048 | tf_op jit(solution)/shard_map/ppermute | solution.py:251
  413.9 26.4 %orth.5 = f32[512,512]{1,0:T(8,128)} custom-call(f32[1280,128]{1,0:T(8,128)S(1)} %pad_maximum_fusion.4.gram_ref, f32[512,512]{1,0:T(8,128)S(1)} %get-tuple-element.22.rows_ref), custom_call_target="tpu_custom_call" | custom-call | tf_op jit(solution)/shard_map/orth/pallas_call | solution.py:218
  (150 shorter events, 117.7 us)
Async XLA Ops:
  10.0 12.4 %collective-permute-start.4 = (bf16[4,1,64,512]{3,2,0,1:T(8,128)(2,1)S(1)}, bf16[4,1,64,512]{3,2,0,1:T(8,128)(2,1)S(1)}, u32[]{:S(2)}, u32[]{:S(2)}) collective-permute-start(bf16[4,1,64,512]{3,2,0,1:T(8,128)(2,1)S(1)} %get-tuple-element.54), channel_id=1, source_target_pairs={{0,16},{4,20},{8,24},{12,28},{16,0},{20,4},{24,8},{28,12},{32,48},... | collective-permute-start | bytes 786440 | tf_op jit(solution)/shard_map/ppermute | solution.py:251
  12.8 11.4 %collective-permute-start.3 = (bf16[4,1,64,512]{3,2,0,1:T(8,128)(2,1)S(1)}, bf16[4,1,64,512]{3,2,0,1:T(8,128)(2,1)S(1)}, u32[]{:S(2)}, u32[]{:S(2)}) collective-permute-start(bf16[4,1,64,512]{3,2,0,1:T(8,128)(2,1)S(1)} %get-tuple-element.54), channel_id=1, source_target_pairs={{0,24},{4,28},{8,0},{12,4},{16,8},{20,12},{24,16},{28,20},{32,56},... | collective-permute-start | bytes 786440 | tf_op jit(solution)/shard_map/ppermute | solution.py:251
  13.6 10.6 %collective-permute-start.5 = (bf16[4,1,64,512]{3,2,0,1:T(8,128)(2,1)S(1)}, bf16[4,1,64,512]{3,2,0,1:T(8,128)(2,1)S(1)}, u32[]{:S(2)}, u32[]{:S(2)}) collective-permute-start(bf16[4,1,64,512]{3,2,0,1:T(8,128)(2,1)S(1)} %get-tuple-element.54), channel_id=1, source_target_pairs={{0,8},{4,12},{8,16},{12,20},{16,24},{20,28},{24,0},{28,4},{32,40},... | collective-permute-start | bytes 786440 | tf_op jit(solution)/shard_map/ppermute | solution.py:251
  35.8 27.0 %collective-permute-start.7 = (f32[512,512]{1,0:T(8,128)S(1)}, f32[512,512]{1,0:T(8,128)S(1)}, u32[]{:S(2)}, u32[]{:S(2)}) collective-permute-start(f32[512,512]{1,0:T(8,128)S(1)} %fusion.18), channel_id=1, source_target_pairs={{0,1},{1,2},{2,3},{3,0},{4,5},{5,6},{6,7},{7,4},{8,9},{9,10},{10,1... | collective-permute-start | bytes 3145736 | tf_op jit(solution)/shard_map/ppermute | solution.py:247
  37.5 48.7 %collective-permute-start.8 = (f32[512,512]{1,0:T(8,128)S(1)}, f32[512,512]{1,0:T(8,128)S(1)}, u32[]{:S(2)}, u32[]{:S(2)}) collective-permute-start(f32[512,512]{1,0:T(8,128)S(1)} %fusion.14), channel_id=1, source_target_pairs={{0,2},{1,3},{2,0},{3,1},{4,6},{5,7},{6,4},{7,5},{8,10},{9,11},{10,... | collective-permute-start | bytes 3145736 | tf_op jit(solution)/shard_map/ppermute | solution.py:247
  40.8 45.4 %collective-permute-start.9 = (f32[512,512]{1,0:T(8,128)S(1)}, f32[512,512]{1,0:T(8,128)S(1)}, u32[]{:S(2)}, u32[]{:S(2)}) collective-permute-start(f32[512,512]{1,0:T(8,128)S(1)} %fusion.10), channel_id=1, source_target_pairs={{0,3},{1,0},{2,1},{3,2},{4,7},{5,4},{6,5},{7,6},{8,11},{9,8},{10,9... | collective-permute-start | bytes 3145736 | tf_op jit(solution)/shard_map/ppermute | solution.py:247
  155.1 25.6 %collective-permute-start.17 = (bf16[512,512]{1,0:T(8,128)(2,1)S(1)}, bf16[512,512]{1,0:T(8,128)(2,1)S(1)}, u32[]{:S(2)}, u32[]{:S(2)}) collective-permute-start(bf16[512,512]{1,0:T(8,128)(2,1)S(1)} %get-tuple-element.17), channel_id=1, source_target_pairs={{0,1},{1,2},{2,3},{3,0},{4,5},{5,6},{6,7},{7,4},{8,9},{9,10},{10,1... | collective-permute-start | bytes 1572872 | tf_op jit(solution)/shard_map/ppermute | solution.py:247
  155.1 25.6 %collective-permute-start.16 = (bf16[512,512]{1,0:T(8,128)(2,1)S(1)}, bf16[512,512]{1,0:T(8,128)(2,1)S(1)}, u32[]{:S(2)}, u32[]{:S(2)}) collective-permute-start(bf16[512,512]{1,0:T(8,128)(2,1)S(1)} %get-tuple-element.17), channel_id=1, source_target_pairs={{0,2},{1,3},{2,0},{3,1},{4,6},{5,7},{6,4},{7,5},{8,10},{9,11},{10,... | collective-permute-start | bytes 1572872 | tf_op jit(solution)/shard_map/ppermute | solution.py:247
  156.2 24.8 %collective-permute-start.15 = (bf16[512,512]{1,0:T(8,128)(2,1)S(1)}, bf16[512,512]{1,0:T(8,128)(2,1)S(1)}, u32[]{:S(2)}, u32[]{:S(2)}) collective-permute-start(bf16[512,512]{1,0:T(8,128)(2,1)S(1)} %get-tuple-element.17), channel_id=1, source_target_pairs={{0,3},{1,0},{2,1},{3,2},{4,7},{5,4},{6,5},{7,6},{8,11},{9,8},{10,9... | collective-permute-start | bytes 1572872 | tf_op jit(solution)/shard_map/ppermute | solution.py:247
  194.7 14.4 %collective-permute-start.22 = (f32[4,32,512]{2,1,0:T(8,128)S(1)}, f32[4,32,512]{2,1,0:T(8,128)S(1)}, u32[]{:S(2)}, u32[]{:S(2)}) collective-permute-start(f32[4,32,512]{2,1,0:T(8,128)S(1)} %get-tuple-element.31), channel_id=1, source_target_pairs={{0,8},{4,12},{8,16},{12,20},{16,24},{20,28},{24,0},{28,4},{32,40},... | collective-permute-start | bytes 786440 | tf_op jit(solution)/shard_map/ppermute | solution.py:251
  195.0 14.1 %collective-permute-start.23 = (f32[4,32,512]{2,1,0:T(8,128)S(1)}, f32[4,32,512]{2,1,0:T(8,128)S(1)}, u32[]{:S(2)}, u32[]{:S(2)}) collective-permute-start(f32[4,32,512]{2,1,0:T(8,128)S(1)} %get-tuple-element.32), channel_id=1, source_target_pairs={{0,16},{4,20},{8,24},{12,28},{16,0},{20,4},{24,8},{28,12},{32,48},... | collective-permute-start | bytes 786440 | tf_op jit(solution)/shard_map/ppermute | solution.py:251
  196.2 13.2 %collective-permute-start.24 = (f32[4,32,512]{2,1,0:T(8,128)S(1)}, f32[4,32,512]{2,1,0:T(8,128)S(1)}, u32[]{:S(2)}, u32[]{:S(2)}) collective-permute-start(f32[4,32,512]{2,1,0:T(8,128)S(1)} %get-tuple-element.33), channel_id=1, source_target_pairs={{0,24},{4,28},{8,0},{12,4},{16,8},{20,12},{24,16},{28,20},{32,56},... | collective-permute-start | bytes 786440 | tf_op jit(solution)/shard_map/ppermute | solution.py:251
  197.5 11.9 %collective-permute-start.19 = (f32[4,32,512]{2,1,0:T(8,128)S(1)}, f32[4,32,512]{2,1,0:T(8,128)S(1)}, u32[]{:S(2)}, u32[]{:S(2)}) collective-permute-start(f32[4,32,512]{2,1,0:T(8,128)S(1)} %get-tuple-element.28), channel_id=1, source_target_pairs={{0,32},{4,36},{8,40},{12,44},{16,48},{20,52},{24,56},{28,60},{32,6... | collective-permute-start | bytes 786440 | tf_op jit(solution)/shard_map/ppermute | solution.py:251
  197.8 11.6 %collective-permute-start.21 = (f32[4,32,512]{2,1,0:T(8,128)S(1)}, f32[4,32,512]{2,1,0:T(8,128)S(1)}, u32[]{:S(2)}, u32[]{:S(2)}) collective-permute-start(f32[4,32,512]{2,1,0:T(8,128)S(1)} %get-tuple-element.29), channel_id=1, source_target_pairs={{0,96},{4,100},{8,104},{12,108},{16,112},{20,116},{24,120},{28,124... | collective-permute-start | bytes 786440 | tf_op jit(solution)/shard_map/ppermute | solution.py:251
  209.1 8.1 %collective-permute-start.20 = (f32[4,32,512]{2,1,0:T(8,128)S(1)}, f32[4,32,512]{2,1,0:T(8,128)S(1)}, u32[]{:S(2)}, u32[]{:S(2)}) collective-permute-start(f32[4,32,512]{2,1,0:T(8,128)S(1)} %get-tuple-element.30), channel_id=1, source_target_pairs={{0,64},{4,68},{8,72},{12,76},{16,80},{20,84},{24,88},{28,92},{32,9... | collective-permute-start | bytes 786440 | tf_op jit(solution)/shard_map/ppermute | solution.py:251
  217.6 6.2 %collective-permute-start.25 = (f32[32,512]{1,0:T(8,128)S(1)}, f32[32,512]{1,0:T(8,128)S(1)}, u32[]{:S(2)}, u32[]{:S(2)}) collective-permute-start(f32[32,512]{1,0:T(8,128)S(1)} %get-tuple-element.47), channel_id=1, source_target_pairs={{0,8},{4,12},{8,16},{12,20},{16,24},{20,28},{24,0},{28,4},{32,40},... | collective-permute-start | bytes 196616 | tf_op jit(solution)/shard_map/ppermute | solution.py:251
  292.3 6.2 %collective-permute-start.38 = (bf16[1,64,512]{2,1,0:T(8,128)(2,1)S(1)}, bf16[1,64,512]{2,1,0:T(8,128)(2,1)S(1)}, u32[]{:S(2)}, u32[]{:S(2)}) collective-permute-start(bf16[1,64,512]{2,1,0:T(8,128)(2,1)S(1)} %bitcast.144), channel_id=1, source_target_pairs={{0,32},{4,36},{8,40},{12,44},{16,48},{20,52},{24,56},{28,60},{32,6... | collective-permute-start | bytes 196616 | tf_op jit(solution)/shard_map/ppermute | solution.py:251
  292.3 6.2 %collective-permute-start.37 = (bf16[1,64,512]{2,1,0:T(8,128)(2,1)S(1)}, bf16[1,64,512]{2,1,0:T(8,128)(2,1)S(1)}, u32[]{:S(2)}, u32[]{:S(2)}) collective-permute-start(bf16[1,64,512]{2,1,0:T(8,128)(2,1)S(1)} %bitcast.145), channel_id=1, source_target_pairs={{0,64},{4,68},{8,72},{12,76},{16,80},{20,84},{24,88},{28,92},{32,9... | collective-permute-start | bytes 196616 | tf_op jit(solution)/shard_map/ppermute | solution.py:251
  298.6 8.9 %collective-permute-start.41 = (bf16[4,1,64,512]{3,2,1,0:T(8,128)(2,1)S(1)}, bf16[4,1,64,512]{3,2,1,0:T(8,128)(2,1)S(1)}, u32[]{:S(2)}, u32[]{:S(2)}) collective-permute-start(bf16[4,1,64,512]{3,2,1,0:T(8,128)(2,1)S(1)} %get-tuple-element.44), channel_id=1, source_target_pairs={{0,8},{4,12},{8,16},{12,20},{16,24},{20,28},{24,0},{28,4},{32,40},... | collective-permute-start | bytes 786440 | tf_op jit(solution)/shard_map/ppermute | solution.py:251
  299.0 11.6 %collective-permute-start.40 = (bf16[4,1,64,512]{3,2,0,1:T(8,128)(2,1)S(1)}, bf16[4,1,64,512]{3,2,0,1:T(8,128)(2,1)S(1)}, u32[]{:S(2)}, u32[]{:S(2)}) collective-permute-start(bf16[4,1,64,512]{3,2,0,1:T(8,128)(2,1)S(1)} %get-tuple-element.43), channel_id=1, source_target_pairs={{0,16},{4,20},{8,24},{12,28},{16,0},{20,4},{24,8},{28,12},{32,48},... | collective-permute-start | bytes 786440 | tf_op jit(solution)/shard_map/ppermute | solution.py:251
  300.3 12.8 %collective-permute-start.39 = (bf16[4,1,64,512]{3,2,0,1:T(8,128)(2,1)S(1)}, bf16[4,1,64,512]{3,2,0,1:T(8,128)(2,1)S(1)}, u32[]{:S(2)}, u32[]{:S(2)}) collective-permute-start(bf16[4,1,64,512]{3,2,0,1:T(8,128)(2,1)S(1)} %get-tuple-element.43), channel_id=1, source_target_pairs={{0,24},{4,28},{8,0},{12,4},{16,8},{20,12},{24,16},{28,20},{32,56},... | collective-permute-start | bytes 786440 | tf_op jit(solution)/shard_map/ppermute | solution.py:251
  323.7 48.1 %collective-permute-start.43 = (f32[512,512]{1,0:T(8,128)S(1)}, f32[512,512]{1,0:T(8,128)S(1)}, u32[]{:S(2)}, u32[]{:S(2)}) collective-permute-start(f32[512,512]{1,0:T(8,128)S(1)} %fusion.16), channel_id=1, source_target_pairs={{0,1},{1,2},{2,3},{3,0},{4,5},{5,6},{6,7},{7,4},{8,9},{9,10},{10,1... | collective-permute-start | bytes 3145736 | tf_op jit(solution)/shard_map/ppermute | solution.py:247
  323.7 48.0 %collective-permute-start.44 = (f32[512,512]{1,0:T(8,128)S(1)}, f32[512,512]{1,0:T(8,128)S(1)}, u32[]{:S(2)}, u32[]{:S(2)}) collective-permute-start(f32[512,512]{1,0:T(8,128)S(1)} %fusion.12), channel_id=1, source_target_pairs={{0,2},{1,3},{2,0},{3,1},{4,6},{5,7},{6,4},{7,5},{8,10},{9,11},{10,... | collective-permute-start | bytes 3145736 | tf_op jit(solution)/shard_map/ppermute | solution.py:247
  325.6 46.5 %collective-permute-start.45 = (f32[512,512]{1,0:T(8,128)S(1)}, f32[512,512]{1,0:T(8,128)S(1)}, u32[]{:S(2)}, u32[]{:S(2)}) collective-permute-start(f32[512,512]{1,0:T(8,128)S(1)} %fusion.8), channel_id=1, source_target_pairs={{0,3},{1,0},{2,1},{3,2},{4,7},{5,4},{6,5},{7,6},{8,11},{9,8},{10,9... | collective-permute-start | bytes 3145736 | tf_op jit(solution)/shard_map/ppermute | solution.py:247
  (30 other events, 170.2 us)

commit v3 on v2

--- a/solution.py
+++ b/solution.py
@@ -59,13 +59,21 @@
     return [(p, t) for p in range(panels) for t in range(p, panels)]
 
 
-def gram_kernel(*refs):
-    parts, (total_ref, gram_ref) = refs[:-2], refs[-2:]
-    total = parts[0][...]
-    for part in parts[1:]:
-        total = total + part[...]
-    total_ref[...] = total
-    rank = total.shape[1]
+def gram_kernel(*refs, count):
+    parts, (left_ref, right_ref, gram_ref) = refs[:-3], refs[-3:]
+    rows, half = left_ref.shape
+    whole = len(parts) == count
+    for total_ref, mine, lane in (
+        (left_ref, parts[:count], 0), (right_ref, parts if whole else parts[count:], half if whole else 0)
+    ):
+        total = None
+        for part in mine:
+            for at in range(0, part.shape[0], rows):
+                chunk = part[at:at + rows, lane:lane + half]
+                total = chunk if total is None else total + chunk
+        total_ref[...] = total
+    total = jnp.concatenate([left_ref[...], right_ref[...]], axis=1)
+    rank = 2 * half
     at = 0
     for p in range(rank // TILE):
         row = lax.dot_general(
@@ -77,18 +85,16 @@
             at += TILE
 
 
-def sum_and_gram(parts):
-    rows, rank = parts[0].shape
-    packed = len(tile_pairs(rank)) * TILE
+def sum_and_gram(left_parts, right_parts, rows):
+    half = left_parts[0].shape[1] // (1 if right_parts else 2)
+    packed = len(tile_pairs(2 * half)) * TILE
+    share = jax.ShapeDtypeStruct((rows, half), jnp.float32)
     return pl.pallas_call(
-        gram_kernel,
-        out_shape=(
-            jax.ShapeDtypeStruct((rows, rank), jnp.float32),
-            jax.ShapeDtypeStruct((packed, TILE), jnp.float32),
-        ),
+        functools.partial(gram_kernel, count=len(left_parts)),
+        out_shape=(share, share, jax.ShapeDtypeStruct((packed, TILE), jnp.float32)),
         compiler_params=pltpu.CompilerParams(vmem_limit_bytes=VMEM_BYTES),
         name="gram",
-    )(*parts)
+    )(*left_parts, *right_parts)
 
 
 def eliminate(panel_ref, spread_ref):
@@ -152,23 +158,9 @@
                 panel_ref[there, t * TILE:(t + 1) * TILE] = v
 
 
-def orth_kernel(gram_ref, rows_ref, *refs, scale, rounded):
-    if rounded:
-        round_ref, out_ref, work_ref, left_ref, panel_ref, spread_ref = refs
-    else:
-        out_ref, work_ref, left_ref, panel_ref, spread_ref = refs
-    rank = rows_ref.shape[1]
-    panels = rank // TILE
-    pairs = tile_pairs(rank)
-    for t in range(panels):
-        for p in range(panels):
-            rows = slice(p * TILE, (p + 1) * TILE)
-            if (p, t) in pairs:
-                at = pairs.index((p, t)) * TILE
-                work_ref[t, rows, :] = gram_ref[at:at + TILE, :] * scale
-            else:
-                work_ref[t, rows, :] = jnp.zeros((TILE, TILE), jnp.float32)
-        left_ref[t] = rows_ref[:, t * TILE:(t + 1) * TILE]
+def factor_and_solve(work_ref, left_ref, panel_ref, spread_ref, store):
+    panels = work_ref.shape[0]
+    rank = panels * TILE
     row_ids = lax.broadcasted_iota(jnp.int32, (TILE, TILE), 0)
     lane_ids = lax.broadcasted_iota(jnp.int32, (TILE, TILE), 1)
     unit = jnp.where(row_ids == lane_ids, 1.0, 0.0).astype(jnp.float32)
@@ -186,9 +178,8 @@
         for t in range(panels):
             @pl.when(p == t)
             def _():
-                out_ref[:, t * TILE:(t + 1) * TILE] = solved
-                if rounded:
-                    round_ref[:, t * TILE:(t + 1) * TILE] = solved.astype(jnp.bfloat16)
+                store(t, solved)
+
         @pl.when(p < panels - 1)
         def _():
             across = panel_ref[:, TILE:rank]
@@ -211,22 +202,124 @@
     lax.fori_loop(0, panels, panel_step, 0)
 
 
-def orthonormal(matrix, gram, total_rows, rounded):
-    rank = matrix.shape[1]
-    wide = jax.ShapeDtypeStruct(matrix.shape, jnp.float32)
-    narrow = jax.ShapeDtypeStruct(matrix.shape, jnp.bfloat16)
+def tile_of(gram_ref, rank, p, t, scale):
+    at = tile_pairs(rank).index((p, t)) * TILE
+    return gram_ref[at:at + TILE, :] * scale
+
+
+def left_kernel(gram_ref, rows_ref, *refs, scale, rounded):
+    if rounded:
+        round_ref, out_ref, factor_ref, work_ref, left_ref, panel_ref, spread_ref = refs
+    else:
+        out_ref, factor_ref, work_ref, left_ref, panel_ref, spread_ref = refs
+    half = rows_ref.shape[1]
+    panels = half // TILE
+    for t in range(panels):
+        lanes = slice(t * TILE, (t + 1) * TILE)
+        for p in range(panels):
+            rows = slice(p * TILE, (p + 1) * TILE)
+            if p <= t:
+                work_ref[t, rows, :] = tile_of(gram_ref, 2 * half, p, t, scale)
+            else:
+                work_ref[t, rows, :] = jnp.zeros((TILE, TILE), jnp.float32)
+        left_ref[t] = rows_ref[:, lanes]
+
+    def store(t, solved):
+        lanes = slice(t * TILE, (t + 1) * TILE)
+        out_ref[:, lanes] = solved
+        if rounded:
+            round_ref[:, lanes] = solved.astype(jnp.bfloat16)
+        factor_ref[t] = panel_ref[...]
+
+    factor_and_solve(work_ref, left_ref, panel_ref, spread_ref, store)
+
+
+def right_kernel(gram_ref, rows_ref, first_ref, factor_ref, *refs, scale, rounded):
+    if rounded:
+        round_ref, out_ref, work_ref, left_ref, panel_ref, spread_ref = refs
+    else:
+        out_ref, work_ref, left_ref, panel_ref, spread_ref = refs
+    half = rows_ref.shape[1]
+    panels = half // TILE
+    rank = 2 * half
+
+    def dot(a, b, dims):
+        return lax.dot_general(
+            a, b, ((dims[:1], dims[1:]), ((), ())), precision=highest,
+            preferred_element_type=jnp.float32,
+        )
+
+    above = []
+    for p in range(panels):
+        g = jnp.concatenate(
+            [tile_of(gram_ref, rank, p, panels + t, scale) for t in range(panels)], axis=1
+        )
+        for q in range(p):
+            g = g - dot(factor_ref[q, :, (p - q) * TILE:(p - q + 1) * TILE], above[q], (0, 0))
+        above.append(dot(factor_ref[p, :, half:half + TILE], g, (1, 0)))
+    above = jnp.concatenate(above, axis=0)
+    update = dot(above, above, (0, 0))
+    moved = rows_ref[...] - dot(first_ref[...], above, (1, 0))
+    for t in range(panels):
+        lanes = slice(t * TILE, (t + 1) * TILE)
+        for p in range(panels):
+            rows = slice(p * TILE, (p + 1) * TILE)
+            if p <= t:
+                work_ref[t, rows, :] = (
+                    tile_of(gram_ref, rank, panels + p, panels + t, scale) - update[rows, lanes]
+                )
+            else:
+                work_ref[t, rows, :] = jnp.zeros((TILE, TILE), jnp.float32)
+        left_ref[t] = moved[:, lanes]
+    out_ref[:, :half] = first_ref[...]
+
+    def store(t, solved):
+        lanes = slice(t * TILE, (t + 1) * TILE)
+        out_ref[:, half + t * TILE:half + (t + 1) * TILE] = solved
+        if rounded:
+            round_ref[:, lanes] = solved.astype(jnp.bfloat16)
+
+    factor_and_solve(work_ref, left_ref, panel_ref, spread_ref, store)
+
+
+def orth_scratch(rows, half):
+    return [
+        pltpu.VMEM((half // TILE, half, TILE), jnp.float32),
+        pltpu.VMEM((half // TILE, rows, TILE), jnp.float32),
+        pltpu.VMEM((TILE, half + TILE), jnp.float32),
+        pltpu.VMEM((2, SUB, SUB, TILE), jnp.float32),
+    ]
+
+
+def orth_left(matrix, gram, total_rows, rounded):
+    rows, half = matrix.shape
+    outs = [
+        jax.ShapeDtypeStruct((rows, half), jnp.float32),
+        jax.ShapeDtypeStruct((half // TILE, TILE, half + TILE), jnp.float32),
+    ]
+    if rounded:
+        outs.insert(0, jax.ShapeDtypeStruct((rows, half), jnp.bfloat16))
     return pl.pallas_call(
-        functools.partial(orth_kernel, scale=1.0 / total_rows, rounded=rounded),
-        out_shape=(narrow, wide) if rounded else wide,
-        scratch_shapes=[
-            pltpu.VMEM((rank // TILE, rank, TILE), jnp.float32),
-            pltpu.VMEM((rank // TILE, matrix.shape[0], TILE), jnp.float32),
-            pltpu.VMEM((TILE, rank + TILE), jnp.float32),
-            pltpu.VMEM((2, SUB, SUB, TILE), jnp.float32),
-        ],
+        functools.partial(left_kernel, scale=1.0 / total_rows, rounded=rounded),
+        out_shape=tuple(outs),
+        scratch_shapes=orth_scratch(rows, half),
         compiler_params=pltpu.CompilerParams(vmem_limit_bytes=VMEM_BYTES),
-        name="orth",
+        name="orth_left",
     )(gram, matrix)
+
+
+def orth_right(matrix, gram, first, factor, total_rows, rounded):
+    rows, half = matrix.shape
+    outs = [jax.ShapeDtypeStruct((rows, 2 * half), jnp.float32)]
+    if rounded:
+        outs.insert(0, jax.ShapeDtypeStruct((rows, half), jnp.bfloat16))
+    return pl.pallas_call(
+        functools.partial(right_kernel, scale=1.0 / total_rows, rounded=rounded),
+        out_shape=tuple(outs),
+        scratch_shapes=orth_scratch(rows, half),
+        compiler_params=pltpu.CompilerParams(vmem_limit_bytes=VMEM_BYTES),
+        name="orth_right",
+    )(gram, matrix, first, factor)
 
 
 def along(axis, step):
@@ -255,19 +348,24 @@
     return jnp.concatenate([value] + [to_suf(value, -k) for k in range(1, RING)], axis=0)
 
 
-def gather_pre(value, core, beside=None):
-    held = value[None]
-    for axis in ("y", "x"):
-        held = jnp.stack([held] + [to_pre(held, axis, -k) for k in range(1, RING)], axis=0)
-    held = jnp.swapaxes(held[:, :, 0], 0, 1)
-    if beside is not None:
-        held, beside = lax.optimization_barrier((held, beside))
+def swap_chips(value):
+    groups = [[chip * 2 + core for chip in range(RING * RING)] for core in range(2)]
+    return lax.all_to_all(value, "pre", 0, 0, axis_index_groups=groups, tiled=True)
+
+
+def tie(first, second):
+    return lax.optimization_barrier((first, second))
+
+
+def gather_chips(value):
+    return swap_chips(jnp.broadcast_to(value[None], (RING * RING,) + value.shape))
+
+
+def gather_cores(held, core):
     other = to_pre(held, "core")
     first = jnp.where(core == 0, held, other)
     second = jnp.where(core == 0, other, held)
-    full = jnp.stack([first, second], axis=2)
-    full = full.reshape(-1, value.shape[-1])
-    return full if beside is None else (full, beside)
+    return jnp.stack([first, second], axis=1).reshape(-1, held.shape[-1])
 
 
 def scatter_suf(chunks):
@@ -275,25 +373,26 @@
     return [chunks[0]] + [moved[k] for k in (1, 2, 3)]
 
 
-def scatter_pre(partial_value, core):
+def scatter_cores(partial_value, core):
     rows, columns = partial_value.shape
-    share = rows // (RING * RING * 2)
-    held = partial_value.reshape(RING, RING, 2, share, columns)
-    mine = jnp.where(core == 0, held[:, :, 0], held[:, :, 1])
-    theirs = jnp.where(core == 0, held[:, :, 1], held[:, :, 0])
-    held = mine + to_pre(theirs, "core")
-    upper, lower = held[:, :, :share // 2], held[:, :, share // 2:]
-    upper_parts = [upper[k] if k == 0 else to_pre(upper[k], "y", k) for k in range(RING)]
-    lower_parts = [lower[:, k] if k == 0 else to_pre(lower[:, k], "x", k) for k in range(RING)]
-    upper, lower = sum(upper_parts[1:], upper_parts[0]), sum(lower_parts[1:], lower_parts[0])
-    upper_parts = [upper[k] if k == 0 else to_pre(upper[k], "x", k) for k in range(RING)]
-    lower_parts = [lower[k] if k == 0 else to_pre(lower[k], "y", k) for k in range(RING)]
-    return [jnp.concatenate(pair, axis=0) for pair in zip(upper_parts, lower_parts)]
-
-
-def swap_chips(value):
-    groups = [[chip * 2 + core for chip in range(RING * RING)] for core in range(2)]
-    return lax.all_to_all(value, "pre", 0, 0, axis_index_groups=groups, tiled=True)
+    chips = RING * RING
+    held = partial_value.reshape(chips, 2, rows // (chips * 2), columns)
+    mine = jnp.where(core == 0, held[:, 0], held[:, 1])
+    theirs = jnp.where(core == 0, held[:, 1], held[:, 0])
+    return mine + to_pre(theirs, "core")
+
+
+def scatter_chips(held, axes, place):
+    held = held.reshape((RING, RING) + held.shape[1:])
+    if axes[0] == "x":
+        held = jnp.swapaxes(held, 0, 1)
+    for axis in axes:
+        parts = []
+        for k in range(RING):
+            part = lax.dynamic_index_in_dim(held, (place[axis] + k) % RING, 0, keepdims=False)
+            parts.append(part if k == 0 else to_pre(part, axis, k))
+        held = sum(parts[1:], parts[0])
+    return parts
 
 
 def sum_all(gram, core):
@@ -317,36 +416,59 @@
 
 def local(values, block_rows, block_cols, block_count, test_matrix):
     pre, suf = lax.axis_index("pre"), lax.axis_index("suf")
-    core, x, y = pre % 2, pre // 2 % RING, pre // (2 * RING)
+    core = pre % 2
+    place = {"y": pre // (2 * RING), "x": pre // 2 % RING}
     prefix_total = PB * BLK * lax.axis_size("pre")
     suffix_total = SB * BLK * lax.axis_size("suf")
     row_ids = ((block_rows[0] // RING - suf) % RING) * RING + block_rows[0] % RING
-    col_ids = ((block_cols[0] // RING - y) % RING) * RING + (block_cols[0] % RING - x) % RING
-    dense = dense_blocks(values[0], row_ids, col_ids, block_count)
-    panel, dense = gather_pre(test_matrix, core, dense)
-    share_rows = PB * BLK // RING
-
-    def prefix_sums(panel):
+    dense = dense_blocks(values[0], row_ids, block_cols[0], block_count)
+    prefix_share = PB * BLK // RING
+    suffix_share = test_matrix.shape[0]
+
+    def prefix_chunks(panel):
         chunks = [None] * RING
         for k in (2, 1, 3, 0):
             chunks[k] = jnp.dot(
-                dense[k * share_rows:(k + 1) * share_rows], panel,
+                dense[k * prefix_share:(k + 1) * prefix_share], panel,
                 preferred_element_type=jnp.float32,
             )
-        return sum_and_gram(scatter_suf(chunks))
-
-    sketch, gram = prefix_sums(panel)
-    first_rounded, _ = orthonormal(sketch, sum_all(gram, core), prefix_total, True)
-    suffix_partial = lax.dot_general(
-        dense, gather_suf(first_rounded), (((0,), (0,)), ((), ())),
-        preferred_element_type=jnp.float32,
-    )
-    suffix_raw, gram = sum_and_gram(scatter_pre(suffix_partial, core))
-    suffix_rounded, suffix_basis = orthonormal(
-        suffix_raw, sum_all(gram, core), suffix_total, True
-    )
-    refined, gram = prefix_sums(gather_pre(suffix_rounded, core))
-    prefix_basis = orthonormal(refined, sum_all(gram, core), prefix_total, False)
+        return chunks
+
+    def suffix_sums(panel):
+        partial_value = lax.dot_general(
+            dense, panel, (((0,), (0,)), ((), ())), preferred_element_type=jnp.float32
+        )
+        return scatter_cores(partial_value, core)
+
+    held, dense = tie(gather_chips(test_matrix), dense)
+    chunks = prefix_chunks(gather_cores(held, core))
+    left, right, gram = sum_and_gram(scatter_suf(chunks), [], prefix_share)
+    gram = sum_all(gram, core)
+
+    rounded, first, factor = orth_left(left, gram, prefix_total, True)
+    left = gather_suf(rounded)
+    rounded, _ = orth_right(right, gram, first, factor, prefix_total, True)
+    rounded, left = tie(rounded, left)
+    right = gather_suf(rounded)
+    left = suffix_sums(left)
+    right, left = tie(right, left)
+    left = scatter_chips(left, "yx", place)
+    right = scatter_chips(suffix_sums(right), "xy", place)
+    left, right, gram = sum_and_gram(left, right, suffix_share)
+    gram = sum_all(gram, core)
+
+    rounded, first, factor = orth_left(left, gram, suffix_total, True)
+    left = gather_chips(rounded)
+    rounded, suffix_basis = orth_right(right, gram, first, factor, suffix_total, True)
+    rounded, left = tie(rounded, left)
+    right = gather_chips(rounded)
+    left = scatter_suf(prefix_chunks(gather_cores(left, core)))
+    right, left[2] = tie(right, left[2])
+    right = scatter_suf(prefix_chunks(gather_cores(right, core)))
+    left, right, gram = sum_and_gram(left, right, prefix_share)
+    gram = sum_all(gram, core)
+    first, factor = orth_left(left, gram, prefix_total, False)
+    (prefix_basis,) = orth_right(right, gram, first, factor, prefix_total, False)
     return (prefix_basis, suffix_basis)
 
 

time: 449 us -> 415 us (0.924)
  waiting for transfers between devices: 179 us -> 130 us
  blocking collectives: 74.9 us -> 85.4 us
  Pallas kernels: 86.9 us -> 78.8 us
  starting transfers between devices: 71.1 us -> 77 us
  matrix products: 16.9 us -> 22.8 us
    ppermute x18 -> x24, waiting for transfers between devices: 121 us -> 91.6 us  [to_suf(): lax.ppermute(value, 'suf', [(s, (s + step) % RING) for s in range(RING)])]
    ppermute x33 -> x23, waiting for transfers between devices: 58.1 us -> 29.2 us  [to_pre(): return lax.ppermute(value, 'pre', along(axis, step))]
    ppermute x33 -> x23, starting transfers between devices: 49.4 us -> 35.2 us  [to_pre(): return lax.ppermute(value, 'pre', along(axis, step))]
    all_to_all x0 -> x2, starting transfers between devices: none -> 11.2 us  [swap_chips(): lax.all_to_all(value, 'pre', 0, 0, axis_index_groups=groups, tiled=True)]
    all_to_all x6 -> x7, blocking collectives: 74.9 us -> 85.4 us  [swap_chips(): lax.all_to_all(value, 'pre', 0, 0, axis_index_groups=groups, tiled=True)]
    all_to_all x0 -> x2, waiting for transfers between devices: none -> 9.39 us  [swap_chips(): lax.all_to_all(value, 'pre', 0, 0, axis_index_groups=groups, tiled=True)]
    ppermute x18 -> x24, starting transfers between devices: 21.7 us -> 30.7 us  [to_suf(): lax.ppermute(value, 'suf', [(s, (s + step) % RING) for s in range(RING)])]
    pallas_call x6 -> x9, Pallas kernels: 80.2 us -> 72.9 us  [the longest x3 38.2 us: orth_right(): pl.pallas_call(functools.partial(right_kernel, scale=1.0 / total_rows, ro...]
  transfers between devices with their start and end apart: 51 -> 49, of which waited for: 36 -> 31; matrix products, arithmetic and copies ran while one was open for 1% -> 2% of each run, Pallas kernels for 2% -> 8%
where the time goes in v3:
time: 415 us; the launch traced here: 407 us
  waiting for transfers between devices  130 us (31%)
  blocking collectives  85.4 us (21%)
  Pallas kernels  78.8 us (19%)
  starting transfers between devices  77 us (19%)
  matrix products  22.8 us (5%)
  local copies, waits for them, and re-layouts  6.23 us (2%)
  other arithmetic  4.58 us (1%)
    ppermute x24, waiting for transfers between devices, to_suf(): lax.ppermute(value, 'suf', [(s, (s + step) % RING) for s in range(RING)])  91.6 us
    all_to_all x7, blocking collectives, swap_chips(): lax.all_to_all(value, 'pre', 0, 0, axis_index_groups=groups, tiled=True)  85.4 us
    pallas_call x3, Pallas kernels, orth_right(): pl.pallas_call(functools.partial(right_kernel, scale=1.0 / total_rows, ro...  38.2 us
    ppermute x23, starting transfers between devices, to_pre(): return lax.ppermute(value, 'pre', along(axis, step))  35.2 us
    ppermute x24, starting transfers between devices, to_suf(): lax.ppermute(value, 'suf', [(s, (s + step) % RING) for s in range(RING)])  30.7 us
    pallas_call x3, Pallas kernels, orth_left(): pl.pallas_call(functools.partial(left_kernel, scale=1.0 / total_rows, rou...  30.6 us
    ppermute x23, waiting for transfers between devices, to_pre(): return lax.ppermute(value, 'pre', along(axis, step))  29.2 us
    dot_general x12, matrix products, prefix_chunks(): jnp.dot(dense[k * prefix_share:(k + 1) * prefix_share], panel, preferred_...  14 us
  transfers between devices with their start and end apart: 49, of which 31 were waited for; matrix products, arithmetic and copies ran while one was open for 2% of the time, Pallas kernels for 8%

profile of v3, /device:TPU:1, one launch (start us, length us, event | category | flops | bytes accessed | tf_op | source)
XLA Modules:
  0.0 407.4 jit_solution(3729153359919976762)
XLA Ops:
  2.6 7.6 %all-to-all-start = ((bf16[16,64,512]{2,1,0:T(8,128)(2,1)}), bf16[16,64,512]{2,1,0:T(8,128)(2,1)S(1)}, u32[]{:S(2)}, u32[]{:S(2)}) async-start(bf16[16,64,512]{2,1,0:T(8,128)(2,1)} %broadcast_in_dim.12), calls=%async_computation | async-start | bytes 2097152 | tf_op jit(solution)/shard_map/all_to_all | solution.py:353
  10.9 5.9 %dense_blocks.1 = bf16[2048,2048]{1,0:T(8,128)(2,1)} custom-call(s32[1]{0:T(128)S(6)} %copy.37.count_ref, s32[192]{0:T(256)S(1)} %fusion.31.rows_ref, s32[192]{0:T(256)S(1)} %bitcast.136, bf16[192,128,128]{2,1,0:T(8,128)(2,1)} %bitcast.145), custom_call_target="tpu_custom_call" | custom-call | tf_op jit(solution)/shard_map/dense_blocks/pallas_call | solution.py:46
  16.8 9.4 %all-to-all-done = bf16[16,64,512]{2,1,0:T(8,128)(2,1)S(1)} async-done(((bf16[16,64,512]{2,1,0:T(8,128)(2,1)}), bf16[16,64,512]{2,1,0:T(8,128)(2,1)S(1)}, u32[]{:S(2)}, u32[]{:S(2)}) %all-to-all-start) | async-done | bytes 1048608 | tf_op jit(solution)/shard_map/all_to_all | solution.py:353
  45.2 20.0 %collective-permute-done.1.refs_1_ = f32[512,512]{1,0:T(8,128)S(1)} collective-permute-done((f32[512,512]{1,0:T(8,128)S(1)}, f32[512,512]{1,0:T(8,128)S(1)}, u32[]{:S(2)}, u32[]{:S(2)}) %collective-permute-start.1) | collective-permute-done | bytes 1048608 | tf_op jit(solution)/shard_map/ppermute | solution.py:340
  65.2 23.3 %collective-permute-done.2.refs_2_ = f32[512,512]{1,0:T(8,128)S(1)} collective-permute-done((f32[512,512]{1,0:T(8,128)S(1)}, f32[512,512]{1,0:T(8,128)S(1)}, u32[]{:S(2)}, u32[]{:S(2)}) %collective-permute-start.2) | collective-permute-done | bytes 1048608 | tf_op jit(solution)/shard_map/ppermute | solution.py:340
  92.9 11.6 %all_to_all.69 = f32[16,40,128]{2,1,0:T(8,128)S(1)} all-to-all(f32[16,40,128]{2,1,0:T(8,128)S(1)} %bitcast.157), channel_id=1, replica_groups={{0,8,16,24,32,40,48,56,64,72,80,88,96,104,112,120},{4,12,20,28,36,44,52..., dimensions={0} | all-to-all | bytes 655360 | tf_op jit(solution)/shard_map/all_to_all | solution.py:353
  111.2 11.0 %all_to_all.70 = f32[16,40,128]{2,1,0:T(8,128)S(1)} all-to-all(f32[16,40,128]{2,1,0:T(8,128)S(1)} %broadcast_in_dim.13), channel_id=1, replica_groups={{0,8,16,24,32,40,48,56,64,72,80,88,96,104,112,120},{4,12,20,28,36,44,52..., dimensions={0} | all-to-all | bytes 655360 | tf_op jit(solution)/shard_map/all_to_all | solution.py:353
  127.8 10.4 %orth_left.3 = (bf16[512,256]{1,0:T(8,128)(2,1)S(1)}, f32[512,256]{1,0:T(8,128)S(1)}, f32[2,128,384]{2,1,0:T(8,128)S(1)}) custom-call(f32[1280,128]{1,0:T(8,128)S(1)} %pad_maximum_fusion.5.gram_ref, f32[512,256]{1,0:T(8,128)S(1)} %get-tuple-element.36.rows_ref), custom_call_target="tpu_custom_call" | custom-call | tf_op jit(solution)/shard_map/orth_left/pallas_call | solution.py:302
  141.2 13.1 %orth_right.3 = (bf16[512,256]{1,0:T(8,128)(2,1)S(1)}, f32[512,512]{1,0:T(8,128)}) custom-call(f32[1280,128]{1,0:T(8,128)S(1)} %pad_maximum_fusion.5.gram_ref, f32[512,256]{1,0:T(8,128)S(1)} %get-tuple-element.35.rows_ref, f32[512,256]{1,0:T(8,128)S(1)} %get-tuple-element.37.first_ref, f32[2,128,384]{2,1,0:T(8,128)S(1)} %get-tuple-element.38.factor_ref), custom_call_target="tpu_custom_call" | custom-call | tf_op jit(solution)/shard_map/orth_right/pallas_call | solution.py:316
  154.4 6.2 %fusion.33 = f32[2048,256]{1,0:T(8,128)S(1)} fusion(bf16[2048,2048]{1,0:T(8,128)(2,1)} %dense_blocks.1, bf16[2048,256]{1,0:T(8,128)(2,1)S(1)} %pad_maximum_fusion.1), kind=kOutput, calls=%fused_computation.92 | convolution fusion | flops 2147483648 | bytes 11534336 | tf_op jit(solution)/shard_map/dot_general | solution.py:438
  166.6 4.8 %collective-permute-done.14 = bf16[512,256]{1,0:T(8,128)(2,1)S(1)} collective-permute-done((bf16[512,256]{1,0:T(8,128)(2,1)S(1)}, bf16[512,256]{1,0:T(8,128)(2,1)S(1)}, u32[]{:S(2)}, u32[]{:S(2)}) %collective-permute-start.14) | collective-permute-done | bytes 262176 | tf_op jit(solution)/shard_map/ppermute | solution.py:340
  171.4 5.1 %collective-permute-done.13 = bf16[512,256]{1,0:T(8,128)(2,1)S(1)} collective-permute-done((bf16[512,256]{1,0:T(8,128)(2,1)S(1)}, bf16[512,256]{1,0:T(8,128)(2,1)S(1)}, u32[]{:S(2)}, u32[]{:S(2)}) %collective-permute-start.13) | collective-permute-done | bytes 262176 | tf_op jit(solution)/shard_map/ppermute | solution.py:340
  188.2 9.0 %collective-permute-done.16 = f32[4,64,256]{2,1,0:T(8,128)S(1)} collective-permute-done((f32[4,64,256]{2,1,0:T(8,128)S(1)}, f32[4,64,256]{2,1,0:T(8,128)S(1)}, u32[]{:S(2)}, u32[]{:S(2)}) %collective-permute-start.16) | collective-permute-done | bytes 262176 | tf_op jit(solution)/shard_map/ppermute | solution.py:344
  216.5 12.4 %all_to_all.71 = f32[16,40,128]{2,1,0:T(8,128)S(1)} all-to-all(f32[16,40,128]{2,1,0:T(8,128)S(1)} %bitcast.158), channel_id=1, replica_groups={{0,8,16,24,32,40,48,56,64,72,80,88,96,104,112,120},{4,12,20,28,36,44,52..., dimensions={0} | all-to-all | bytes 655360 | tf_op jit(solution)/shard_map/all_to_all | solution.py:353
  236.1 10.7 %all_to_all.72 = f32[16,40,128]{2,1,0:T(8,128)S(1)} all-to-all(f32[16,40,128]{2,1,0:T(8,128)S(1)} %broadcast_in_dim.14), channel_id=1, replica_groups={{0,8,16,24,32,40,48,56,64,72,80,88,96,104,112,120},{4,12,20,28,36,44,52..., dimensions={0} | all-to-all | bytes 655360 | tf_op jit(solution)/shard_map/all_to_all | solution.py:353
  252.8 9.8 %orth_left.4 = (bf16[64,256]{1,0:T(8,128)(2,1)S(1)}, f32[64,256]{1,0:T(8,128)S(1)}, f32[2,128,384]{2,1,0:T(8,128)S(1)}) custom-call(f32[1280,128]{1,0:T(8,128)S(1)} %pad_maximum_fusion.6.gram_ref, f32[64,256]{1,0:T(8,128)S(1)} %get-tuple-element.47.rows_ref), custom_call_target="tpu_custom_call" | custom-call | tf_op jit(solution)/shard_map/orth_left/pallas_call | solution.py:302
  267.0 12.0 %orth_right.4 = (bf16[64,256]{1,0:T(8,128)(2,1)S(1)}, f32[64,512]{1,0:T(8,128)}) custom-call(f32[1280,128]{1,0:T(8,128)S(1)} %pad_maximum_fusion.6.gram_ref, f32[64,256]{1,0:T(8,128)S(1)} %get-tuple-element.46.rows_ref, f32[64,256]{1,0:T(8,128)S(1)} %get-tuple-element.48.first_ref, f32[2,128,384]{2,1,0:T(8,128)S(1)} %get-tuple-element.49.factor_ref), custom_call_target="tpu_custom_call" | custom-call | tf_op jit(solution)/shard_map/orth_right/pallas_call | solution.py:316
  284.7 17.4 %all_to_all.73 = bf16[16,64,256]{2,1,0:T(8,128)(2,1)S(1)} all-to-all(bf16[16,64,256]{2,1,0:T(8,128)(2,1)S(1)} %broadcast_in_dim.16), channel_id=1, replica_groups={{0,8,16,24,32,40,48,56,64,72,80,88,96,104,112,120},{4,12,20,28,36,44,52..., dimensions={0} | all-to-all | bytes 1048576 | tf_op jit(solution)/shard_map/all_to_all | solution.py:353
  321.2 10.8 %collective-permute-done.37.refs_3_ = f32[512,256]{1,0:T(8,128)S(1)} collective-permute-done((f32[512,256]{1,0:T(8,128)S(1)}, f32[512,256]{1,0:T(8,128)S(1)}, u32[]{:S(2)}, u32[]{:S(2)}) %collective-permute-start.37) | collective-permute-done | bytes 524320 | tf_op jit(solution)/shard_map/ppermute | solution.py:340
  332.0 11.7 %collective-permute-done.39.refs_5_ = f32[512,256]{1,0:T(8,128)S(1)} collective-permute-done((f32[512,256]{1,0:T(8,128)S(1)}, f32[512,256]{1,0:T(8,128)S(1)}, u32[]{:S(2)}, u32[]{:S(2)}) %collective-permute-start.39) | collective-permute-done | bytes 524320 | tf_op jit(solution)/shard_map/ppermute | solution.py:340
  347.9 11.5 %all_to_all.74 = f32[16,40,128]{2,1,0:T(8,128)S(1)} all-to-all(f32[16,40,128]{2,1,0:T(8,128)S(1)} %bitcast.159), channel_id=1, replica_groups={{0,8,16,24,32,40,48,56,64,72,80,88,96,104,112,120},{4,12,20,28,36,44,52..., dimensions={0} | all-to-all | bytes 655360 | tf_op jit(solution)/shard_map/all_to_all | solution.py:353
  367.0 10.9 %all_to_all.75 = f32[16,40,128]{2,1,0:T(8,128)S(1)} all-to-all(f32[16,40,128]{2,1,0:T(8,128)S(1)} %broadcast_in_dim.17), channel_id=1, replica_groups={{0,8,16,24,32,40,48,56,64,72,80,88,96,104,112,120},{4,12,20,28,36,44,52..., dimensions={0} | all-to-all | bytes 655360 | tf_op jit(solution)/shard_map/all_to_all | solution.py:353
  383.5 10.4 %orth_left.5 = (f32[512,256]{1,0:T(8,128)S(1)}, f32[2,128,384]{2,1,0:T(8,128)S(1)}) custom-call(f32[1280,128]{1,0:T(8,128)S(1)} %pad_maximum_fusion.7.gram_ref, f32[512,256]{1,0:T(8,128)S(1)} %get-tuple-element.58.rows_ref), custom_call_target="tpu_custom_call" | custom-call | tf_op jit(solution)/shard_map/orth_left/pallas_call | solution.py:302
  393.9 13.1 %orth_right.5 = f32[512,512]{1,0:T(8,128)} custom-call(f32[1280,128]{1,0:T(8,128)S(1)} %pad_maximum_fusion.7.gram_ref, f32[512,256]{1,0:T(8,128)S(1)} %get-tuple-element.57.rows_ref, f32[512,256]{1,0:T(8,128)S(1)} %get-tuple-element.59.first_ref, f32[2,128,384]{2,1,0:T(8,128)S(1)} %get-tuple-element.60.factor_ref), custom_call_target="tpu_custom_call" | custom-call | tf_op jit(solution)/shard_map/orth_right/pallas_call | solution.py:316
  (165 shorter events, 137.2 us)
Async XLA Ops:
  2.6 23.6 %all-to-all-start = ((bf16[16,64,512]{2,1,0:T(8,128)(2,1)}), bf16[16,64,512]{2,1,0:T(8,128)(2,1)S(1)}, u32[]{:S(2)}, u32[]{:S(2)}) async-start(bf16[16,64,512]{2,1,0:T(8,128)(2,1)} %broadcast_in_dim.12), calls=%async_computation | async-start | bytes 2097152 | tf_op jit(solution)/shard_map/all_to_all | solution.py:353
  38.2 27.0 %collective-permute-start.1 = (f32[512,512]{1,0:T(8,128)S(1)}, f32[512,512]{1,0:T(8,128)S(1)}, u32[]{:S(2)}, u32[]{:S(2)}) collective-permute-start(f32[512,512]{1,0:T(8,128)S(1)} %fusion.16), channel_id=1, source_target_pairs={{0,1},{1,2},{2,3},{3,0},{4,5},{5,6},{6,7},{7,4},{8,9},{9,10},{10,1... | collective-permute-start | bytes 3145736 | tf_op jit(solution)/shard_map/ppermute | solution.py:340
  39.9 48.6 %collective-permute-start.2 = (f32[512,512]{1,0:T(8,128)S(1)}, f32[512,512]{1,0:T(8,128)S(1)}, u32[]{:S(2)}, u32[]{:S(2)}) collective-permute-start(f32[512,512]{1,0:T(8,128)S(1)} %fusion.10), channel_id=1, source_target_pairs={{0,2},{1,3},{2,0},{3,1},{4,6},{5,7},{6,4},{7,5},{8,10},{9,11},{10,... | collective-permute-start | bytes 3145736 | tf_op jit(solution)/shard_map/ppermute | solution.py:340
  43.2 45.4 %collective-permute-start.3 = (f32[512,512]{1,0:T(8,128)S(1)}, f32[512,512]{1,0:T(8,128)S(1)}, u32[]{:S(2)}, u32[]{:S(2)}) collective-permute-start(f32[512,512]{1,0:T(8,128)S(1)} %fusion.4), channel_id=1, source_target_pairs={{0,3},{1,0},{2,1},{3,2},{4,7},{5,4},{6,5},{7,6},{8,11},{9,8},{10,9... | collective-permute-start | bytes 3145736 | tf_op jit(solution)/shard_map/ppermute | solution.py:340
  138.2 16.1 %collective-permute-start.11 = (bf16[512,256]{1,0:T(8,128)(2,1)S(1)}, bf16[512,256]{1,0:T(8,128)(2,1)S(1)}, u32[]{:S(2)}, u32[]{:S(2)}) collective-permute-start(bf16[512,256]{1,0:T(8,128)(2,1)S(1)} %get-tuple-element.40), channel_id=1, source_target_pairs={{0,1},{1,2},{2,3},{3,0},{4,5},{5,6},{6,7},{7,4},{8,9},{9,10},{10,1... | collective-permute-start | bytes 786440 | tf_op jit(solution)/shard_map/ppermute | solution.py:340
  138.3 16.1 %collective-permute-start.10 = (bf16[512,256]{1,0:T(8,128)(2,1)S(1)}, bf16[512,256]{1,0:T(8,128)(2,1)S(1)}, u32[]{:S(2)}, u32[]{:S(2)}) collective-permute-start(bf16[512,256]{1,0:T(8,128)(2,1)S(1)} %get-tuple-element.40), channel_id=1, source_target_pairs={{0,2},{1,3},{2,0},{3,1},{4,6},{5,7},{6,4},{7,5},{8,10},{9,11},{10,... | collective-permute-start | bytes 786440 | tf_op jit(solution)/shard_map/ppermute | solution.py:340
  139.3 15.0 %collective-permute-start.9 = (bf16[512,256]{1,0:T(8,128)(2,1)S(1)}, bf16[512,256]{1,0:T(8,128)(2,1)S(1)}, u32[]{:S(2)}, u32[]{:S(2)}) collective-permute-start(bf16[512,256]{1,0:T(8,128)(2,1)S(1)} %get-tuple-element.40), channel_id=1, source_target_pairs={{0,3},{1,0},{2,1},{3,2},{4,7},{5,4},{6,5},{7,6},{8,11},{9,8},{10,9... | collective-permute-start | bytes 786440 | tf_op jit(solution)/shard_map/ppermute | solution.py:340
  160.7 16.4 %collective-permute-start.15 = (f32[16,64,256]{2,1,0:T(8,128)S(1)}, f32[16,64,256]{2,1,0:T(8,128)S(1)}, u32[]{:S(2)}, u32[]{:S(2)}) collective-permute-start(f32[16,64,256]{2,1,0:T(8,128)S(1)} %select_bitcast_fusion.1), channel_id=1, source_target_pairs={{0,4},{4,0},{8,12},{12,8},{16,20},{20,16},{24,28},{28,24},{32,36},... | collective-permute-start | bytes 3145736 | tf_op jit(solution)/shard_map/ppermute | solution.py:344
  162.0 9.4 %collective-permute-start.14 = (bf16[512,256]{1,0:T(8,128)(2,1)S(1)}, bf16[512,256]{1,0:T(8,128)(2,1)S(1)}, u32[]{:S(2)}, u32[]{:S(2)}) collective-permute-start(bf16[512,256]{1,0:T(8,128)(2,1)S(1)} %get-tuple-element.41), channel_id=1, source_target_pairs={{0,1},{1,2},{2,3},{3,0},{4,5},{5,6},{6,7},{7,4},{8,9},{9,10},{10,1... | collective-permute-start | bytes 786440 | tf_op jit(solution)/shard_map/ppermute | solution.py:340
  162.0 14.4 %collective-permute-start.13 = (bf16[512,256]{1,0:T(8,128)(2,1)S(1)}, bf16[512,256]{1,0:T(8,128)(2,1)S(1)}, u32[]{:S(2)}, u32[]{:S(2)}) collective-permute-start(bf16[512,256]{1,0:T(8,128)(2,1)S(1)} %get-tuple-element.41), channel_id=1, source_target_pairs={{0,2},{1,3},{2,0},{3,1},{4,6},{5,7},{6,4},{7,5},{8,10},{9,11},{10,... | collective-permute-start | bytes 786440 | tf_op jit(solution)/shard_map/ppermute | solution.py:340
  164.4 12.6 %collective-permute-start.12 = (bf16[512,256]{1,0:T(8,128)(2,1)S(1)}, bf16[512,256]{1,0:T(8,128)(2,1)S(1)}, u32[]{:S(2)}, u32[]{:S(2)}) collective-permute-start(bf16[512,256]{1,0:T(8,128)(2,1)S(1)} %get-tuple-element.41), channel_id=1, source_target_pairs={{0,3},{1,0},{2,1},{3,2},{4,7},{5,4},{6,5},{7,6},{8,11},{9,8},{10,9... | collective-permute-start | bytes 786440 | tf_op jit(solution)/shard_map/ppermute | solution.py:340
  182.4 14.8 %collective-permute-start.16 = (f32[4,64,256]{2,1,0:T(8,128)S(1)}, f32[4,64,256]{2,1,0:T(8,128)S(1)}, u32[]{:S(2)}, u32[]{:S(2)}) collective-permute-start(f32[4,64,256]{2,1,0:T(8,128)S(1)} %get-tuple-element.71), channel_id=1, source_target_pairs={{0,32},{4,36},{8,40},{12,44},{16,48},{20,52},{24,56},{28,60},{32,6... | collective-permute-start | bytes 786440 | tf_op jit(solution)/shard_map/ppermute | solution.py:344
  182.5 15.1 %collective-permute-start.18 = (f32[4,64,256]{2,1,0:T(8,128)S(1)}, f32[4,64,256]{2,1,0:T(8,128)S(1)}, u32[]{:S(2)}, u32[]{:S(2)}) collective-permute-start(f32[4,64,256]{2,1,0:T(8,128)S(1)} %get-tuple-element.72), channel_id=1, source_target_pairs={{0,96},{4,100},{8,104},{12,108},{16,112},{20,116},{24,120},{28,124... | collective-permute-start | bytes 786440 | tf_op jit(solution)/shard_map/ppermute | solution.py:344
  185.2 12.4 %collective-permute-start.17 = (f32[4,64,256]{2,1,0:T(8,128)S(1)}, f32[4,64,256]{2,1,0:T(8,128)S(1)}, u32[]{:S(2)}, u32[]{:S(2)}) collective-permute-start(f32[4,64,256]{2,1,0:T(8,128)S(1)} %get-tuple-element.73), channel_id=1, source_target_pairs={{0,64},{4,68},{8,72},{12,76},{16,80},{20,84},{24,88},{28,92},{32,9... | collective-permute-start | bytes 786440 | tf_op jit(solution)/shard_map/ppermute | solution.py:344
  186.7 14.2 %collective-permute-start.23 = (f32[4,64,256]{2,1,0:T(8,128)S(1)}, f32[4,64,256]{2,1,0:T(8,128)S(1)}, u32[]{:S(2)}, u32[]{:S(2)}) collective-permute-start(f32[4,64,256]{2,1,0:T(8,128)S(1)} %get-tuple-element.68), channel_id=1, source_target_pairs={{0,8},{4,12},{8,16},{12,20},{16,24},{20,28},{24,0},{28,4},{32,40},... | collective-permute-start | bytes 786440 | tf_op jit(solution)/shard_map/ppermute | solution.py:344
  187.0 13.9 %collective-permute-start.24 = (f32[4,64,256]{2,1,0:T(8,128)S(1)}, f32[4,64,256]{2,1,0:T(8,128)S(1)}, u32[]{:S(2)}, u32[]{:S(2)}) collective-permute-start(f32[4,64,256]{2,1,0:T(8,128)S(1)} %get-tuple-element.69), channel_id=1, source_target_pairs={{0,16},{4,20},{8,24},{12,28},{16,0},{20,4},{24,8},{28,12},{32,48},... | collective-permute-start | bytes 786440 | tf_op jit(solution)/shard_map/ppermute | solution.py:344
  263.4 15.6 %all-to-all-start.5 = ((bf16[16,64,256]{2,1,0:T(8,128)(2,1)}), bf16[16,64,256]{2,1,0:T(8,128)(2,1)S(1)}, u32[]{:S(2)}, u32[]{:S(2)}) async-start(bf16[16,64,256]{2,1,0:T(8,128)(2,1)} %broadcast_in_dim.15), calls=%async_computation.5 | async-start | bytes 1048576 | tf_op jit(solution)/shard_map/all_to_all | solution.py:353
  283.7 18.4 %collective-permute-start.36 = (f32[512,256]{1,0:T(8,128)S(1)}, f32[512,256]{1,0:T(8,128)S(1)}, u32[]{:S(2)}, u32[]{:S(2)}) collective-permute-start(f32[512,256]{1,0:T(8,128)S(1)} %fusion.8), channel_id=1, source_target_pairs={{0,2},{1,3},{2,0},{3,1},{4,6},{5,7},{6,4},{7,5},{8,10},{9,11},{10,... | collective-permute-start | bytes 1572872 | tf_op jit(solution)/shard_map/ppermute | solution.py:340
  302.1 8.1 %collective-permute-start.38 = (bf16[16,64,256]{2,1,0:T(8,128)(2,1)S(1)}, bf16[16,64,256]{2,1,0:T(8,128)(2,1)S(1)}, u32[]{:S(2)}, u32[]{:S(2)}) collective-permute-start(bf16[16,64,256]{2,1,0:T(8,128)(2,1)S(1)} %all_to_all.73), channel_id=1, source_target_pairs={{0,4},{4,0},{8,12},{12,8},{16,20},{20,16},{24,28},{28,24},{32,36},... | collective-permute-start | bytes 1572872 | tf_op jit(solution)/shard_map/ppermute | solution.py:344
  306.4 14.8 %collective-permute-start.35 = (f32[512,256]{1,0:T(8,128)S(1)}, f32[512,256]{1,0:T(8,128)S(1)}, u32[]{:S(2)}, u32[]{:S(2)}) collective-permute-start(f32[512,256]{1,0:T(8,128)S(1)} %fusion.14), channel_id=1, source_target_pairs={{0,1},{1,2},{2,3},{3,0},{4,5},{5,6},{6,7},{7,4},{8,9},{9,10},{10,1... | collective-permute-start | bytes 1572872 | tf_op jit(solution)/shard_map/ppermute | solution.py:340
  307.2 24.8 %collective-permute-start.37 = (f32[512,256]{1,0:T(8,128)S(1)}, f32[512,256]{1,0:T(8,128)S(1)}, u32[]{:S(2)}, u32[]{:S(2)}) collective-permute-start(f32[512,256]{1,0:T(8,128)S(1)} %fusion.2), channel_id=1, source_target_pairs={{0,3},{1,0},{2,1},{3,2},{4,7},{5,4},{6,5},{7,6},{8,11},{9,8},{10,9... | collective-permute-start | bytes 1572872 | tf_op jit(solution)/shard_map/ppermute | solution.py:340
  312.6 31.1 %collective-permute-start.39 = (f32[512,256]{1,0:T(8,128)S(1)}, f32[512,256]{1,0:T(8,128)S(1)}, u32[]{:S(2)}, u32[]{:S(2)}) collective-permute-start(f32[512,256]{1,0:T(8,128)S(1)} %fusion.12), channel_id=1, source_target_pairs={{0,1},{1,2},{2,3},{3,0},{4,5},{5,6},{6,7},{7,4},{8,9},{9,10},{10,1... | collective-permute-start | bytes 1572872 | tf_op jit(solution)/shard_map/ppermute | solution.py:340
  312.7 31.0 %collective-permute-start.40 = (f32[512,256]{1,0:T(8,128)S(1)}, f32[512,256]{1,0:T(8,128)S(1)}, u32[]{:S(2)}, u32[]{:S(2)}) collective-permute-start(f32[512,256]{1,0:T(8,128)S(1)} %fusion.6), channel_id=1, source_target_pairs={{0,2},{1,3},{2,0},{3,1},{4,6},{5,7},{6,4},{7,5},{8,10},{9,11},{10,... | collective-permute-start | bytes 1572872 | tf_op jit(solution)/shard_map/ppermute | solution.py:340
  313.9 30.0 %collective-permute-start.41 = (f32[512,256]{1,0:T(8,128)S(1)}, f32[512,256]{1,0:T(8,128)S(1)}, u32[]{:S(2)}, u32[]{:S(2)}) collective-permute-start(f32[512,256]{1,0:T(8,128)S(1)} %fusion), channel_id=1, source_target_pairs={{0,3},{1,0},{2,1},{3,2},{4,7},{5,4},{6,5},{7,6},{8,11},{9,8},{10,9... | collective-permute-start | bytes 1572872 | tf_op jit(solution)/shard_map/ppermute | solution.py:340
  (32 other events, 230.0 us)

commit v4 on v3

--- a/solution.py
+++ b/solution.py
@@ -12,6 +12,7 @@
 SB = 16
 TILE = 128
 SUB = 8
+STAGE = 8
 RING = 4
 VMEM_BYTES = 48 * 1024 * 1024
 
@@ -140,7 +141,8 @@
             panel_ref[here, t * TILE:(t + 1) * TILE] = v
             if t == 0:
                 turned = v.T
-        for g in range(b + 1, groups):
+        stage = (b // STAGE + 1) * STAGE
+        for g in range(b + 1, stage):
             there = slice(g * SUB, (g + 1) * SUB)
             if g == b + 1:
                 cols = []
@@ -156,6 +158,12 @@
                 for k in range(SUB):
                     v = v - cols[k] * r[k][t]
                 panel_ref[there, t * TILE:(t + 1) * TILE] = v
+        if b + 1 == stage and stage < groups:
+            done, low = slice((stage - STAGE) * SUB, stage * SUB), stage * SUB
+            panel_ref[low:, :] = panel_ref[low:, :] - lax.dot_general(
+                panel_ref[done, low:TILE], panel_ref[done, :], (((0,), (0,)), ((), ())),
+                precision=highest, preferred_element_type=jnp.float32,
+            )
 
 
 def factor_and_solve(work_ref, left_ref, panel_ref, spread_ref, store):

time: 415 us -> 409 us (0.986)
  Pallas kernels: 78.8 us -> 73.4 us
where the time goes in v4:
time: 409 us; the launch traced here: 401 us
  waiting for transfers between devices  130 us (32%)
  blocking collectives  84.4 us (21%)
  starting transfers between devices  77.5 us (19%)
  Pallas kernels  73.4 us (18%)
  matrix products  22.8 us (6%)
  local copies, waits for them, and re-layouts  6.23 us (2%)
  other arithmetic  4.58 us (1%)
    ppermute x24, waiting for transfers between devices, to_suf(): lax.ppermute(value, 'suf', [(s, (s + step) % RING) for s in range(RING)])  92.7 us
    all_to_all x7, blocking collectives, swap_chips(): lax.all_to_all(value, 'pre', 0, 0, axis_index_groups=groups, tiled=True)  84.4 us
    ppermute x23, starting transfers between devices, to_pre(): return lax.ppermute(value, 'pre', along(axis, step))  36.4 us
    pallas_call x3, Pallas kernels, orth_right(): pl.pallas_call(functools.partial(right_kernel, scale=1.0 / total_rows, ro...  34.8 us
    ppermute x24, starting transfers between devices, to_suf(): lax.ppermute(value, 'suf', [(s, (s + step) % RING) for s in range(RING)])  29.9 us
    ppermute x23, waiting for transfers between devices, to_pre(): return lax.ppermute(value, 'pre', along(axis, step))  29.2 us
    pallas_call x3, Pallas kernels, orth_left(): pl.pallas_call(functools.partial(left_kernel, scale=1.0 / total_rows, rou...  27.2 us
    dot_general x12, matrix products, prefix_chunks(): jnp.dot(dense[k * prefix_share:(k + 1) * prefix_share], panel, preferred_...  14 us
  transfers between devices with their start and end apart: 49, of which 31 were waited for; matrix products, arithmetic and copies ran while one was open for 2% of the time, Pallas kernels for 8%

profile of v4, /device:TPU:1, one launch (start us, length us, event | category | flops | bytes accessed | tf_op | source)
XLA Modules:
  0.0 401.0 jit_solution(12698500296934688441)
XLA Ops:
  2.6 7.6 %all-to-all-start = ((bf16[16,64,512]{2,1,0:T(8,128)(2,1)}), bf16[16,64,512]{2,1,0:T(8,128)(2,1)S(1)}, u32[]{:S(2)}, u32[]{:S(2)}) async-start(bf16[16,64,512]{2,1,0:T(8,128)(2,1)} %broadcast_in_dim.12), calls=%async_computation | async-start | bytes 2097152 | tf_op jit(solution)/shard_map/all_to_all | solution.py:361
  10.9 7.2 %dense_blocks.1 = bf16[2048,2048]{1,0:T(8,128)(2,1)} custom-call(s32[1]{0:T(128)S(6)} %copy.37.count_ref, s32[192]{0:T(256)S(1)} %fusion.31.rows_ref, s32[192]{0:T(256)S(1)} %bitcast.136, bf16[192,128,128]{2,1,0:T(8,128)(2,1)} %bitcast.145), custom_call_target="tpu_custom_call" | custom-call | tf_op jit(solution)/shard_map/dense_blocks/pallas_call | solution.py:47
  18.1 8.0 %all-to-all-done = bf16[16,64,512]{2,1,0:T(8,128)(2,1)S(1)} async-done(((bf16[16,64,512]{2,1,0:T(8,128)(2,1)}), bf16[16,64,512]{2,1,0:T(8,128)(2,1)S(1)}, u32[]{:S(2)}, u32[]{:S(2)}) %all-to-all-start) | async-done | bytes 1048608 | tf_op jit(solution)/shard_map/all_to_all | solution.py:361
  45.2 20.0 %collective-permute-done.1.refs_1_ = f32[512,512]{1,0:T(8,128)S(1)} collective-permute-done((f32[512,512]{1,0:T(8,128)S(1)}, f32[512,512]{1,0:T(8,128)S(1)}, u32[]{:S(2)}, u32[]{:S(2)}) %collective-permute-start.1) | collective-permute-done | bytes 1048608 | tf_op jit(solution)/shard_map/ppermute | solution.py:348
  65.2 23.3 %collective-permute-done.2.refs_2_ = f32[512,512]{1,0:T(8,128)S(1)} collective-permute-done((f32[512,512]{1,0:T(8,128)S(1)}, f32[512,512]{1,0:T(8,128)S(1)}, u32[]{:S(2)}, u32[]{:S(2)}) %collective-permute-start.2) | collective-permute-done | bytes 1048608 | tf_op jit(solution)/shard_map/ppermute | solution.py:348
  92.9 11.6 %all_to_all.69 = f32[16,40,128]{2,1,0:T(8,128)S(1)} all-to-all(f32[16,40,128]{2,1,0:T(8,128)S(1)} %bitcast.157), channel_id=1, replica_groups={{0,8,16,24,32,40,48,56,64,72,80,88,96,104,112,120},{4,12,20,28,36,44,52..., dimensions={0} | all-to-all | bytes 655360 | tf_op jit(solution)/shard_map/all_to_all | solution.py:361
  111.2 11.0 %all_to_all.70 = f32[16,40,128]{2,1,0:T(8,128)S(1)} all-to-all(f32[16,40,128]{2,1,0:T(8,128)S(1)} %broadcast_in_dim.13), channel_id=1, replica_groups={{0,8,16,24,32,40,48,56,64,72,80,88,96,104,112,120},{4,12,20,28,36,44,52..., dimensions={0} | all-to-all | bytes 655360 | tf_op jit(solution)/shard_map/all_to_all | solution.py:361
  127.8 9.2 %orth_left.3 = (bf16[512,256]{1,0:T(8,128)(2,1)S(1)}, f32[512,256]{1,0:T(8,128)S(1)}, f32[2,128,384]{2,1,0:T(8,128)S(1)}) custom-call(f32[1280,128]{1,0:T(8,128)S(1)} %pad_maximum_fusion.5.gram_ref, f32[512,256]{1,0:T(8,128)S(1)} %get-tuple-element.36.rows_ref), custom_call_target="tpu_custom_call" | custom-call | tf_op jit(solution)/shard_map/orth_left/pallas_call | solution.py:310
  140.0 11.9 %orth_right.3 = (bf16[512,256]{1,0:T(8,128)(2,1)S(1)}, f32[512,512]{1,0:T(8,128)}) custom-call(f32[1280,128]{1,0:T(8,128)S(1)} %pad_maximum_fusion.5.gram_ref, f32[512,256]{1,0:T(8,128)S(1)} %get-tuple-element.35.rows_ref, f32[512,256]{1,0:T(8,128)S(1)} %get-tuple-element.37.first_ref, f32[2,128,384]{2,1,0:T(8,128)S(1)} %get-tuple-element.38.factor_ref), custom_call_target="tpu_custom_call" | custom-call | tf_op jit(solution)/shard_map/orth_right/pallas_call | solution.py:324
  152.1 6.2 %fusion.33 = f32[2048,256]{1,0:T(8,128)S(1)} fusion(bf16[2048,2048]{1,0:T(8,128)(2,1)} %dense_blocks.1, bf16[2048,256]{1,0:T(8,128)(2,1)S(1)} %pad_maximum_fusion.1), kind=kOutput, calls=%fused_computation.92 | convolution fusion | flops 2147483648 | bytes 11534336 | tf_op jit(solution)/shard_map/dot_general | solution.py:446
  164.2 5.0 %collective-permute-done.14 = bf16[512,256]{1,0:T(8,128)(2,1)S(1)} collective-permute-done((bf16[512,256]{1,0:T(8,128)(2,1)S(1)}, bf16[512,256]{1,0:T(8,128)(2,1)S(1)}, u32[]{:S(2)}, u32[]{:S(2)}) %collective-permute-start.14) | collective-permute-done | bytes 262176 | tf_op jit(solution)/shard_map/ppermute | solution.py:348
  169.2 6.5 %collective-permute-done.13 = bf16[512,256]{1,0:T(8,128)(2,1)S(1)} collective-permute-done((bf16[512,256]{1,0:T(8,128)(2,1)S(1)}, bf16[512,256]{1,0:T(8,128)(2,1)S(1)}, u32[]{:S(2)}, u32[]{:S(2)}) %collective-permute-start.13) | collective-permute-done | bytes 262176 | tf_op jit(solution)/shard_map/ppermute | solution.py:348
  186.6 9.0 %collective-permute-done.16 = f32[4,64,256]{2,1,0:T(8,128)S(1)} collective-permute-done((f32[4,64,256]{2,1,0:T(8,128)S(1)}, f32[4,64,256]{2,1,0:T(8,128)S(1)}, u32[]{:S(2)}, u32[]{:S(2)}) %collective-permute-start.16) | collective-permute-done | bytes 262176 | tf_op jit(solution)/shard_map/ppermute | solution.py:352
  214.9 12.4 %all_to_all.71 = f32[16,40,128]{2,1,0:T(8,128)S(1)} all-to-all(f32[16,40,128]{2,1,0:T(8,128)S(1)} %bitcast.158), channel_id=1, replica_groups={{0,8,16,24,32,40,48,56,64,72,80,88,96,104,112,120},{4,12,20,28,36,44,52..., dimensions={0} | all-to-all | bytes 655360 | tf_op jit(solution)/shard_map/all_to_all | solution.py:361
  234.2 10.7 %all_to_all.72 = f32[16,40,128]{2,1,0:T(8,128)S(1)} all-to-all(f32[16,40,128]{2,1,0:T(8,128)S(1)} %broadcast_in_dim.14), channel_id=1, replica_groups={{0,8,16,24,32,40,48,56,64,72,80,88,96,104,112,120},{4,12,20,28,36,44,52..., dimensions={0} | all-to-all | bytes 655360 | tf_op jit(solution)/shard_map/all_to_all | solution.py:361
  250.8 8.8 %orth_left.4 = (bf16[64,256]{1,0:T(8,128)(2,1)S(1)}, f32[64,256]{1,0:T(8,128)S(1)}, f32[2,128,384]{2,1,0:T(8,128)S(1)}) custom-call(f32[1280,128]{1,0:T(8,128)S(1)} %pad_maximum_fusion.6.gram_ref, f32[64,256]{1,0:T(8,128)S(1)} %get-tuple-element.47.rows_ref), custom_call_target="tpu_custom_call" | custom-call | tf_op jit(solution)/shard_map/orth_left/pallas_call | solution.py:310
  264.0 11.0 %orth_right.4 = (bf16[64,256]{1,0:T(8,128)(2,1)S(1)}, f32[64,512]{1,0:T(8,128)}) custom-call(f32[1280,128]{1,0:T(8,128)S(1)} %pad_maximum_fusion.6.gram_ref, f32[64,256]{1,0:T(8,128)S(1)} %get-tuple-element.46.rows_ref, f32[64,256]{1,0:T(8,128)S(1)} %get-tuple-element.48.first_ref, f32[2,128,384]{2,1,0:T(8,128)S(1)} %get-tuple-element.49.factor_ref), custom_call_target="tpu_custom_call" | custom-call | tf_op jit(solution)/shard_map/orth_right/pallas_call | solution.py:324
  281.8 16.3 %all_to_all.73 = bf16[16,64,256]{2,1,0:T(8,128)(2,1)S(1)} all-to-all(bf16[16,64,256]{2,1,0:T(8,128)(2,1)S(1)} %broadcast_in_dim.16), channel_id=1, replica_groups={{0,8,16,24,32,40,48,56,64,72,80,88,96,104,112,120},{4,12,20,28,36,44,52..., dimensions={0} | all-to-all | bytes 1048576 | tf_op jit(solution)/shard_map/all_to_all | solution.py:361
  317.2 10.8 %collective-permute-done.37.refs_3_ = f32[512,256]{1,0:T(8,128)S(1)} collective-permute-done((f32[512,256]{1,0:T(8,128)S(1)}, f32[512,256]{1,0:T(8,128)S(1)}, u32[]{:S(2)}, u32[]{:S(2)}) %collective-permute-start.37) | collective-permute-done | bytes 524320 | tf_op jit(solution)/shard_map/ppermute | solution.py:348
  328.0 11.7 %collective-permute-done.39.refs_5_ = f32[512,256]{1,0:T(8,128)S(1)} collective-permute-done((f32[512,256]{1,0:T(8,128)S(1)}, f32[512,256]{1,0:T(8,128)S(1)}, u32[]{:S(2)}, u32[]{:S(2)}) %collective-permute-start.39) | collective-permute-done | bytes 524320 | tf_op jit(solution)/shard_map/ppermute | solution.py:348
  343.9 11.5 %all_to_all.74 = f32[16,40,128]{2,1,0:T(8,128)S(1)} all-to-all(f32[16,40,128]{2,1,0:T(8,128)S(1)} %bitcast.159), channel_id=1, replica_groups={{0,8,16,24,32,40,48,56,64,72,80,88,96,104,112,120},{4,12,20,28,36,44,52..., dimensions={0} | all-to-all | bytes 655360 | tf_op jit(solution)/shard_map/all_to_all | solution.py:361
  363.0 10.9 %all_to_all.75 = f32[16,40,128]{2,1,0:T(8,128)S(1)} all-to-all(f32[16,40,128]{2,1,0:T(8,128)S(1)} %broadcast_in_dim.17), channel_id=1, replica_groups={{0,8,16,24,32,40,48,56,64,72,80,88,96,104,112,120},{4,12,20,28,36,44,52..., dimensions={0} | all-to-all | bytes 655360 | tf_op jit(solution)/shard_map/all_to_all | solution.py:361
  379.5 9.2 %orth_left.5 = (f32[512,256]{1,0:T(8,128)S(1)}, f32[2,128,384]{2,1,0:T(8,128)S(1)}) custom-call(f32[1280,128]{1,0:T(8,128)S(1)} %pad_maximum_fusion.7.gram_ref, f32[512,256]{1,0:T(8,128)S(1)} %get-tuple-element.58.rows_ref), custom_call_target="tpu_custom_call" | custom-call | tf_op jit(solution)/shard_map/orth_left/pallas_call | solution.py:310
  388.7 11.9 %orth_right.5 = f32[512,512]{1,0:T(8,128)} custom-call(f32[1280,128]{1,0:T(8,128)S(1)} %pad_maximum_fusion.7.gram_ref, f32[512,256]{1,0:T(8,128)S(1)} %get-tuple-element.57.rows_ref, f32[512,256]{1,0:T(8,128)S(1)} %get-tuple-element.59.first_ref, f32[2,128,384]{2,1,0:T(8,128)S(1)} %get-tuple-element.60.factor_ref), custom_call_target="tpu_custom_call" | custom-call | tf_op jit(solution)/shard_map/orth_right/pallas_call | solution.py:324
  (165 shorter events, 137.1 us)
Async XLA Ops:
  2.6 23.6 %all-to-all-start = ((bf16[16,64,512]{2,1,0:T(8,128)(2,1)}), bf16[16,64,512]{2,1,0:T(8,128)(2,1)S(1)}, u32[]{:S(2)}, u32[]{:S(2)}) async-start(bf16[16,64,512]{2,1,0:T(8,128)(2,1)} %broadcast_in_dim.12), calls=%async_computation | async-start | bytes 2097152 | tf_op jit(solution)/shard_map/all_to_all | solution.py:361
  38.2 27.0 %collective-permute-start.1 = (f32[512,512]{1,0:T(8,128)S(1)}, f32[512,512]{1,0:T(8,128)S(1)}, u32[]{:S(2)}, u32[]{:S(2)}) collective-permute-start(f32[512,512]{1,0:T(8,128)S(1)} %fusion.16), channel_id=1, source_target_pairs={{0,1},{1,2},{2,3},{3,0},{4,5},{5,6},{6,7},{7,4},{8,9},{9,10},{10,1... | collective-permute-start | bytes 3145736 | tf_op jit(solution)/shard_map/ppermute | solution.py:348
  39.9 48.6 %collective-permute-start.2 = (f32[512,512]{1,0:T(8,128)S(1)}, f32[512,512]{1,0:T(8,128)S(1)}, u32[]{:S(2)}, u32[]{:S(2)}) collective-permute-start(f32[512,512]{1,0:T(8,128)S(1)} %fusion.10), channel_id=1, source_target_pairs={{0,2},{1,3},{2,0},{3,1},{4,6},{5,7},{6,4},{7,5},{8,10},{9,11},{10,... | collective-permute-start | bytes 3145736 | tf_op jit(solution)/shard_map/ppermute | solution.py:348
  43.2 45.4 %collective-permute-start.3 = (f32[512,512]{1,0:T(8,128)S(1)}, f32[512,512]{1,0:T(8,128)S(1)}, u32[]{:S(2)}, u32[]{:S(2)}) collective-permute-start(f32[512,512]{1,0:T(8,128)S(1)} %fusion.4), channel_id=1, source_target_pairs={{0,3},{1,0},{2,1},{3,2},{4,7},{5,4},{6,5},{7,6},{8,11},{9,8},{10,9... | collective-permute-start | bytes 3145736 | tf_op jit(solution)/shard_map/ppermute | solution.py:348
  137.0 15.0 %collective-permute-start.11 = (bf16[512,256]{1,0:T(8,128)(2,1)S(1)}, bf16[512,256]{1,0:T(8,128)(2,1)S(1)}, u32[]{:S(2)}, u32[]{:S(2)}) collective-permute-start(bf16[512,256]{1,0:T(8,128)(2,1)S(1)} %get-tuple-element.40), channel_id=1, source_target_pairs={{0,1},{1,2},{2,3},{3,0},{4,5},{5,6},{6,7},{7,4},{8,9},{9,10},{10,1... | collective-permute-start | bytes 786440 | tf_op jit(solution)/shard_map/ppermute | solution.py:348
  137.1 14.9 %collective-permute-start.10 = (bf16[512,256]{1,0:T(8,128)(2,1)S(1)}, bf16[512,256]{1,0:T(8,128)(2,1)S(1)}, u32[]{:S(2)}, u32[]{:S(2)}) collective-permute-start(bf16[512,256]{1,0:T(8,128)(2,1)S(1)} %get-tuple-element.40), channel_id=1, source_target_pairs={{0,2},{1,3},{2,0},{3,1},{4,6},{5,7},{6,4},{7,5},{8,10},{9,11},{10,... | collective-permute-start | bytes 786440 | tf_op jit(solution)/shard_map/ppermute | solution.py:348
  138.2 13.8 %collective-permute-start.9 = (bf16[512,256]{1,0:T(8,128)(2,1)S(1)}, bf16[512,256]{1,0:T(8,128)(2,1)S(1)}, u32[]{:S(2)}, u32[]{:S(2)}) collective-permute-start(bf16[512,256]{1,0:T(8,128)(2,1)S(1)} %get-tuple-element.40), channel_id=1, source_target_pairs={{0,3},{1,0},{2,1},{3,2},{4,7},{5,4},{6,5},{7,6},{8,11},{9,8},{10,9... | collective-permute-start | bytes 786440 | tf_op jit(solution)/shard_map/ppermute | solution.py:348
  158.4 17.4 %collective-permute-start.15 = (f32[16,64,256]{2,1,0:T(8,128)S(1)}, f32[16,64,256]{2,1,0:T(8,128)S(1)}, u32[]{:S(2)}, u32[]{:S(2)}) collective-permute-start(f32[16,64,256]{2,1,0:T(8,128)S(1)} %select_bitcast_fusion.1), channel_id=1, source_target_pairs={{0,4},{4,0},{8,12},{12,8},{16,20},{20,16},{24,28},{28,24},{32,36},... | collective-permute-start | bytes 3145736 | tf_op jit(solution)/shard_map/ppermute | solution.py:352
  160.1 9.1 %collective-permute-start.14 = (bf16[512,256]{1,0:T(8,128)(2,1)S(1)}, bf16[512,256]{1,0:T(8,128)(2,1)S(1)}, u32[]{:S(2)}, u32[]{:S(2)}) collective-permute-start(bf16[512,256]{1,0:T(8,128)(2,1)S(1)} %get-tuple-element.41), channel_id=1, source_target_pairs={{0,1},{1,2},{2,3},{3,0},{4,5},{5,6},{6,7},{7,4},{8,9},{9,10},{10,1... | collective-permute-start | bytes 786440 | tf_op jit(solution)/shard_map/ppermute | solution.py:348
  160.4 15.3 %collective-permute-start.13 = (bf16[512,256]{1,0:T(8,128)(2,1)S(1)}, bf16[512,256]{1,0:T(8,128)(2,1)S(1)}, u32[]{:S(2)}, u32[]{:S(2)}) collective-permute-start(bf16[512,256]{1,0:T(8,128)(2,1)S(1)} %get-tuple-element.41), channel_id=1, source_target_pairs={{0,2},{1,3},{2,0},{3,1},{4,6},{5,7},{6,4},{7,5},{8,10},{9,11},{10,... | collective-permute-start | bytes 786440 | tf_op jit(solution)/shard_map/ppermute | solution.py:348
  163.7 12.0 %collective-permute-start.12 = (bf16[512,256]{1,0:T(8,128)(2,1)S(1)}, bf16[512,256]{1,0:T(8,128)(2,1)S(1)}, u32[]{:S(2)}, u32[]{:S(2)}) collective-permute-start(bf16[512,256]{1,0:T(8,128)(2,1)S(1)} %get-tuple-element.41), channel_id=1, source_target_pairs={{0,3},{1,0},{2,1},{3,2},{4,7},{5,4},{6,5},{7,6},{8,11},{9,8},{10,9... | collective-permute-start | bytes 786440 | tf_op jit(solution)/shard_map/ppermute | solution.py:348
  180.8 14.8 %collective-permute-start.16 = (f32[4,64,256]{2,1,0:T(8,128)S(1)}, f32[4,64,256]{2,1,0:T(8,128)S(1)}, u32[]{:S(2)}, u32[]{:S(2)}) collective-permute-start(f32[4,64,256]{2,1,0:T(8,128)S(1)} %get-tuple-element.71), channel_id=1, source_target_pairs={{0,32},{4,36},{8,40},{12,44},{16,48},{20,52},{24,56},{28,60},{32,6... | collective-permute-start | bytes 786440 | tf_op jit(solution)/shard_map/ppermute | solution.py:352
  180.8 15.1 %collective-permute-start.18 = (f32[4,64,256]{2,1,0:T(8,128)S(1)}, f32[4,64,256]{2,1,0:T(8,128)S(1)}, u32[]{:S(2)}, u32[]{:S(2)}) collective-permute-start(f32[4,64,256]{2,1,0:T(8,128)S(1)} %get-tuple-element.72), channel_id=1, source_target_pairs={{0,96},{4,100},{8,104},{12,108},{16,112},{20,116},{24,120},{28,124... | collective-permute-start | bytes 786440 | tf_op jit(solution)/shard_map/ppermute | solution.py:352
  183.5 12.4 %collective-permute-start.17 = (f32[4,64,256]{2,1,0:T(8,128)S(1)}, f32[4,64,256]{2,1,0:T(8,128)S(1)}, u32[]{:S(2)}, u32[]{:S(2)}) collective-permute-start(f32[4,64,256]{2,1,0:T(8,128)S(1)} %get-tuple-element.73), channel_id=1, source_target_pairs={{0,64},{4,68},{8,72},{12,76},{16,80},{20,84},{24,88},{28,92},{32,9... | collective-permute-start | bytes 786440 | tf_op jit(solution)/shard_map/ppermute | solution.py:352
  185.0 14.2 %collective-permute-start.23 = (f32[4,64,256]{2,1,0:T(8,128)S(1)}, f32[4,64,256]{2,1,0:T(8,128)S(1)}, u32[]{:S(2)}, u32[]{:S(2)}) collective-permute-start(f32[4,64,256]{2,1,0:T(8,128)S(1)} %get-tuple-element.68), channel_id=1, source_target_pairs={{0,8},{4,12},{8,16},{12,20},{16,24},{20,28},{24,0},{28,4},{32,40},... | collective-permute-start | bytes 786440 | tf_op jit(solution)/shard_map/ppermute | solution.py:352
  185.4 13.8 %collective-permute-start.24 = (f32[4,64,256]{2,1,0:T(8,128)S(1)}, f32[4,64,256]{2,1,0:T(8,128)S(1)}, u32[]{:S(2)}, u32[]{:S(2)}) collective-permute-start(f32[4,64,256]{2,1,0:T(8,128)S(1)} %get-tuple-element.69), channel_id=1, source_target_pairs={{0,16},{4,20},{8,24},{12,28},{16,0},{20,4},{24,8},{28,12},{32,48},... | collective-permute-start | bytes 786440 | tf_op jit(solution)/shard_map/ppermute | solution.py:352
  260.4 14.5 %all-to-all-start.5 = ((bf16[16,64,256]{2,1,0:T(8,128)(2,1)}), bf16[16,64,256]{2,1,0:T(8,128)(2,1)S(1)}, u32[]{:S(2)}, u32[]{:S(2)}) async-start(bf16[16,64,256]{2,1,0:T(8,128)(2,1)} %broadcast_in_dim.15), calls=%async_computation.5 | async-start | bytes 1048576 | tf_op jit(solution)/shard_map/all_to_all | solution.py:361
  280.7 17.4 %collective-permute-start.36 = (f32[512,256]{1,0:T(8,128)S(1)}, f32[512,256]{1,0:T(8,128)S(1)}, u32[]{:S(2)}, u32[]{:S(2)}) collective-permute-start(f32[512,256]{1,0:T(8,128)S(1)} %fusion.8), channel_id=1, source_target_pairs={{0,2},{1,3},{2,0},{3,1},{4,6},{5,7},{6,4},{7,5},{8,10},{9,11},{10,... | collective-permute-start | bytes 1572872 | tf_op jit(solution)/shard_map/ppermute | solution.py:348
  298.1 8.1 %collective-permute-start.38 = (bf16[16,64,256]{2,1,0:T(8,128)(2,1)S(1)}, bf16[16,64,256]{2,1,0:T(8,128)(2,1)S(1)}, u32[]{:S(2)}, u32[]{:S(2)}) collective-permute-start(bf16[16,64,256]{2,1,0:T(8,128)(2,1)S(1)} %all_to_all.73), channel_id=1, source_target_pairs={{0,4},{4,0},{8,12},{12,8},{16,20},{20,16},{24,28},{28,24},{32,36},... | collective-permute-start | bytes 1572872 | tf_op jit(solution)/shard_map/ppermute | solution.py:352
  302.4 14.8 %collective-permute-start.35 = (f32[512,256]{1,0:T(8,128)S(1)}, f32[512,256]{1,0:T(8,128)S(1)}, u32[]{:S(2)}, u32[]{:S(2)}) collective-permute-start(f32[512,256]{1,0:T(8,128)S(1)} %fusion.14), channel_id=1, source_target_pairs={{0,1},{1,2},{2,3},{3,0},{4,5},{5,6},{6,7},{7,4},{8,9},{9,10},{10,1... | collective-permute-start | bytes 1572872 | tf_op jit(solution)/shard_map/ppermute | solution.py:348
  303.2 24.8 %collective-permute-start.37 = (f32[512,256]{1,0:T(8,128)S(1)}, f32[512,256]{1,0:T(8,128)S(1)}, u32[]{:S(2)}, u32[]{:S(2)}) collective-permute-start(f32[512,256]{1,0:T(8,128)S(1)} %fusion.2), channel_id=1, source_target_pairs={{0,3},{1,0},{2,1},{3,2},{4,7},{5,4},{6,5},{7,6},{8,11},{9,8},{10,9... | collective-permute-start | bytes 1572872 | tf_op jit(solution)/shard_map/ppermute | solution.py:348
  308.6 31.1 %collective-permute-start.39 = (f32[512,256]{1,0:T(8,128)S(1)}, f32[512,256]{1,0:T(8,128)S(1)}, u32[]{:S(2)}, u32[]{:S(2)}) collective-permute-start(f32[512,256]{1,0:T(8,128)S(1)} %fusion.12), channel_id=1, source_target_pairs={{0,1},{1,2},{2,3},{3,0},{4,5},{5,6},{6,7},{7,4},{8,9},{9,10},{10,1... | collective-permute-start | bytes 1572872 | tf_op jit(solution)/shard_map/ppermute | solution.py:348
  308.7 31.0 %collective-permute-start.40 = (f32[512,256]{1,0:T(8,128)S(1)}, f32[512,256]{1,0:T(8,128)S(1)}, u32[]{:S(2)}, u32[]{:S(2)}) collective-permute-start(f32[512,256]{1,0:T(8,128)S(1)} %fusion.6), channel_id=1, source_target_pairs={{0,2},{1,3},{2,0},{3,1},{4,6},{5,7},{6,4},{7,5},{8,10},{9,11},{10,... | collective-permute-start | bytes 1572872 | tf_op jit(solution)/shard_map/ppermute | solution.py:348
  309.9 29.9 %collective-permute-start.41 = (f32[512,256]{1,0:T(8,128)S(1)}, f32[512,256]{1,0:T(8,128)S(1)}, u32[]{:S(2)}, u32[]{:S(2)}) collective-permute-start(f32[512,256]{1,0:T(8,128)S(1)} %fusion), channel_id=1, source_target_pairs={{0,3},{1,0},{2,1},{3,2},{4,7},{5,4},{6,5},{7,6},{8,11},{9,8},{10,9... | collective-permute-start | bytes 1572872 | tf_op jit(solution)/shard_map/ppermute | solution.py:348
  (32 other events, 230.4 us)

commit v5 on v4

--- a/solution.py
+++ b/solution.py
@@ -14,7 +14,7 @@
 SUB = 8
 STAGE = 8
 RING = 4
-VMEM_BYTES = 48 * 1024 * 1024
+VMEM_BYTES = 20 * 1024 * 1024
 
 highest = lax.Precision.HIGHEST
 
@@ -448,8 +448,7 @@
         )
         return scatter_cores(partial_value, core)
 
-    held, dense = tie(gather_chips(test_matrix), dense)
-    chunks = prefix_chunks(gather_cores(held, core))
+    chunks = prefix_chunks(gather_cores(gather_chips(test_matrix), core))
     left, right, gram = sum_and_gram(scatter_suf(chunks), [], prefix_share)
     gram = sum_all(gram, core)
 

time: 409 us -> 406 us (level)
  blocking collectives: 84.4 us -> 108 us
  waiting for transfers between devices: 130 us -> 119 us
  starting transfers between devices: 77.5 us -> 71.2 us
  Pallas kernels: 73.4 us -> 69.1 us
    all_to_all x7 -> x8, blocking collectives: 84.4 us -> 108 us  [swap_chips(): lax.all_to_all(value, 'pre', 0, 0, axis_index_groups=groups, tiled=True)]
    all_to_all x2 -> x1, waiting for transfers between devices: 8.05 us -> 0.01 us  [swap_chips(): lax.all_to_all(value, 'pre', 0, 0, axis_index_groups=groups, tiled=True)]
    all_to_all x2 -> x1, starting transfers between devices: 11.2 us -> 3.57 us  [swap_chips(): lax.all_to_all(value, 'pre', 0, 0, axis_index_groups=groups, tiled=True)]
    pallas_call x1, Pallas kernels: 7.24 us -> 3.02 us  [dense_blocks(): pl.pallas_call(dense_kernel, out_shape=jax.ShapeDtypeStruct((PB * BLK, SB...]
  transfers between devices with their start and end apart: 49 -> 48, of which waited for: 31 -> 28; matrix products, arithmetic and copies ran while one was open for 2% -> 2% of each run, Pallas kernels for 8% -> 7%
where the time goes in v5:
time: 406 us; the launch traced here: 398 us
  waiting for transfers between devices  119 us (29%)
  blocking collectives  108 us (27%)
  starting transfers between devices  71.2 us (18%)
  Pallas kernels  69.1 us (17%)
  matrix products  19 us (5%)
  local copies, waits for them, and re-layouts  4.95 us (1%)
  other arithmetic  4.54 us (1%)
    all_to_all x8, blocking collectives, swap_chips(): lax.all_to_all(value, 'pre', 0, 0, axis_index_groups=groups, tiled=True)  108 us
    ppermute x24, waiting for transfers between devices, to_suf(): lax.ppermute(value, 'suf', [(s, (s + step) % RING) for s in range(RING)])  91.7 us
    ppermute x23, starting transfers between devices, to_pre(): return lax.ppermute(value, 'pre', along(axis, step))  34.9 us
    pallas_call x3, Pallas kernels, orth_right(): pl.pallas_call(functools.partial(right_kernel, scale=1.0 / total_rows, ro...  34.8 us
    ppermute x24, starting transfers between devices, to_suf(): lax.ppermute(value, 'suf', [(s, (s + step) % RING) for s in range(RING)])  32.6 us
    pallas_call x3, Pallas kernels, orth_left(): pl.pallas_call(functools.partial(left_kernel, scale=1.0 / total_rows, rou...  27.2 us
    ppermute x23, waiting for transfers between devices, to_pre(): return lax.ppermute(value, 'pre', along(axis, step))  26.9 us
    dot_general x12, matrix products, prefix_chunks(): jnp.dot(dense[k * prefix_share:(k + 1) * prefix_share], panel, preferred_...  14 us
  transfers between devices with their start and end apart: 48, of which 28 were waited for; matrix products, arithmetic and copies ran while one was open for 2% of the time, Pallas kernels for 7%

profile of v5, /device:TPU:1, one launch (start us, length us, event | category | flops | bytes accessed | tf_op | source)
XLA Modules:
  0.0 398.1 jit_solution(5856660919028277678)
XLA Ops:
  1.6 23.5 %all_to_all.69 = bf16[16,64,512]{2,1,0:T(8,128)(2,1)S(1)} all-to-all(bf16[16,64,512]{2,1,0:T(8,128)(2,1)S(1)} %broadcast_in_dim.12), channel_id=1, replica_groups={{0,8,16,24,32,40,48,56,64,72,80,88,96,104,112,120},{4,12,20,28,36,44,52..., dimensions={0} | all-to-all | bytes 2097152 | tf_op jit(solution)/shard_map/all_to_all | solution.py:361
  46.3 19.6 %collective-permute-done.1.refs_1_ = f32[512,512]{1,0:T(8,128)S(1)} collective-permute-done((f32[512,512]{1,0:T(8,128)S(1)}, f32[512,512]{1,0:T(8,128)S(1)}, u32[]{:S(2)}, u32[]{:S(2)}) %collective-permute-start.1) | collective-permute-done | bytes 1048608 | tf_op jit(solution)/shard_map/ppermute | solution.py:348
  65.9 23.5 %collective-permute-done.2.refs_2_ = f32[512,512]{1,0:T(8,128)S(1)} collective-permute-done((f32[512,512]{1,0:T(8,128)S(1)}, f32[512,512]{1,0:T(8,128)S(1)}, u32[]{:S(2)}, u32[]{:S(2)}) %collective-permute-start.2) | collective-permute-done | bytes 1048608 | tf_op jit(solution)/shard_map/ppermute | solution.py:348
  92.9 11.9 %all_to_all.70 = f32[16,40,128]{2,1,0:T(8,128)S(1)} all-to-all(f32[16,40,128]{2,1,0:T(8,128)S(1)} %bitcast.155), channel_id=1, replica_groups={{0,8,16,24,32,40,48,56,64,72,80,88,96,104,112,120},{4,12,20,28,36,44,52..., dimensions={0} | all-to-all | bytes 655360 | tf_op jit(solution)/shard_map/all_to_all | solution.py:361
  112.1 11.2 %all_to_all.71 = f32[16,40,128]{2,1,0:T(8,128)S(1)} all-to-all(f32[16,40,128]{2,1,0:T(8,128)S(1)} %broadcast_in_dim.13), channel_id=1, replica_groups={{0,8,16,24,32,40,48,56,64,72,80,88,96,104,112,120},{4,12,20,28,36,44,52..., dimensions={0} | all-to-all | bytes 655360 | tf_op jit(solution)/shard_map/all_to_all | solution.py:361
  128.7 9.2 %orth_left.3 = (bf16[512,256]{1,0:T(8,128)(2,1)S(1)}, f32[512,256]{1,0:T(8,128)S(1)}, f32[2,128,384]{2,1,0:T(8,128)S(1)}) custom-call(f32[1280,128]{1,0:T(8,128)S(1)} %pad_maximum_fusion.5.gram_ref, f32[512,256]{1,0:T(8,128)S(1)} %get-tuple-element.32.rows_ref), custom_call_target="tpu_custom_call" | custom-call | tf_op jit(solution)/shard_map/orth_left/pallas_call | solution.py:310
  141.1 11.9 %orth_right.3 = (bf16[512,256]{1,0:T(8,128)(2,1)S(1)}, f32[512,512]{1,0:T(8,128)}) custom-call(f32[1280,128]{1,0:T(8,128)S(1)} %pad_maximum_fusion.5.gram_ref, f32[512,256]{1,0:T(8,128)S(1)} %get-tuple-element.31.rows_ref, f32[512,256]{1,0:T(8,128)S(1)} %get-tuple-element.33.first_ref, f32[2,128,384]{2,1,0:T(8,128)S(1)} %get-tuple-element.34.factor_ref), custom_call_target="tpu_custom_call" | custom-call | tf_op jit(solution)/shard_map/orth_right/pallas_call | solution.py:324
  161.5 5.0 %collective-permute-done.14 = bf16[512,256]{1,0:T(8,128)(2,1)S(1)} collective-permute-done((bf16[512,256]{1,0:T(8,128)(2,1)S(1)}, bf16[512,256]{1,0:T(8,128)(2,1)S(1)}, u32[]{:S(2)}, u32[]{:S(2)}) %collective-permute-start.14) | collective-permute-done | bytes 262176 | tf_op jit(solution)/shard_map/ppermute | solution.py:348
  166.6 6.4 %collective-permute-done.13 = bf16[512,256]{1,0:T(8,128)(2,1)S(1)} collective-permute-done((bf16[512,256]{1,0:T(8,128)(2,1)S(1)}, bf16[512,256]{1,0:T(8,128)(2,1)S(1)}, u32[]{:S(2)}, u32[]{:S(2)}) %collective-permute-start.13) | collective-permute-done | bytes 262176 | tf_op jit(solution)/shard_map/ppermute | solution.py:348
  183.6 9.0 %collective-permute-done.16 = f32[4,64,256]{2,1,0:T(8,128)S(1)} collective-permute-done((f32[4,64,256]{2,1,0:T(8,128)S(1)}, f32[4,64,256]{2,1,0:T(8,128)S(1)}, u32[]{:S(2)}, u32[]{:S(2)}) %collective-permute-start.16) | collective-permute-done | bytes 262176 | tf_op jit(solution)/shard_map/ppermute | solution.py:352
  206.2 4.4 %collective-permute-start.29 = (f32[640,128]{1,0:T(8,128)S(1)}, f32[640,128]{1,0:T(8,128)S(1)}, u32[]{:S(2)}, u32[]{:S(2)}) collective-permute-start(f32[640,128]{1,0:T(8,128)S(1)} %slice_select_fusion.1), channel_id=1, source_target_pairs={{0,4},{4,0},{8,12},{12,8},{16,20},{20,16},{24,28},{28,24},{32,36},... | collective-permute-start | bytes 983048 | tf_op jit(solution)/shard_map/ppermute | solution.py:352
  211.9 12.4 %all_to_all.72 = f32[16,40,128]{2,1,0:T(8,128)S(1)} all-to-all(f32[16,40,128]{2,1,0:T(8,128)S(1)} %bitcast.156), channel_id=1, replica_groups={{0,8,16,24,32,40,48,56,64,72,80,88,96,104,112,120},{4,12,20,28,36,44,52..., dimensions={0} | all-to-all | bytes 655360 | tf_op jit(solution)/shard_map/all_to_all | solution.py:361
  231.2 10.7 %all_to_all.73 = f32[16,40,128]{2,1,0:T(8,128)S(1)} all-to-all(f32[16,40,128]{2,1,0:T(8,128)S(1)} %broadcast_in_dim.14), channel_id=1, replica_groups={{0,8,16,24,32,40,48,56,64,72,80,88,96,104,112,120},{4,12,20,28,36,44,52..., dimensions={0} | all-to-all | bytes 655360 | tf_op jit(solution)/shard_map/all_to_all | solution.py:361
  241.9 4.6 %collective-permute-start.33 = (f32[640,128]{1,0:T(8,128)S(1)}, f32[640,128]{1,0:T(8,128)S(1)}, u32[]{:S(2)}, u32[]{:S(2)}) collective-permute-start(f32[640,128]{1,0:T(8,128)S(1)} %bitcast.154), channel_id=1, source_target_pairs={{0,4},{4,0},{8,12},{12,8},{16,20},{20,16},{24,28},{28,24},{32,36},... | collective-permute-start | bytes 983048 | tf_op jit(solution)/shard_map/ppermute | solution.py:352
  247.9 8.8 %orth_left.4 = (bf16[64,256]{1,0:T(8,128)(2,1)S(1)}, f32[64,256]{1,0:T(8,128)S(1)}, f32[2,128,384]{2,1,0:T(8,128)S(1)}) custom-call(f32[1280,128]{1,0:T(8,128)S(1)} %pad_maximum_fusion.6.gram_ref, f32[64,256]{1,0:T(8,128)S(1)} %get-tuple-element.43.rows_ref), custom_call_target="tpu_custom_call" | custom-call | tf_op jit(solution)/shard_map/orth_left/pallas_call | solution.py:310
  261.1 11.0 %orth_right.4 = (bf16[64,256]{1,0:T(8,128)(2,1)S(1)}, f32[64,512]{1,0:T(8,128)}) custom-call(f32[1280,128]{1,0:T(8,128)S(1)} %pad_maximum_fusion.6.gram_ref, f32[64,256]{1,0:T(8,128)S(1)} %get-tuple-element.42.rows_ref, f32[64,256]{1,0:T(8,128)S(1)} %get-tuple-element.44.first_ref, f32[2,128,384]{2,1,0:T(8,128)S(1)} %get-tuple-element.45.factor_ref), custom_call_target="tpu_custom_call" | custom-call | tf_op jit(solution)/shard_map/orth_right/pallas_call | solution.py:324
  278.8 16.3 %all_to_all.74 = bf16[16,64,256]{2,1,0:T(8,128)(2,1)S(1)} all-to-all(bf16[16,64,256]{2,1,0:T(8,128)(2,1)S(1)} %broadcast_in_dim.16), channel_id=1, replica_groups={{0,8,16,24,32,40,48,56,64,72,80,88,96,104,112,120},{4,12,20,28,36,44,52..., dimensions={0} | all-to-all | bytes 1048576 | tf_op jit(solution)/shard_map/all_to_all | solution.py:361
  310.0 4.3 %collective-permute-done.35.refs_1_ = f32[512,256]{1,0:T(8,128)S(1)} collective-permute-done((f32[512,256]{1,0:T(8,128)S(1)}, f32[512,256]{1,0:T(8,128)S(1)}, u32[]{:S(2)}, u32[]{:S(2)}) %collective-permute-start.35) | collective-permute-done | bytes 524320 | tf_op jit(solution)/shard_map/ppermute | solution.py:348
  314.3 10.9 %collective-permute-done.37.refs_3_ = f32[512,256]{1,0:T(8,128)S(1)} collective-permute-done((f32[512,256]{1,0:T(8,128)S(1)}, f32[512,256]{1,0:T(8,128)S(1)}, u32[]{:S(2)}, u32[]{:S(2)}) %collective-permute-start.37) | collective-permute-done | bytes 524320 | tf_op jit(solution)/shard_map/ppermute | solution.py:348
  325.1 11.6 %collective-permute-done.39.refs_5_ = f32[512,256]{1,0:T(8,128)S(1)} collective-permute-done((f32[512,256]{1,0:T(8,128)S(1)}, f32[512,256]{1,0:T(8,128)S(1)}, u32[]{:S(2)}, u32[]{:S(2)}) %collective-permute-start.39) | collective-permute-done | bytes 524320 | tf_op jit(solution)/shard_map/ppermute | solution.py:348
  340.9 11.5 %all_to_all.75 = f32[16,40,128]{2,1,0:T(8,128)S(1)} all-to-all(f32[16,40,128]{2,1,0:T(8,128)S(1)} %bitcast.157), channel_id=1, replica_groups={{0,8,16,24,32,40,48,56,64,72,80,88,96,104,112,120},{4,12,20,28,36,44,52..., dimensions={0} | all-to-all | bytes 655360 | tf_op jit(solution)/shard_map/all_to_all | solution.py:361
  360.1 10.9 %all_to_all.76 = f32[16,40,128]{2,1,0:T(8,128)S(1)} all-to-all(f32[16,40,128]{2,1,0:T(8,128)S(1)} %broadcast_in_dim.17), channel_id=1, replica_groups={{0,8,16,24,32,40,48,56,64,72,80,88,96,104,112,120},{4,12,20,28,36,44,52..., dimensions={0} | all-to-all | bytes 655360 | tf_op jit(solution)/shard_map/all_to_all | solution.py:361
  376.6 9.2 %orth_left.5 = (f32[512,256]{1,0:T(8,128)S(1)}, f32[2,128,384]{2,1,0:T(8,128)S(1)}) custom-call(f32[1280,128]{1,0:T(8,128)S(1)} %pad_maximum_fusion.7.gram_ref, f32[512,256]{1,0:T(8,128)S(1)} %get-tuple-element.54.rows_ref), custom_call_target="tpu_custom_call" | custom-call | tf_op jit(solution)/shard_map/orth_left/pallas_call | solution.py:310
  385.8 11.9 %orth_right.5 = f32[512,512]{1,0:T(8,128)} custom-call(f32[1280,128]{1,0:T(8,128)S(1)} %pad_maximum_fusion.7.gram_ref, f32[512,256]{1,0:T(8,128)S(1)} %get-tuple-element.53.rows_ref, f32[512,256]{1,0:T(8,128)S(1)} %get-tuple-element.55.first_ref, f32[2,128,384]{2,1,0:T(8,128)S(1)} %get-tuple-element.56.factor_ref), custom_call_target="tpu_custom_call" | custom-call | tf_op jit(solution)/shard_map/orth_right/pallas_call | solution.py:324
  (163 shorter events, 126.1 us)
Async XLA Ops:
  25.1 8.5 %collective-permute-start = (bf16[16,64,512]{2,1,0:T(8,128)(2,1)S(1)}, bf16[16,64,512]{2,1,0:T(8,128)(2,1)S(1)}, u32[]{:S(2)}, u32[]{:S(2)}) collective-permute-start(bf16[16,64,512]{2,1,0:T(8,128)(2,1)S(1)} %all_to_all.69), channel_id=1, source_target_pairs={{0,4},{4,0},{8,12},{12,8},{16,20},{20,16},{24,28},{28,24},{32,36},... | collective-permute-start | bytes 3145736 | tf_op jit(solution)/shard_map/ppermute | solution.py:352
  37.7 28.1 %collective-permute-start.1 = (f32[512,512]{1,0:T(8,128)S(1)}, f32[512,512]{1,0:T(8,128)S(1)}, u32[]{:S(2)}, u32[]{:S(2)}) collective-permute-start(f32[512,512]{1,0:T(8,128)S(1)} %fusion.16), channel_id=1, source_target_pairs={{0,1},{1,2},{2,3},{3,0},{4,5},{5,6},{6,7},{7,4},{8,9},{9,10},{10,1... | collective-permute-start | bytes 3145736 | tf_op jit(solution)/shard_map/ppermute | solution.py:348
  39.7 49.7 %collective-permute-start.2 = (f32[512,512]{1,0:T(8,128)S(1)}, f32[512,512]{1,0:T(8,128)S(1)}, u32[]{:S(2)}, u32[]{:S(2)}) collective-permute-start(f32[512,512]{1,0:T(8,128)S(1)} %fusion.10), channel_id=1, source_target_pairs={{0,2},{1,3},{2,0},{3,1},{4,6},{5,7},{6,4},{7,5},{8,10},{9,11},{10,... | collective-permute-start | bytes 3145736 | tf_op jit(solution)/shard_map/ppermute | solution.py:348
  43.5 45.9 %collective-permute-start.3 = (f32[512,512]{1,0:T(8,128)S(1)}, f32[512,512]{1,0:T(8,128)S(1)}, u32[]{:S(2)}, u32[]{:S(2)}) collective-permute-start(f32[512,512]{1,0:T(8,128)S(1)} %fusion.4), channel_id=1, source_target_pairs={{0,3},{1,0},{2,1},{3,2},{4,7},{5,4},{6,5},{7,6},{8,11},{9,8},{10,9... | collective-permute-start | bytes 3145736 | tf_op jit(solution)/shard_map/ppermute | solution.py:348
  138.0 15.1 %collective-permute-start.11 = (bf16[512,256]{1,0:T(8,128)(2,1)S(1)}, bf16[512,256]{1,0:T(8,128)(2,1)S(1)}, u32[]{:S(2)}, u32[]{:S(2)}) collective-permute-start(bf16[512,256]{1,0:T(8,128)(2,1)S(1)} %get-tuple-element.36), channel_id=1, source_target_pairs={{0,1},{1,2},{2,3},{3,0},{4,5},{5,6},{6,7},{7,4},{8,9},{9,10},{10,1... | collective-permute-start | bytes 786440 | tf_op jit(solution)/shard_map/ppermute | solution.py:348
  138.0 15.0 %collective-permute-start.10 = (bf16[512,256]{1,0:T(8,128)(2,1)S(1)}, bf16[512,256]{1,0:T(8,128)(2,1)S(1)}, u32[]{:S(2)}, u32[]{:S(2)}) collective-permute-start(bf16[512,256]{1,0:T(8,128)(2,1)S(1)} %get-tuple-element.36), channel_id=1, source_target_pairs={{0,2},{1,3},{2,0},{3,1},{4,6},{5,7},{6,4},{7,5},{8,10},{9,11},{10,... | collective-permute-start | bytes 786440 | tf_op jit(solution)/shard_map/ppermute | solution.py:348
  139.7 13.3 %collective-permute-start.9 = (bf16[512,256]{1,0:T(8,128)(2,1)S(1)}, bf16[512,256]{1,0:T(8,128)(2,1)S(1)}, u32[]{:S(2)}, u32[]{:S(2)}) collective-permute-start(bf16[512,256]{1,0:T(8,128)(2,1)S(1)} %get-tuple-element.36), channel_id=1, source_target_pairs={{0,3},{1,0},{2,1},{3,2},{4,7},{5,4},{6,5},{7,6},{8,11},{9,8},{10,9... | collective-permute-start | bytes 786440 | tf_op jit(solution)/shard_map/ppermute | solution.py:348
  155.8 17.3 %collective-permute-start.15 = (f32[16,64,256]{2,1,0:T(8,128)S(1)}, f32[16,64,256]{2,1,0:T(8,128)S(1)}, u32[]{:S(2)}, u32[]{:S(2)}) collective-permute-start(f32[16,64,256]{2,1,0:T(8,128)S(1)} %select_bitcast_fusion.1), channel_id=1, source_target_pairs={{0,4},{4,0},{8,12},{12,8},{16,20},{20,16},{24,28},{28,24},{32,36},... | collective-permute-start | bytes 3145736 | tf_op jit(solution)/shard_map/ppermute | solution.py:352
  157.5 9.1 %collective-permute-start.14 = (bf16[512,256]{1,0:T(8,128)(2,1)S(1)}, bf16[512,256]{1,0:T(8,128)(2,1)S(1)}, u32[]{:S(2)}, u32[]{:S(2)}) collective-permute-start(bf16[512,256]{1,0:T(8,128)(2,1)S(1)} %get-tuple-element.37), channel_id=1, source_target_pairs={{0,1},{1,2},{2,3},{3,0},{4,5},{5,6},{6,7},{7,4},{8,9},{9,10},{10,1... | collective-permute-start | bytes 786440 | tf_op jit(solution)/shard_map/ppermute | solution.py:348
  157.8 15.2 %collective-permute-start.13 = (bf16[512,256]{1,0:T(8,128)(2,1)S(1)}, bf16[512,256]{1,0:T(8,128)(2,1)S(1)}, u32[]{:S(2)}, u32[]{:S(2)}) collective-permute-start(bf16[512,256]{1,0:T(8,128)(2,1)S(1)} %get-tuple-element.37), channel_id=1, source_target_pairs={{0,2},{1,3},{2,0},{3,1},{4,6},{5,7},{6,4},{7,5},{8,10},{9,11},{10,... | collective-permute-start | bytes 786440 | tf_op jit(solution)/shard_map/ppermute | solution.py:348
  161.0 12.0 %collective-permute-start.12 = (bf16[512,256]{1,0:T(8,128)(2,1)S(1)}, bf16[512,256]{1,0:T(8,128)(2,1)S(1)}, u32[]{:S(2)}, u32[]{:S(2)}) collective-permute-start(bf16[512,256]{1,0:T(8,128)(2,1)S(1)} %get-tuple-element.37), channel_id=1, source_target_pairs={{0,3},{1,0},{2,1},{3,2},{4,7},{5,4},{6,5},{7,6},{8,11},{9,8},{10,9... | collective-permute-start | bytes 786440 | tf_op jit(solution)/shard_map/ppermute | solution.py:348
  177.8 14.8 %collective-permute-start.16 = (f32[4,64,256]{2,1,0:T(8,128)S(1)}, f32[4,64,256]{2,1,0:T(8,128)S(1)}, u32[]{:S(2)}, u32[]{:S(2)}) collective-permute-start(f32[4,64,256]{2,1,0:T(8,128)S(1)} %get-tuple-element.67), channel_id=1, source_target_pairs={{0,32},{4,36},{8,40},{12,44},{16,48},{20,52},{24,56},{28,60},{32,6... | collective-permute-start | bytes 786440 | tf_op jit(solution)/shard_map/ppermute | solution.py:352
  177.9 15.1 %collective-permute-start.18 = (f32[4,64,256]{2,1,0:T(8,128)S(1)}, f32[4,64,256]{2,1,0:T(8,128)S(1)}, u32[]{:S(2)}, u32[]{:S(2)}) collective-permute-start(f32[4,64,256]{2,1,0:T(8,128)S(1)} %get-tuple-element.68), channel_id=1, source_target_pairs={{0,96},{4,100},{8,104},{12,108},{16,112},{20,116},{24,120},{28,124... | collective-permute-start | bytes 786440 | tf_op jit(solution)/shard_map/ppermute | solution.py:352
  180.5 12.4 %collective-permute-start.17 = (f32[4,64,256]{2,1,0:T(8,128)S(1)}, f32[4,64,256]{2,1,0:T(8,128)S(1)}, u32[]{:S(2)}, u32[]{:S(2)}) collective-permute-start(f32[4,64,256]{2,1,0:T(8,128)S(1)} %get-tuple-element.69), channel_id=1, source_target_pairs={{0,64},{4,68},{8,72},{12,76},{16,80},{20,84},{24,88},{28,92},{32,9... | collective-permute-start | bytes 786440 | tf_op jit(solution)/shard_map/ppermute | solution.py:352
  182.1 14.2 %collective-permute-start.23 = (f32[4,64,256]{2,1,0:T(8,128)S(1)}, f32[4,64,256]{2,1,0:T(8,128)S(1)}, u32[]{:S(2)}, u32[]{:S(2)}) collective-permute-start(f32[4,64,256]{2,1,0:T(8,128)S(1)} %get-tuple-element.64), channel_id=1, source_target_pairs={{0,8},{4,12},{8,16},{12,20},{16,24},{20,28},{24,0},{28,4},{32,40},... | collective-permute-start | bytes 786440 | tf_op jit(solution)/shard_map/ppermute | solution.py:352
  182.4 13.8 %collective-permute-start.24 = (f32[4,64,256]{2,1,0:T(8,128)S(1)}, f32[4,64,256]{2,1,0:T(8,128)S(1)}, u32[]{:S(2)}, u32[]{:S(2)}) collective-permute-start(f32[4,64,256]{2,1,0:T(8,128)S(1)} %get-tuple-element.65), channel_id=1, source_target_pairs={{0,16},{4,20},{8,24},{12,28},{16,0},{20,4},{24,8},{28,12},{32,48},... | collective-permute-start | bytes 786440 | tf_op jit(solution)/shard_map/ppermute | solution.py:352
  257.5 14.5 %all-to-all-start.5 = ((bf16[16,64,256]{2,1,0:T(8,128)(2,1)}), bf16[16,64,256]{2,1,0:T(8,128)(2,1)S(1)}, u32[]{:S(2)}, u32[]{:S(2)}) async-start(bf16[16,64,256]{2,1,0:T(8,128)(2,1)} %broadcast_in_dim.15), calls=%async_computation.5 | async-start | bytes 1048576 | tf_op jit(solution)/shard_map/all_to_all | solution.py:361
  277.7 17.4 %collective-permute-start.36 = (f32[512,256]{1,0:T(8,128)S(1)}, f32[512,256]{1,0:T(8,128)S(1)}, u32[]{:S(2)}, u32[]{:S(2)}) collective-permute-start(f32[512,256]{1,0:T(8,128)S(1)} %fusion.8), channel_id=1, source_target_pairs={{0,2},{1,3},{2,0},{3,1},{4,6},{5,7},{6,4},{7,5},{8,10},{9,11},{10,... | collective-permute-start | bytes 1572872 | tf_op jit(solution)/shard_map/ppermute | solution.py:348
  295.1 8.1 %collective-permute-start.38 = (bf16[16,64,256]{2,1,0:T(8,128)(2,1)S(1)}, bf16[16,64,256]{2,1,0:T(8,128)(2,1)S(1)}, u32[]{:S(2)}, u32[]{:S(2)}) collective-permute-start(bf16[16,64,256]{2,1,0:T(8,128)(2,1)S(1)} %all_to_all.74), channel_id=1, source_target_pairs={{0,4},{4,0},{8,12},{12,8},{16,20},{20,16},{24,28},{28,24},{32,36},... | collective-permute-start | bytes 1572872 | tf_op jit(solution)/shard_map/ppermute | solution.py:352
  299.5 14.8 %collective-permute-start.35 = (f32[512,256]{1,0:T(8,128)S(1)}, f32[512,256]{1,0:T(8,128)S(1)}, u32[]{:S(2)}, u32[]{:S(2)}) collective-permute-start(f32[512,256]{1,0:T(8,128)S(1)} %fusion.14), channel_id=1, source_target_pairs={{0,1},{1,2},{2,3},{3,0},{4,5},{5,6},{6,7},{7,4},{8,9},{9,10},{10,1... | collective-permute-start | bytes 1572872 | tf_op jit(solution)/shard_map/ppermute | solution.py:348
  300.3 24.9 %collective-permute-start.37 = (f32[512,256]{1,0:T(8,128)S(1)}, f32[512,256]{1,0:T(8,128)S(1)}, u32[]{:S(2)}, u32[]{:S(2)}) collective-permute-start(f32[512,256]{1,0:T(8,128)S(1)} %fusion.2), channel_id=1, source_target_pairs={{0,3},{1,0},{2,1},{3,2},{4,7},{5,4},{6,5},{7,6},{8,11},{9,8},{10,9... | collective-permute-start | bytes 1572872 | tf_op jit(solution)/shard_map/ppermute | solution.py:348
  305.6 31.1 %collective-permute-start.39 = (f32[512,256]{1,0:T(8,128)S(1)}, f32[512,256]{1,0:T(8,128)S(1)}, u32[]{:S(2)}, u32[]{:S(2)}) collective-permute-start(f32[512,256]{1,0:T(8,128)S(1)} %fusion.12), channel_id=1, source_target_pairs={{0,1},{1,2},{2,3},{3,0},{4,5},{5,6},{6,7},{7,4},{8,9},{9,10},{10,1... | collective-permute-start | bytes 1572872 | tf_op jit(solution)/shard_map/ppermute | solution.py:348
  305.7 31.0 %collective-permute-start.40 = (f32[512,256]{1,0:T(8,128)S(1)}, f32[512,256]{1,0:T(8,128)S(1)}, u32[]{:S(2)}, u32[]{:S(2)}) collective-permute-start(f32[512,256]{1,0:T(8,128)S(1)} %fusion.6), channel_id=1, source_target_pairs={{0,2},{1,3},{2,0},{3,1},{4,6},{5,7},{6,4},{7,5},{8,10},{9,11},{10,... | collective-permute-start | bytes 1572872 | tf_op jit(solution)/shard_map/ppermute | solution.py:348
  306.9 29.9 %collective-permute-start.41 = (f32[512,256]{1,0:T(8,128)S(1)}, f32[512,256]{1,0:T(8,128)S(1)}, u32[]{:S(2)}, u32[]{:S(2)}) collective-permute-start(f32[512,256]{1,0:T(8,128)S(1)} %fusion), channel_id=1, source_target_pairs={{0,3},{1,0},{2,1},{3,2},{4,7},{5,4},{6,5},{7,6},{8,11},{9,8},{10,9... | collective-permute-start | bytes 1572872 | tf_op jit(solution)/shard_map/ppermute | solution.py:348
  (31 other events, 263.6 us)
